TPU v7x, 32 devices: a whole 2x2x4 slice. The times are simulated.
32 devices in a mesh: tm: 8 (over z, x), panel: 4 (over y, core).
Axes of the slice: x: 2, y: 2, z: 4, core: 2. Of those that a mesh axis runs over, the one named last changes fastest.
Arguments:
- design: bfloat16 [2048, 7680], P('tm', 'panel'), may hold values from -6 to 6
- partials: bfloat16 [2048, 64], P('tm'), may hold values from -0.119628906 to 0.119628906
- observed: bfloat16 [2048], P('tm'), may hold values from -6 to 6
- arc_of_row: int32 [2048, 1], replicated, may hold values from 0 to 7, as said below
- autoreg: float32 [8], replicated, may hold values from -0.55 to 0.5
- movavg: float32 [8], replicated, may hold values from 0.3 to 0.9
Outputs:
- normal: float32 [7680, 7680], P('tm', 'panel')
- right_hand: float32 [7680], P('panel')
Inputs may be any that keep to these rules, and one draw needn't show every extreme that they name: arc_of_row never falls along the epochs and names every arc; arcs 2b and 2b + 1 together have 2 * 256 epochs, one of them 384 // 3 to 160 epochs and the other 352 to 384; one arc has exactly 384 epochs and its partner exactly 128, so that at most 48 rows of one device belong to one arc, and every device holds exactly 48 rows of the longest arc; arc a is held by index a of tm.
All inputs are finite; a program needn't handle non-finite values.
Results may differ from a plain program's by a relative error of at most 0.02.
Values may be sent and summed in bfloat16 or wider, within the bound.
No kernel may reach another device: no remote copies, remote signals or barrier semaphores. Data moves between devices by JAX's collectives and lax.ppermute only.
A program may use at most 192 MiB of HBM per device.

v0:
```python
import jax
import jax.numpy as jnp
from jax import lax
from jax.sharding import PartitionSpec as P


def whiten_matrix(order_row, order_col, usable_row, usable_col, ar_value, ma_value):
    spacing = order_row[:, None] - order_col[None, :]
    lag_steps = jnp.maximum(spacing - 1, 0)
    parity = (lag_steps % 2).astype(jnp.float32)
    flip_sign = 1.0 - 2.0 * parity
    decayed = (
        -(ar_value + ma_value)
        * flip_sign
        * jnp.exp(lag_steps.astype(jnp.float32) * jnp.log(ma_value))
    )
    entry = jnp.where(spacing == 0, jnp.float32(1.0), decayed)
    allowed = usable_row[:, None] & usable_col[None, :] & (spacing >= 0)
    return jnp.where(allowed, entry, jnp.float32(0.0)).astype(jnp.bfloat16)


def eliminate(whitener, rows_design, rows_params, rows_obs, scale):
    white_design = jnp.dot(whitener, rows_design, preferred_element_type=jnp.float32)
    white_params = jnp.dot(whitener, rows_params, preferred_element_type=jnp.float32)
    white_obs = jnp.dot(whitener, rows_obs, preferred_element_type=jnp.float32)
    param_count = rows_params.shape[1]
    param_gram = jnp.dot(white_params.T, white_params, precision=lax.Precision.HIGHEST) + jnp.eye(
        param_count, dtype=jnp.float32
    )
    factor = jnp.linalg.cholesky(param_gram)
    basis = lax.linalg.triangular_solve(factor, white_params.T, left_side=True, lower=True)
    arc_terms = jnp.dot(basis, white_design, precision=lax.Precision.HIGHEST)
    arc_rhs = jnp.dot(basis, white_obs, precision=lax.Precision.HIGHEST)
    right_part = (
        jnp.dot(white_design.T, white_obs, precision=lax.Precision.HIGHEST)
        - jnp.dot(arc_terms.T, arc_rhs, precision=lax.Precision.HIGHEST)
    ) * scale
    return (white_design.astype(jnp.bfloat16), arc_terms.astype(jnp.bfloat16), right_part)


def body(design, partials, observed, arc_of_row, autoreg, movavg):
    tile_count = lax.axis_size("tm")
    device_index = lax.axis_index("tm")
    rows_dev = design.shape[0]
    panel_width = design.shape[1]
    param_count = partials.shape[1]
    capacity = 3 * rows_dev // 2 // tile_count
    slot_count = tile_count * capacity
    scale = 1.0 / (rows_dev * tile_count)
    arc_ids = arc_of_row[:, 0]
    epoch_table = arc_ids.reshape(rows_dev, tile_count)
    local_arcs = lax.dynamic_slice_in_dim(epoch_table, device_index, 1, 1)[:, 0]
    onehot = (local_arcs[:, None] == jnp.arange(tile_count, dtype=jnp.int32)[None, :]).astype(
        jnp.int32
    )
    earlier = jnp.cumsum(onehot, axis=0) - onehot
    within = jnp.sum(earlier * onehot, axis=1)
    target_slot = local_arcs * capacity + within
    source_row = (
        jnp.zeros((slot_count,), jnp.int32)
        .at[target_slot]
        .set(jnp.arange(1, rows_dev + 1, dtype=jnp.int32))
    )

    def pick_rows(values):
        padded = jnp.concatenate([jnp.zeros((1,) + values.shape[1:], values.dtype), values], axis=0)
        return jnp.take(padded, source_row, axis=0)

    send_design = pick_rows(design).reshape(tile_count, capacity, panel_width)
    send_params = pick_rows(partials).reshape(tile_count, capacity, param_count)
    send_obs = pick_rows(observed).reshape(tile_count, capacity)
    got_design, got_params, got_obs = (
        lax.all_to_all(send_design, "tm", split_axis=0, concat_axis=0, tiled=True),
        lax.all_to_all(send_params, "tm", split_axis=0, concat_axis=0, tiled=True),
        lax.all_to_all(send_obs, "tm", split_axis=0, concat_axis=0, tiled=True),
    )
    got_design = got_design.reshape(slot_count, panel_width)
    got_params = got_params.reshape(slot_count, param_count)
    got_obs = got_obs.reshape(slot_count)
    per_source = jnp.sum((epoch_table == device_index).astype(jnp.int32), axis=0)
    arc_start = jnp.sum((arc_ids < device_index).astype(jnp.int32))
    first_pos = jnp.mod(jnp.arange(tile_count, dtype=jnp.int32) - arc_start, tile_count)
    offset_in = jnp.arange(capacity, dtype=jnp.int32)
    order_pos = (first_pos[:, None] + offset_in[None, :] * tile_count).reshape(slot_count)
    usable = (offset_in[None, :] < per_source[:, None]).reshape(slot_count)
    whitener = whiten_matrix(
        order_pos, order_pos, usable, usable, autoreg[device_index], movavg[device_index]
    )
    design_bf, terms_bf, right_part = eliminate(whitener, got_design, got_params, got_obs, scale)
    right_hand = lax.psum(right_part, "tm")
    own_rows = jnp.concatenate([design_bf, terms_bf], axis=0)
    signed_rows = jnp.concatenate([design_bf, -terms_bf], axis=0)
    gathered = lax.all_gather(signed_rows, "panel", axis=1, tiled=True)
    product = lax.dot_general(
        gathered, own_rows, (((0,), (0,)), ((), ())), preferred_element_type=jnp.float32
    )
    normal = lax.psum_scatter(
        (product * scale).astype(jnp.bfloat16), "tm", scatter_dimension=0, tiled=True
    ).astype(jnp.float32)
    return (normal, right_hand)


def solution(mesh):
    in_specs = (P("tm", "panel"), P("tm", None), P("tm"), P(), P(), P())
    out_specs = (P("tm", "panel"), P("panel"))
    return jax.shard_map(body, mesh=mesh, in_specs=in_specs, out_specs=out_specs, check_vma=False)
```

profile of v0, /device:TPU:0, one launch (start us, length us, event | category | flops | bytes accessed | tf_op | source)
XLA Modules:
  0.0 630.5 jit_solution(10669916997776109319)
XLA Ops:
  7.2 1.0 copy.14
  8.7 2.0 fusion.37
  12.2 1.4 scatter_custom_fusion
  13.7 0.7 pad_maximum_fusion.1
  14.4 2.8 gather_fusion.2
  17.4 1.4 gather_fusion.1
  18.9 0.7 reshape.232
  19.7 7.3 %all-to-all-start.1 = ((bf16[8,2,1536]{2,1,0:T(2,128)(2,1)}), bf16[8,2,1536]{2,1,0:T(2,128)(2,1)S(1)}, u32[]{:S(2)}, u32[]{:S(2)}) async-start(bf16[8,2,1536]{2,1,0:T(2,128)(2,1)} %reshape.232), calls=%async_computation.1 | async-start | bytes 98304 | tf_op jit(solution)/shard_map/all_to_all | solution.py:74
  27.2 2.5 gather_fusion
  29.7 1.3 broadcast_select_fusion
  31.1 2.7 all-to-all-done.1
  33.7 3.6 all-to-all-start
  37.4 0.7 dynamic_slice.10
  40.6 0.7 and_select_fusion
  41.8 0.7 fusion.27
  42.9 5.8 cholesky.17
  48.8 0.6 compare_reduce_fusion
  49.4 0.7 fusion.32
  50.1 4.9 custom-call.6
  55.3 16.2 %all-to-all-done = bf16[8,48,1920]{2,1,0:T(8,128)(2,1)S(1)} async-done(((bf16[8,48,1920]{2,1,0:T(8,128)(2,1)}), bf16[8,48,1920]{2,1,0:T(8,128)(2,1)S(1)}, u32[]{:S(2)}, u32[]{:S(2)}) %all-to-all-start) | async-done | bytes 1474592 | tf_op jit(solution)/shard_map/all_to_all | solution.py:73
  71.5 1.1 copy-done
  72.6 2.7 fusion.67
  75.4 2.4 fusion.66
  77.7 1.3 pad_maximum_fusion
  79.3 48.6 %all-gather.2.cloned.1.call-done = bf16[448,7680]{1,0:T(8,128)(2,1)} async-done(((bf16[448,1920]{1,0:T(8,128)(2,1)}), bf16[448,7680]{1,0:T(8,128)(2,1)}) %all-gather.2.cloned.1.call-update) | async-done | bytes 6881296 | tf_op jit(solution)/shard_map/all_gather | solution.py:93
  127.8 22.9 %multiply_convert_fusion = bf16[7680,1920]{1,0:T(8,128)(2,1)} fusion(bf16[448,7680]{1,0:T(8,128)(2,1)} %all-gather.2.cloned.1.call-done, bf16[64,1920]{1,0:T(8,128)(2,1)} %get-tuple-element.7, bf16[384,1920]{1,0:T(8,128)(2,1)} %copy-done.1), kind=kOutput, calls=%fused_computation.4 | convolution fusion | flops 13244989440 | bytes 38092800 | tf_op jit(solution)/shard_map/dot_general | solution.py:94
  150.8 11.9 %all_to_all.16 = bf16[8,1,48]{2,1,0:T(2,128)(2,1)S(1)} all-to-all(bf16[8,1,48]{2,1,0:T(2,128)(2,1)S(1)} %select_n.84), channel_id=1, replica_groups=mesh['tm'=8,'panel'=4] {'tm'}, dimensions={0} | all-to-all | bytes 1536 | tf_op jit(solution)/shard_map/all_to_all | solution.py:75
  162.8 0.7 convolution_bitcast_fusion
  164.1 1.7 fusion.5
  165.8 19.7 %psum.7 = f32[1920]{0:T(1024)} all-reduce(f32[1920]{0:T(1024)S(1)} %subtract_multiply_fusion), channel_id=1, replica_groups=mesh['tm'=8,'panel'=4] {'tm'}, use_global_device_ids=true, to_apply=%region_9.10 | all-reduce | flops 1920 | bytes 15360 | tf_op jit(solution)/shard_map/psum | solution.py:90
  185.5 432.6 %reduce-scatter.2.cloned.1.call-done = bf16[960,1920]{1,0:T(8,128)(2,1)} async-done(((bf16[7680,1920]{1,0:T(8,128)(2,1)}), bf16[960,1920]{1,0:T(8,128)(2,1)}) %reduce-scatter.2.cloned.1.call-update) | async-done | bytes 3686416 | tf_op jit(solution)/shard_map/reduce_scatter | solution.py:97
  618.1 5.6 convert_element_type.57
  (51 shorter events, 5.5 us)
Async XLA Ops:
  7.2 19.8 %copy-start.2 = (bf16[256,1920]{1,0:T(8,128)(2,1)S(1)}, bf16[256,1920]{1,0:T(8,128)(2,1)}, u32[]{:S(2)}) copy-start(bf16[256,1920]{1,0:T(8,128)(2,1)} %param.6) | copy-start | bytes 2949124
  19.7 14.0 %all-to-all-start.1 = ((bf16[8,2,1536]{2,1,0:T(2,128)(2,1)}), bf16[8,2,1536]{2,1,0:T(2,128)(2,1)S(1)}, u32[]{:S(2)}, u32[]{:S(2)}) async-start(bf16[8,2,1536]{2,1,0:T(2,128)(2,1)} %reshape.232), calls=%async_computation.1 | async-start | bytes 98304 | tf_op jit(solution)/shard_map/all_to_all | solution.py:74
  29.7 7.7 %copy-start.3 = (f32[8]{0:T(128)S(1)}, f32[8]{0:T(128)}, u32[]{:S(2)}) copy-start(f32[8]{0:T(128)} %param.11) | copy-start | bytes 100
  29.7 9.1 %copy-start.4 = (f32[8]{0:T(128)S(1)}, f32[8]{0:T(128)}, u32[]{:S(2)}) copy-start(f32[8]{0:T(128)} %param.10) | copy-start | bytes 100
  33.7 37.8 %all-to-all-start = ((bf16[8,48,1920]{2,1,0:T(8,128)(2,1)}), bf16[8,48,1920]{2,1,0:T(8,128)(2,1)S(1)}, u32[]{:S(2)}, u32[]{:S(2)}) async-start(bf16[8,48,1920]{2,1,0:T(8,128)(2,1)} %broadcast_select_fusion), calls=%async_computation | async-start | bytes 2949120 | tf_op jit(solution)/shard_map/all_to_all | solution.py:73
  37.3 90.5 %all-gather.2.cloned.1.call-start = ((), (), s32[]{:S(2)}) async-start(), calls=%async_computation.4 | async-start | bytes 8601600 | tf_op jit(solution)/shard_map/all_gather | solution.py:93
  71.5 1.1 copy-start
  75.3 2.4 copy-start.1
  79.0 539.1 %reduce-scatter.2.cloned.1.call-start = ((), (), s32[]{:S(2)}) async-start(), calls=%async_computation.5 | async-start | bytes 33177600 | tf_op jit(solution)/shard_map/reduce_scatter | solution.py:97
Sparse Core Ops, SparseCore 0:
  79.2 48.6 all-gather.1
  150.9 467.2 reduce-scatter.1
where the time goes:
time: 631 us
  waiting for transfers between devices  500 us (79%)
  matrix products  32.2 us (5%)
  blocking collectives  31.6 us (5%)
  other arithmetic  25 us (4%)
  between operations  16.3 us (3%)
  local copies, waits for them, and re-layouts  14.3 us (2%)
  starting transfers between devices  11.1 us (2%)
    reduce_scatter x1, waiting for transfers between devices, body(): lax.psum_scatter((product * scale).astype(jnp.bfloat16), 'tm', scatter_di...  433 us
    all_gather x1, waiting for transfers between devices, body(): gathered = lax.all_gather(signed_rows, 'panel', axis=1, tiled=True)  48.6 us
    dot_general x1, matrix products, body(): lax.dot_general(gathered, own_rows, (((0,), (0,)), ((), ())), preferred_e...  22.9 us
    psum x1, blocking collectives, body(): right_hand = lax.psum(right_part, 'tm')  19.7 us
    all_to_all x1, waiting for transfers between devices, body(): lax.all_to_all(send_design, 'tm', split_axis=0, concat_axis=0, tiled=True)  16.2 us
  transfers between devices with their start and end apart: 4, of which 4 were waited for; matrix products, arithmetic and copies ran while one was open for 4% of the time, Pallas kernels for 0%

commit v1 on v0

v1 whole, which is shorter than its diff:
```python
import functools

import jax
import jax.numpy as jnp
from jax import lax
from jax.experimental import pallas as pl
from jax.experimental.pallas import tpu as pltpu
from jax.sharding import PartitionSpec as P

AXES = ("tm", "panel")
HIGHEST = lax.Precision.HIGHEST
ROWS_ACROSS = (((0,), (0,)), ((), ()))
SWEEPS = 16
EXTRA = 16
HBM = pl.BlockSpec(memory_space=pl.ANY)
SMEM = pl.BlockSpec(memory_space=pltpu.SMEM)
FROM_Z = ((1, 3, 0, 2), (2, 0, 3, 1), (3, 2, 1, 0))
SEND_Z = (((1, 0), (3, 1), (0, 2), (2, 3)), ((2, 0), (0, 1), (3, 2), (1, 3)), ((1, 0), (3, 1), (0, 2), (2, 3)))


def params(mib, **more):
    return pltpu.CompilerParams(vmem_limit_bytes=mib * 1024 * 1024, **more)


def whiten_kernel(
    shard_ref, length_ref, gain_ref, log_ref, slots_ref, gram_ref, across_ref, square_ref, obs_ref, held
):
    tile_count, pair_rows, width = slots_ref.shape
    size = tile_count * pair_rows
    shift = pair_rows.bit_length() - 1
    pair = pl.program_id(0)
    length = length_ref[pair]

    def epoch(shape, axis):
        at = lax.broadcasted_iota(jnp.int32, shape, axis)
        return jnp.bitwise_and(at, pair_rows - 1) * tile_count + jnp.right_shift(at, shift)

    epoch_row, epoch_col = epoch((size, 1), 0), epoch((1, size), 1)
    first_row = jnp.where(epoch_row < length, 1, 0)
    first_col = jnp.where(epoch_col < length, 1, 0)
    gain = jnp.where(epoch_row < length, gain_ref[2 * pair], gain_ref[2 * pair + 1])
    log_ma = jnp.where(epoch_row < length, log_ref[2 * pair], log_ref[2 * pair + 1])
    spacing = epoch_row - epoch_col
    lag = jnp.maximum(spacing - 1, 0)
    size_of = gain * jnp.exp(lag.astype(jnp.float32) * log_ma)
    decayed = jnp.where(jnp.bitwise_and(lag, 1) == 1, size_of, -size_of)
    entry = jnp.where(spacing == 0, jnp.float32(1.0), decayed)
    allowed = (first_row == first_col) & (spacing >= 0)
    whitener = jnp.where(allowed, entry, jnp.float32(0.0)).astype(jnp.bfloat16)

    for n in range(tile_count):
        at = pl.multiple_of(shard_ref[n] * pair_rows, pair_rows)
        held[pl.ds(at, pair_rows), :] = slots_ref[n].astype(jnp.float32)
    rows = held[...]
    obs_ref[0] = rows.T[width // 2 : width // 2 + EXTRA].astype(jnp.bfloat16)
    lane = lax.broadcasted_iota(jnp.int32, (size, width), 1)
    in_first = jnp.where(lane < width // 2, 1, 0)
    rows = jnp.where(in_first == 1, rows, pltpu.roll(rows, width // 2, axis=1))
    rows = jnp.where(in_first == first_row, rows, 0.0).astype(jnp.bfloat16)
    white = jnp.dot(whitener, rows, preferred_element_type=jnp.float32)
    eye = lax.broadcasted_iota(jnp.int32, (width, width), 0) == lax.broadcasted_iota(
        jnp.int32, (width, width), 1
    )
    gram_ref[0] = lax.dot_general(
        white, white, ROWS_ACROSS, precision=HIGHEST, preferred_element_type=jnp.float32
    ) + jnp.where(eye, 1.0, 0.0)
    high = white.astype(jnp.bfloat16)
    rest = white - high.astype(jnp.float32)
    middle = rest.astype(jnp.bfloat16)
    low = (rest - middle.astype(jnp.float32)).astype(jnp.bfloat16)
    across_ref[0] = sum(
        lax.dot_general(part, whitener, ROWS_ACROSS, preferred_element_type=jnp.float32)
        for part in (low, middle, high)
    )
    square_ref[0] = lax.dot_general(
        whitener, whitener, ROWS_ACROSS, preferred_element_type=jnp.float32
    )


def invert_kernel(first, count, gram_ref, out_ref):
    size, arcs, _ = gram_ref.shape
    lane = lax.broadcasted_iota(jnp.int32, (arcs, size), 1)
    source = gram_ref
    for k in range(first, first + count):
        row = source[k]
        here = lane == k
        inverse = 1.0 / row[:, k : k + 1]
        scaled = row * inverse
        for i in [(k + 1 + n) % size for n in range(size - 1)]:
            column = row[:, i : i + 1]
            out_ref[i] = jnp.where(here, column * inverse, source[i] - column * scaled)
        out_ref[k] = jnp.where(here, -inverse, scaled)
        source = out_ref


def middle_kernel(across_ref, minus_inverse_ref, square_ref, obs_ref, out_ref):
    size = square_ref.shape[1]
    across = across_ref[0]
    reduced = jnp.dot(
        minus_inverse_ref[0], across, precision=HIGHEST, preferred_element_type=jnp.float32
    )
    whole = square_ref[0] + lax.dot_general(
        across, reduced, ROWS_ACROSS, precision=HIGHEST, preferred_element_type=jnp.float32
    )
    high = whole.astype(jnp.bfloat16)
    rest = whole - high.astype(jnp.float32)
    middle = rest.astype(jnp.bfloat16)
    low = (rest - middle.astype(jnp.float32)).astype(jnp.bfloat16)
    obs = obs_ref[0]
    value = sum(
        jnp.dot(obs, part, preferred_element_type=jnp.float32) for part in (low, middle, high)
    )
    value_high = value.astype(jnp.bfloat16)
    rest = value - value_high.astype(jnp.float32)
    value_middle = rest.astype(jnp.bfloat16)
    value_low = rest - value_middle.astype(jnp.float32)
    at = lax.broadcasted_iota(jnp.int32, (EXTRA, size), 0)
    parts = jnp.where(
        at == 0,
        value_high.astype(jnp.float32),
        jnp.where(at == 1, value_middle.astype(jnp.float32), jnp.where(at == 2, value_low, 0.0)),
    )
    out_ref[0, :size] = high
    out_ref[0, size : 2 * size] = middle
    out_ref[0, 2 * size :] = parts.astype(jnp.bfloat16)


def pair_matrices(slots, shard, arc_of_row, autoreg, movavg):
    tile_count, rows_dev, width = slots.shape
    param_count = width // 2
    pair_rows = 2 * rows_dev // tile_count
    pair_count = rows_dev // pair_rows
    size = tile_count * pair_rows
    arc_count = 2 * pair_count
    first = 2 * jnp.arange(pair_count, dtype=jnp.int32)
    lengths = jnp.sum((arc_of_row == first[None, :]).astype(jnp.int32), axis=0)

    def per_pair(*shape):
        return pl.BlockSpec((1, *shape), lambda b: (b, 0, 0))

    gram, across, square, obs = pl.pallas_call(
        whiten_kernel,
        grid=(pair_count,),
        in_specs=[SMEM] * 4 + [pl.BlockSpec((tile_count, pair_rows, width), lambda b: (0, b, 0))],
        out_specs=[
            per_pair(width, width),
            per_pair(width, size),
            per_pair(size, size),
            per_pair(EXTRA, size),
        ],
        out_shape=[
            jax.ShapeDtypeStruct((pair_count, width, width), jnp.float32),
            jax.ShapeDtypeStruct((pair_count, width, size), jnp.float32),
            jax.ShapeDtypeStruct((pair_count, size, size), jnp.float32),
            jax.ShapeDtypeStruct((pair_count, EXTRA, size), jnp.bfloat16),
        ],
        scratch_shapes=[pltpu.VMEM((size, width), jnp.float32)],
        compiler_params=params(40),
        name="whiten",
    )(shard, lengths, autoreg + movavg, jnp.log(movavg), slots)
    blocks = jnp.stack(
        [gram[:, :param_count, :param_count], gram[:, param_count:, param_count:]], axis=1
    ).reshape(arc_count, param_count, param_count)
    minus = blocks.transpose(1, 0, 2)
    for first in range(0, param_count, SWEEPS):
        minus = pl.pallas_call(
            functools.partial(invert_kernel, first, SWEEPS),
            out_shape=jax.ShapeDtypeStruct(minus.shape, jnp.float32),
            name="invert",
        )(minus)
    minus = minus.transpose(1, 0, 2).reshape(pair_count, 2, param_count, param_count)
    nothing = jnp.zeros((pair_count, param_count, param_count), jnp.float32)
    minus = jnp.concatenate(
        [
            jnp.concatenate([minus[:, 0], nothing], axis=2),
            jnp.concatenate([nothing, minus[:, 1]], axis=2),
        ],
        axis=1,
    )
    return pl.pallas_call(
        middle_kernel,
        grid=(pair_count,),
        in_specs=[per_pair(width, size), per_pair(width, width), per_pair(size, size), per_pair(EXTRA, size)],
        out_specs=per_pair(2 * size + EXTRA, size),
        out_shape=jax.ShapeDtypeStruct((pair_count, 2 * size + EXTRA, size), jnp.bfloat16),
        compiler_params=params(40),
        name="middle",
    )(across, minus, square, obs)


def pack_kernel(count, width, meta_ref, *refs):
    slots, out, held, sems = refs[:count], refs[count], refs[count + 1], refs[count + 2]
    start = pl.multiple_of(meta_ref[1], 128)

    @pl.when(meta_ref[0] == 1)
    def _():
        into, back, at = [], [], 0
        for n, slot in enumerate(slots):
            here = pl.ds(at, slot.shape[0])
            columns = slot.at[:, pl.ds(start, width)]
            into.append(pltpu.make_async_copy(columns, held.at[here], sems.at[0, n]))
            back.append(pltpu.make_async_copy(held.at[here], out.at[here], sems.at[1, n]))
            at += slot.shape[0]
        for copy in into:
            copy.start()
        for first, second in zip(into, back):
            first.wait()
            second.start()
        for copy in back:
            copy.wait()


def pack(meta, slots, width):
    rows = sum(slot.shape[0] for slot in slots)
    return pl.pallas_call(
        functools.partial(pack_kernel, len(slots), width),
        in_specs=[SMEM] + [HBM] * len(slots),
        out_specs=HBM,
        out_shape=jax.ShapeDtypeStruct((rows, width), slots[0].dtype),
        scratch_shapes=[
            pltpu.VMEM((rows, width), slots[0].dtype),
            pltpu.SemaphoreType.DMA((2, len(slots))),
        ],
        name="pack",
    )(meta, *slots)


def middle_rows_kernel(scale, shard_ref, mid_ref, *refs):
    *slots, out, rhs, panel, middle = refs
    pair_rows = slots[0].shape[0]
    size = len(slots) * pair_rows

    def place(n):
        return pl.ds(pl.multiple_of(shard_ref[n] * pair_rows, pair_rows), pair_rows)

    for n, slot in enumerate(slots):
        panel[place(n), :] = slot[...]
    product = jnp.dot(mid_ref[0], panel[...], preferred_element_type=jnp.float32)
    middle[...] = (product[:size] + product[size : 2 * size]).astype(jnp.bfloat16)
    for n in range(len(slots)):
        out[n] = middle[place(n), :]
    rhs_here = jnp.sum(product[2 * size :], axis=0, keepdims=True) * scale

    @pl.when(pl.program_id(0) == 0)
    def _():
        rhs[...] = rhs_here

    @pl.when(pl.program_id(0) > 0)
    def _():
        rhs[...] += rhs_here


def middle_rows(shard, mids, first_pair, slots, pair_rows, scale):
    rows, width = slots[0].shape
    pair_count = rows // pair_rows
    size = len(slots) * pair_rows
    return pl.pallas_call(
        functools.partial(middle_rows_kernel, scale),
        grid=(pair_count,),
        in_specs=[SMEM, pl.BlockSpec((1, 2 * size + EXTRA, size), lambda b: (b + first_pair, 0, 0))]
        + [pl.BlockSpec((pair_rows, width), lambda b: (b, 0))] * len(slots),
        out_specs=[
            pl.BlockSpec((len(slots), pair_rows, width), lambda b: (0, b, 0)),
            pl.BlockSpec((1, width), lambda b: (0, 0)),
        ],
        out_shape=[
            jax.ShapeDtypeStruct((len(slots), rows, width), jnp.bfloat16),
            jax.ShapeDtypeStruct((1, width), jnp.float32),
        ],
        scratch_shapes=[
            pltpu.VMEM((size, width), jnp.bfloat16),
            pltpu.VMEM((size, width), jnp.bfloat16),
        ],
        compiler_params=params(48),
        cost_estimate=pl.CostEstimate(
            flops=2 * pair_count * (2 * size + EXTRA) * size * width,
            bytes_accessed=2 * len(slots) * rows * width * 2,
            transcendentals=0,
        ),
        name="middle_rows",
    )(shard, mids, *slots)


def tile_kernel(places, block_columns, scale, meta_ref, *refs):
    groups = 1 + max(group for group, _ in places)
    blocks, refs = refs[: 4 * groups], refs[4 * groups :]
    *middles, out, block, turned, sems = refs
    rows = middles[0].shape[1]
    step = middles[0].shape[2]

    def copies(kind):
        return [
            pltpu.make_async_copy(
                blocks[4 * group + kind].at[pl.ds(at, rows)],
                block.at[pl.ds(n * rows, rows)],
                sems.at[n],
            )
            for n, (group, at) in enumerate(places)
        ]

    @pl.when(pl.program_id(0) == 0)
    def _():
        for kind in range(4):

            @pl.when(meta_ref[1] == kind)
            def _(kind=kind):
                for copy in copies(kind):
                    copy.start()

        for n, copy in enumerate(copies(0)):
            copy.wait()
            turned[:, n * rows : (n + 1) * rows] = block[n * rows : (n + 1) * rows, :].T

    middle = jnp.concatenate([one[...].reshape(-1, step) for one in middles], axis=0)
    offset = pl.multiple_of(meta_ref[0], 64)
    out[...] = (
        jnp.dot(
            turned[pl.ds(offset, block_columns), :], middle, preferred_element_type=jnp.float32
        )
        * scale
    )


def tile(meta, middles, places, blocks, block_columns, scale, step):
    count, rows, width = middles[0].shape
    payload = blocks[0][0].shape[1]
    total = count * rows * len(middles)
    return pl.pallas_call(
        functools.partial(tile_kernel, tuple(places), block_columns, scale),
        grid=(pl.cdiv(width, step),),
        in_specs=[SMEM]
        + [HBM] * (4 * len(blocks))
        + [pl.BlockSpec((count, rows, step), lambda j: (0, 0, j))] * len(middles),
        out_specs=pl.BlockSpec((block_columns, step), lambda j: (0, j)),
        out_shape=jax.ShapeDtypeStruct((block_columns, width), jnp.float32),
        scratch_shapes=[
            pltpu.VMEM((total, payload), jnp.bfloat16),
            pltpu.VMEM((payload, total), jnp.bfloat16),
            pltpu.SemaphoreType.DMA((len(places),)),
        ],
        compiler_params=params(56),
        cost_estimate=pl.CostEstimate(
            flops=2 * block_columns * width * total,
            bytes_accessed=block_columns * width * 4 + total * (payload + width) * 2,
            transcendentals=0,
        ),
        name="tile",
    )(meta, *[one for four in blocks for one in four], *middles)


def tie(value, *others):
    return lax.optimization_barrier((value, *others))[0]


def block_body(design, partials, observed, arc_of_row, autoreg, movavg):
    tile_count, panel_count = lax.axis_size("tm"), lax.axis_size("panel")
    rows_dev, width = design.shape
    block_columns = width * panel_count // tile_count
    payload = pl.cdiv(block_columns, 128) * 128
    pair_rows = 2 * rows_dev // tile_count
    scale = 1.0 / (rows_dev * tile_count)
    t, p = lax.axis_index("tm"), lax.axis_index("panel")
    z, x, y, core = t // 2, t % 2, p // 2, p % 2
    near, same_core = y == z // 2, core == z % 2

    def along_z(value, turn):
        pairs = [(2 * s + i, 2 * d + i) for s, d in SEND_Z[turn] for i in range(2)]
        return lax.ppermute(value, "tm", pairs)

    def across_x(value):
        return lax.ppermute(value, "tm", [(s, s ^ 1) for s in range(tile_count)])

    def hop(value, go):
        pairs = []
        for s in range(tile_count * panel_count):
            sz, sy, sc = s // 8, s // 2 % 2, s % 2
            to = go(sy == sz // 2, sc == sz % 2)
            if to is not None:
                pairs.append((s, s - s % 4 + (sy ^ to[0]) * 2 + (sc ^ to[1])))
        return lax.ppermute(value, AXES, pairs)

    line = [z] + [jnp.array(FROM_Z[turn], jnp.int32)[z] for turn in range(3)]
    shard = jnp.stack([2 * s + i for s in line for i in (x, 1 - x)]).astype(jnp.int32)

    sent = jnp.concatenate([partials, jnp.broadcast_to(observed[:, None], partials.shape)], axis=1)
    sent = jnp.stack([sent, across_x(sent)])
    sent_1, sent_2 = along_z(sent, 0), along_z(sent, 1)
    half = rows_dev // 2
    own_a, own_b = design[:half], design[half:]
    z1a = along_z(own_a, 0)
    x0a = across_x(own_a)
    z2a = along_z(own_a, 1)
    x0b = across_x(own_b)
    sent = jnp.concatenate([sent, sent_1, sent_2, along_z(sent_1, 2)])
    mids = pair_matrices(sent, shard, arc_of_row, autoreg, movavg)
    z3a = along_z(z1a, 2)
    z1b = along_z(tie(own_b, z1a), 0)
    z2b = along_z(tie(own_b, z2a), 1)
    x1a = across_x(tie(z1a, x0a))
    x2a = across_x(tie(z2a, x0b))
    z3b = along_z(z1b, 2)
    x3a = across_x(tie(z3a, x1a))
    x1b = across_x(tie(z1b, x2a))
    x2b = across_x(tie(z2b, x3a))
    x3b = across_x(tie(z3b, x1b))

    pack_meta = jnp.stack([(near & same_core).astype(jnp.int32), x * (width - payload)])

    def spread(*slots):
        mine = pack(pack_meta, slots, payload)
        over = hop(mine, lambda near, same: (1, 0) if near and same else None)
        beside = hop(mine, lambda near, same: (0, 1) if near and same else None)
        both = hop(over, lambda near, same: (0, 1) if not near and same else None)
        return mine, over, beside, both

    groups = [
        spread(own_a, own_b, x0a, x0b, z1a, z2a),
        spread(z3a, x1a, x2a, x3a, z1b, z2b),
        spread(z3b, x1b, x2b),
        spread(x3b),
    ]
    slots_a = (own_a, x0a, z1a, x1a, z2a, x2a, z3a, x3a)
    slots_b = (own_b, x0b, z1b, x1b, z2b, x2b, z3b, x3b)
    places_a = [(0, 0), (0, 2), (0, 4), (1, 1), (0, 5), (1, 2), (1, 0), (1, 3)]
    places_b = [(0, 1), (0, 3), (1, 4), (2, 1), (1, 5), (2, 2), (2, 0), (3, 0)]
    places = [(group, at * half) for group, at in places_a + places_b]

    kind = jnp.where(same_core, jnp.where(near, 0, 1), jnp.where(near, 2, 3))
    meta = jnp.stack([x * (payload - block_columns), kind]).astype(jnp.int32)
    middle_a, rhs_a = middle_rows(shard, mids, 0, slots_a, pair_rows, scale)
    middle_b, rhs_b = middle_rows(shard, mids, half // pair_rows, slots_b, pair_rows, scale)
    normal = tile(meta, (middle_a, middle_b), places, groups, block_columns, scale, 512)
    return normal, (rhs_a + rhs_b)[0]


def line_body(design, partials, observed, arc_of_row, autoreg, movavg):
    tile_count = lax.axis_size("tm")
    rows_dev, width = design.shape
    pair_rows = 2 * rows_dev // tile_count
    pair_count = rows_dev // pair_rows
    size = tile_count * pair_rows
    scale = 1.0 / (rows_dev * tile_count)
    sent = jnp.concatenate([partials, jnp.broadcast_to(observed[:, None], partials.shape)], axis=1)
    sent = lax.all_gather(sent, "tm", axis=0, tiled=False)
    shard = jnp.arange(tile_count, dtype=jnp.int32)
    mids = pair_matrices(sent, shard, arc_of_row, autoreg, movavg)
    panel = lax.all_gather(design, "tm", axis=0, tiled=False)
    whole_rows = lax.all_gather(design, "panel", axis=1, tiled=True)
    block = lax.all_to_all(whole_rows, "tm", split_axis=1, concat_axis=0, tiled=True)
    block = block.reshape(tile_count, rows_dev, -1)

    def one_pair(sums, pair):
        def rows_of(values):
            here = lax.dynamic_slice_in_dim(values, pair * pair_rows, pair_rows, 1)
            return here.reshape(size, values.shape[2])

        product = jnp.dot(mids[pair], rows_of(panel), preferred_element_type=jnp.float32)
        middle = (product[:size] + product[size : 2 * size]).astype(jnp.bfloat16)
        here = lax.dot_general(
            rows_of(block), middle, ROWS_ACROSS, preferred_element_type=jnp.float32
        )
        return (sums[0] + here, sums[1] + jnp.sum(product[2 * size :], axis=0)), None

    start = (jnp.zeros((block.shape[2], width), jnp.float32), jnp.zeros((width,), jnp.float32))
    (normal, right_hand), _ = lax.scan(one_pair, start, jnp.arange(pair_count))
    return normal * scale, right_hand * scale


def solution(mesh):
    in_specs = (P("tm", "panel"), P("tm", None), P("tm"), P(), P(), P())
    out_specs = (P("tm", "panel"), P("panel"))
    body = block_body if (mesh.shape["tm"], mesh.shape["panel"]) == (8, 4) else line_body
    return jax.shard_map(body, mesh=mesh, in_specs=in_specs, out_specs=out_specs, check_vma=False)
```

time: 631 us -> 209 us (0.33)
  waiting for transfers between devices: 500 us -> 44.9 us
  Pallas kernels: 0 us -> 91.3 us
  starting transfers between devices: 11.1 us -> 50 us
  matrix products: 32.2 us -> 0 us
  blocking collectives: 31.6 us -> 0 us
  other arithmetic: 25 us -> 3.87 us
  between operations: 16.3 us -> 3.46 us
    reduce_scatter x1 -> x0, waiting for transfers between devices: 433 us -> none  [body(): lax.psum_scatter((product * scale).astype(jnp.bfloat16), 'tm', scatter_di...]
    pallas_call x0 -> x13, Pallas kernels: none -> 91.3 us  [the longest x4 34.5 us: pair_matrices(): pl.pallas_call(functools.partial(invert_kernel, first, SWEEPS), out_shape...]
    ppermute x0 -> x30, starting transfers between devices: none -> 50 us  [the longest x12 27.1 us: hop(): return lax.ppermute(value, AXES, pairs)]
    all_gather x1 -> x0, waiting for transfers between devices: 48.6 us -> none  [body(): gathered = lax.all_gather(signed_rows, 'panel', axis=1, tiled=True)]
    ppermute x0 -> x30, waiting for transfers between devices: none -> 44.9 us  [the longest x9 24.6 us: along_z(): return lax.ppermute(value, 'tm', pairs)]
    dot_general x9 -> x0, matrix products: 31.9 us -> none  [the longest x1 22.9 us: body(): lax.dot_general(gathered, own_rows, (((0,), (0,)), ((), ())), preferred_e...]
    psum x1 -> x0, blocking collectives: 19.7 us -> none  [body(): right_hand = lax.psum(right_part, 'tm')]
    all_to_all x2 -> x0, waiting for transfers between devices: 18.9 us -> none  [the longest x1 16.2 us: body(): lax.all_to_all(send_design, 'tm', split_axis=0, concat_axis=0, tiled=True)]
  transfers between devices with their start and end apart: 4 -> 30, of which waited for: 4 -> 11; matrix products, arithmetic and copies ran while one was open for 4% -> 4% of each run, Pallas kernels for 0% -> 37%
where the time goes in v1:
time: 209 us; the launch traced here: 208 us
  Pallas kernels  91.3 us (44%)
  starting transfers between devices  50 us (24%)
  waiting for transfers between devices  44.9 us (21%)
  local copies, waits for them, and re-layouts  14.8 us (7%)
  other arithmetic  3.87 us (2%)
  between operations  3.46 us (2%)
    pallas_call x4, Pallas kernels, pair_matrices(): pl.pallas_call(functools.partial(invert_kernel, first, SWEEPS), out_shape...  34.5 us
    ppermute x12, starting transfers between devices, hop(): return lax.ppermute(value, AXES, pairs)  27.1 us
    ppermute x9, waiting for transfers between devices, along_z(): return lax.ppermute(value, 'tm', pairs)  24.6 us
    ppermute x9, waiting for transfers between devices, across_x(): return lax.ppermute(value, 'tm', [(s, s ^ 1) for s in range(tile_count)])  20.3 us
    pallas_call x2, Pallas kernels, middle_rows(): pl.pallas_call(functools.partial(middle_rows_kernel, scale), grid=(pair_c...  16.3 us
    pallas_call x1, Pallas kernels, tile(): pl.pallas_call(functools.partial(tile_kernel, tuple(places), block_column...  15 us
    ppermute x9, starting transfers between devices, across_x(): return lax.ppermute(value, 'tm', [(s, s ^ 1) for s in range(tile_count)])  11.7 us
    ppermute x9, starting transfers between devices, along_z(): return lax.ppermute(value, 'tm', pairs)  11.1 us
  transfers between devices with their start and end apart: 30, of which 11 were waited for; matrix products, arithmetic and copies ran while one was open for 4% of the time, Pallas kernels for 37%

profile of v1, /device:TPU:0, one launch (start us, length us, event | category | flops | bytes accessed | tf_op | source)
XLA Modules:
  0.0 208.3 jit_solution(3963987961765985164)
XLA Ops:
  1.9 4.1 %collective-permute-start.2 = (bf16[128,1920]{1,0:T(8,128)(2,1)S(1)}, bf16[128,1920]{1,0:T(8,128)(2,1)S(1)}, u32[]{:S(2)}, u32[]{:S(2)}) collective-permute-start(bf16[128,1920]{1,0:T(8,128)(2,1)S(1)} %get-tuple-element.35.refs_0_), channel_id=1, source_target_pairs={{8,0},{12,4},{24,8},{28,12},{0,16},{4,20},{16,24},{20,28},{9,1},{1... | collective-permute-start | bytes 1474568 | tf_op jit(solution)/shard_map/ppermute | solution.py:368
  8.1 9.6 %collective-permute-done.2.refs_4_.refs_2_ = bf16[128,1920]{1,0:T(8,128)(2,1)S(1)} collective-permute-done((bf16[128,1920]{1,0:T(8,128)(2,1)S(1)}, bf16[128,1920]{1,0:T(8,128)(2,1)S(1)}, u32[]{:S(2)}, u32[]{:S(2)}) %collective-permute-start.2) | collective-permute-done | bytes 491552 | tf_op jit(solution)/shard_map/ppermute | solution.py:368
  17.7 2.5 %collective-permute-done.refs_2_.refs_1_ = bf16[128,1920]{1,0:T(8,128)(2,1)S(1)} collective-permute-done((bf16[128,1920]{1,0:T(8,128)(2,1)S(1)}, bf16[128,1920]{1,0:T(8,128)(2,1)S(1)}, u32[]{:S(2)}, u32[]{:S(2)}) %collective-permute-start) | collective-permute-done | bytes 491552 | tf_op jit(solution)/shard_map/ppermute | solution.py:371
  23.2 6.8 %collective-permute-done.3.refs_5_.refs_4_ = bf16[128,1920]{1,0:T(8,128)(2,1)S(1)} collective-permute-done((bf16[128,1920]{1,0:T(8,128)(2,1)S(1)}, bf16[128,1920]{1,0:T(8,128)(2,1)S(1)}, u32[]{:S(2)}, u32[]{:S(2)}) %collective-permute-start.3) | collective-permute-done | bytes 491552 | tf_op jit(solution)/shard_map/ppermute | solution.py:368
  34.2 7.0 %collective-permute-done.8.refs_1_.refs_3_ = bf16[128,1920]{1,0:T(8,128)(2,1)S(1)} collective-permute-done((bf16[128,1920]{1,0:T(8,128)(2,1)S(1)}, bf16[128,1920]{1,0:T(8,128)(2,1)S(1)}, u32[]{:S(2)}, u32[]{:S(2)}) %collective-permute-start.8) | collective-permute-done | bytes 491552 | tf_op jit(solution)/shard_map/ppermute | solution.py:371
  42.9 9.0 %collective-permute-done.9.refs_2_.refs_5_ = bf16[128,1920]{1,0:T(8,128)(2,1)} collective-permute-done((bf16[128,1920]{1,0:T(8,128)(2,1)S(1)}, bf16[128,1920]{1,0:T(8,128)(2,1)}, u32[]{:S(2)}, u32[]{:S(2)}) %collective-permute-start.9) | collective-permute-done | bytes 491552 | tf_op jit(solution)/shard_map/ppermute | solution.py:371
  57.1 2.9 %pack.4.refs_0_ = bf16[768,1024]{1,0:T(8,128)(2,1)} custom-call(s32[2]{0:T(128)} %pad_add_fusion.1.meta_ref, bf16[128,1920]{1,0:T(8,128)(2,1)} %copy-done.5, bf16[128,1920]{1,0:T(8,128)(2,1)} %copy-done.3, bf16[128,1920]{1,0:T(8,128)(2,1)} %copy-done.19, bf16[128,1920]{1,0:T(8,128)(2,1)} %copy-done.17, bf16[128,1920]{1,0:T(8,128)(2,1)} %copy-done.15, ...), custom_call_target="tpu_custom_call" | custom-call | tf_op jit(solution)/shard_map/pack/pallas_call | solution.py:215
  61.8 4.6 %collective-permute-start.4 = (bf16[768,1024]{1,0:T(8,128)(2,1)}, bf16[768,1024]{1,0:T(8,128)(2,1)}, u32[]{:S(2)}, u32[]{:S(2)}) collective-permute-start(bf16[768,1024]{1,0:T(8,128)(2,1)} %pack.4.refs_0_), channel_id=1, source_target_pairs={{0,2},{4,6},{9,11},{13,15},{18,16},{22,20},{27,25},{31,29}} | collective-permute-start | bytes 4718600 | tf_op jit(solution)/shard_map/ppermute | solution.py:380
  66.4 2.5 %collective-permute-start.5 = (bf16[768,1024]{1,0:T(8,128)(2,1)}, bf16[768,1024]{1,0:T(8,128)(2,1)}, u32[]{:S(2)}, u32[]{:S(2)}) collective-permute-start(bf16[768,1024]{1,0:T(8,128)(2,1)} %pack.4.refs_0_), channel_id=1, source_target_pairs={{0,1},{4,5},{9,8},{13,12},{18,19},{22,23},{27,26},{31,30}} | collective-permute-start | bytes 4718600 | tf_op jit(solution)/shard_map/ppermute | solution.py:380
  68.9 2.9 %pack.5.refs_4_ = bf16[768,1024]{1,0:T(8,128)(2,1)} custom-call(s32[2]{0:T(128)} %pad_add_fusion.1.meta_ref, bf16[128,1920]{1,0:T(8,128)(2,1)} %collective-permute-done.7.refs_0_.refs_6_, bf16[128,1920]{1,0:T(8,128)(2,1)} %copy-done.23, bf16[128,1920]{1,0:T(8,128)(2,1)} %collective-permute-done.9.refs_2_.refs_5_, ...), custom_call_target="tpu_custom_call" | custom-call | tf_op jit(solution)/shard_map/pack/pallas_call | solution.py:215
  72.9 4.6 %collective-permute-start.13 = (bf16[768,1024]{1,0:T(8,128)(2,1)}, bf16[768,1024]{1,0:T(8,128)(2,1)}, u32[]{:S(2)}, u32[]{:S(2)}) collective-permute-start(bf16[768,1024]{1,0:T(8,128)(2,1)} %pack.5.refs_4_), channel_id=1, source_target_pairs={{0,2},{4,6},{9,11},{13,15},{18,16},{22,20},{27,25},{31,29}} | collective-permute-start | bytes 4718600 | tf_op jit(solution)/shard_map/ppermute | solution.py:380
  80.1 4.4 %collective-permute-done.27 = bf16[2,256,128]{2,1,0:T(8,128)(2,1)S(1)} collective-permute-done((bf16[2,256,128]{2,1,0:T(8,128)(2,1)S(1)}, bf16[2,256,128]{2,1,0:T(8,128)(2,1)S(1)}, u32[]{:S(2)}, u32[]{:S(2)}) %collective-permute-start.27) | collective-permute-done | bytes 131104 | tf_op jit(solution)/shard_map/ppermute | solution.py:368
  92.8 1.8 collective-permute-start.29
  94.7 2.3 %pack.7.refs_12_ = bf16[128,1024]{1,0:T(8,128)(2,1)} custom-call(s32[2]{0:T(128)} %pad_add_fusion.1.meta_ref, bf16[128,1920]{1,0:T(8,128)(2,1)} %copy-done.13), custom_call_target="tpu_custom_call" | custom-call | tf_op jit(solution)/shard_map/pack/pallas_call | solution.py:215
  97.8 2.6 %collective-permute-start.23 = (bf16[128,1024]{1,0:T(8,128)(2,1)}, bf16[128,1024]{1,0:T(8,128)(2,1)}, u32[]{:S(2)}, u32[]{:S(2)}) collective-permute-start(bf16[128,1024]{1,0:T(8,128)(2,1)} %pack.7.refs_12_), channel_id=1, source_target_pairs={{0,2},{4,6},{9,11},{13,15},{18,16},{22,20},{27,25},{31,29}} | collective-permute-start | bytes 786440 | tf_op jit(solution)/shard_map/ppermute | solution.py:380
  100.5 8.0 %whiten.1 = (f32[4,128,128]{2,1,0:T(8,128)S(1)}, f32[4,128,512]{2,1,0:T(8,128)S(1)}, f32[4,512,512]{2,1,0:T(8,128)S(1)}, bf16[4,16,512]{2,1,0:T(8,128)(2,1)S(1)}) custom-call(s32[8]{0:T(128)S(1)} %stack.81.shard_ref, s32[4]{0:T(128)S(1)} %convert_reduce_fusion.length_ref, f32[8]{0:T(128)S(1)} %get-tuple-element.43.gain_ref, f32[8]{0:T(128)S(1)} %get-tuple-element.42.log_ref, ...), custom_call_target="tpu_custom_call" | custom-call | tf_op jit(solution)/shard_map/whiten/pallas_call | solution.py:141
  108.5 2.0 copy-done.1
  111.3 2.6 %pack.6.refs_8_ = bf16[384,1024]{1,0:T(8,128)(2,1)} custom-call(s32[2]{0:T(128)} %pad_add_fusion.1.meta_ref, bf16[128,1920]{1,0:T(8,128)(2,1)} %copy-done.9, bf16[128,1920]{1,0:T(8,128)(2,1)} %copy-done.7, bf16[128,1920]{1,0:T(8,128)(2,1)} %copy-done.11), custom_call_target="tpu_custom_call" | custom-call | tf_op jit(solution)/shard_map/pack/pallas_call | solution.py:215
  113.9 2.2 %collective-permute-start.19 = (bf16[384,1024]{1,0:T(8,128)(2,1)}, bf16[384,1024]{1,0:T(8,128)(2,1)}, u32[]{:S(2)}, u32[]{:S(2)}) collective-permute-start(bf16[384,1024]{1,0:T(8,128)(2,1)} %pack.6.refs_8_), channel_id=1, source_target_pairs={{0,2},{4,6},{9,11},{13,15},{18,16},{22,20},{27,25},{31,29}} | collective-permute-start | bytes 2359304 | tf_op jit(solution)/shard_map/ppermute | solution.py:380
  116.2 2.5 %collective-permute-start.14 = (bf16[768,1024]{1,0:T(8,128)(2,1)}, bf16[768,1024]{1,0:T(8,128)(2,1)}, u32[]{:S(2)}, u32[]{:S(2)}) collective-permute-start(bf16[768,1024]{1,0:T(8,128)(2,1)} %pack.5.refs_4_), channel_id=1, source_target_pairs={{0,1},{4,5},{9,8},{13,12},{18,19},{22,23},{27,26},{31,30}} | collective-permute-start | bytes 4718600 | tf_op jit(solution)/shard_map/ppermute | solution.py:380
  120.0 1.8 collective-permute-start.6
  121.8 1.8 collective-permute-start.15
  124.5 8.6 %invert.4.gram_ref = f32[64,8,64]{2,1,0:T(8,128)} custom-call(f32[64,8,64]{2,1,0:T(8,128)} %bitcast.36), custom_call_target="tpu_custom_call" | custom-call | tf_op jit(solution)/shard_map/invert/pallas_call | solution.py:166
  133.1 8.6 %invert.5.gram_ref = f32[64,8,64]{2,1,0:T(8,128)} custom-call(f32[64,8,64]{2,1,0:T(8,128)} %invert.4.gram_ref), custom_call_target="tpu_custom_call" | custom-call | tf_op jit(solution)/shard_map/invert/pallas_call | solution.py:166
  141.7 8.8 %invert.6.gram_ref = f32[64,8,64]{2,1,0:T(8,128)} custom-call(f32[64,8,64]{2,1,0:T(8,128)} %invert.5.gram_ref), custom_call_target="tpu_custom_call" | custom-call | tf_op jit(solution)/shard_map/invert/pallas_call | solution.py:166
  150.4 8.6 %invert.7 = f32[64,8,64]{2,1,0:T(8,128)} custom-call(f32[64,8,64]{2,1,0:T(8,128)} %invert.6.gram_ref), custom_call_target="tpu_custom_call" | custom-call | tf_op jit(solution)/shard_map/invert/pallas_call | solution.py:166
  161.1 2.2 %copy-done.2 = f32[4,512,512]{2,1,0:T(8,128)S(1)} copy-done((f32[4,512,512]{2,1,0:T(8,128)S(1)}, f32[4,512,512]{2,1,0:T(8,128)}, u32[]{:S(2)}) %copy-start.2) | copy-done | bytes 4194328
  163.3 6.8 %middle.1.mid_ref = bf16[4,1040,512]{2,1,0:T(8,128)(2,1)S(1)} custom-call(f32[4,128,512]{2,1,0:T(8,128)S(1)} %get-tuple-element.26.across_ref, f32[4,128,128]{2,1,0:T(8,128)S(1)} %select_maximum_fusion.minus_inverse_ref, f32[4,512,512]{2,1,0:T(8,128)S(1)} %copy-done.2, bf16[4,16,512]{2,1,0:T(8,128)(2,1)S(1)} %get-tuple-element.29.obs_ref), custom_call_target="tpu_custom_call" | custom-call | tf_op jit(solution)/shard_map/middle/pallas_call | solution.py:180
  170.2 2.0 copy-done
  174.9 8.2 %middle_rows.2 = (bf16[8,128,1920]{2,1,0:T(8,128)(2,1)}, f32[1,1920]{1,0:T(1,128)S(1)}) custom-call(s32[8]{0:T(128)S(1)} %stack.81.shard_ref, bf16[4,1040,512]{2,1,0:T(8,128)(2,1)} %copy-done, bf16[128,1920]{1,0:T(8,128)(2,1)S(1)} %copy-done.6, bf16[128,1920]{1,0:T(8,128)(2,1)S(1)} %copy-done.20, bf16[128,1920]{1,0:T(8,128)(2,1)S(1)} %copy-done.16, ...), custom_call_target="tpu_custom_call" | custom-call | flops 4089446400 | bytes 7864320 | tf_op jit(solution)/shard_map/middle_rows/pallas_call | solution.py:257
  183.2 8.2 %middle_rows.3 = (bf16[8,128,1920]{2,1,0:T(8,128)(2,1)}, f32[1,1920]{1,0:T(1,128)S(1)}) custom-call(s32[8]{0:T(128)S(1)} %stack.81.shard_ref, bf16[4,1040,512]{2,1,0:T(8,128)(2,1)} %copy-done, bf16[128,1920]{1,0:T(8,128)(2,1)S(1)} %copy-done.4, bf16[128,1920]{1,0:T(8,128)(2,1)S(1)} %copy-done.18, bf16[128,1920]{1,0:T(8,128)(2,1)} %collective-permute-done.11.refs_4_.refs_2_, ...), custom_call_target="tpu_custom_call" | custom-call | flops 4089446400 | bytes 7864320 | tf_op jit(solution)/shard_map/middle_rows/pallas_call | solution.py:257
  193.1 15.0 %tile.1 = f32[960,1920]{1,0:T(8,128)} custom-call(s32[2]{0:T(128)} %pad_add_fusion.meta_ref, bf16[768,1024]{1,0:T(8,128)(2,1)} %pack.4.refs_0_, bf16[768,1024]{1,0:T(8,128)(2,1)} %collective-permute-done.4.refs_1_, bf16[768,1024]{1,0:T(8,128)(2,1)} %collective-permute-done.5.refs_2_, bf16[768,1024]{1,0:T(8,128)(2,1)} %collective-permute-done.6.refs_3_, ...), custom_call_target="tpu_custom_call" | custom-call | flops 7549747200 | bytes 19431424 | tf_op jit(solution)/shard_map/tile/pallas_call | solution.py:328
  (151 shorter events, 39.5 us)
Async XLA Ops:
  1.9 55.2 %copy-start.3 = (bf16[128,1920]{1,0:T(8,128)(2,1)}, bf16[128,1920]{1,0:T(8,128)(2,1)S(1)}, u32[]{:S(2)}) copy-start(bf16[128,1920]{1,0:T(8,128)(2,1)S(1)} %get-tuple-element.22.refs_1_.refs_0_) | copy-start | bytes 1474564
  1.9 55.2 %copy-start.5 = (bf16[128,1920]{1,0:T(8,128)(2,1)}, bf16[128,1920]{1,0:T(8,128)(2,1)S(1)}, u32[]{:S(2)}) copy-start(bf16[128,1920]{1,0:T(8,128)(2,1)S(1)} %get-tuple-element.35.refs_0_) | copy-start | bytes 1474564
  1.9 15.8 %collective-permute-start.2 = (bf16[128,1920]{1,0:T(8,128)(2,1)S(1)}, bf16[128,1920]{1,0:T(8,128)(2,1)S(1)}, u32[]{:S(2)}, u32[]{:S(2)}) collective-permute-start(bf16[128,1920]{1,0:T(8,128)(2,1)S(1)} %get-tuple-element.35.refs_0_), channel_id=1, source_target_pairs={{8,0},{12,4},{24,8},{28,12},{0,16},{4,20},{16,24},{20,28},{9,1},{1... | collective-permute-start | bytes 1474568 | tf_op jit(solution)/shard_map/ppermute | solution.py:368
  6.0 14.1 %collective-permute-start = (bf16[128,1920]{1,0:T(8,128)(2,1)S(1)}, bf16[128,1920]{1,0:T(8,128)(2,1)S(1)}, u32[]{:S(2)}, u32[]{:S(2)}) collective-permute-start(bf16[128,1920]{1,0:T(8,128)(2,1)S(1)} %get-tuple-element.35.refs_0_), channel_id=1, source_target_pairs={{0,4},{4,0},{8,12},{12,8},{16,20},{20,16},{24,28},{28,24},{1,5},{5... | collective-permute-start | bytes 1474568 | tf_op jit(solution)/shard_map/ppermute | solution.py:371
  7.5 22.5 %collective-permute-start.3 = (bf16[128,1920]{1,0:T(8,128)(2,1)S(1)}, bf16[128,1920]{1,0:T(8,128)(2,1)S(1)}, u32[]{:S(2)}, u32[]{:S(2)}) collective-permute-start(bf16[128,1920]{1,0:T(8,128)(2,1)S(1)} %get-tuple-element.35.refs_0_), channel_id=1, source_target_pairs={{16,0},{20,4},{0,8},{4,12},{24,16},{28,20},{8,24},{12,28},{17,1},{... | collective-permute-start | bytes 1474568 | tf_op jit(solution)/shard_map/ppermute | solution.py:368
  7.5 23.2 %collective-permute-start.1 = (bf16[128,1920]{1,0:T(8,128)(2,1)S(1)}, bf16[128,1920]{1,0:T(8,128)(2,1)S(1)}, u32[]{:S(2)}, u32[]{:S(2)}) collective-permute-start(bf16[128,1920]{1,0:T(8,128)(2,1)S(1)} %get-tuple-element.22.refs_1_.refs_0_), channel_id=1, source_target_pairs={{0,4},{4,0},{8,12},{12,8},{16,20},{20,16},{24,28},{28,24},{1,5},{5... | collective-permute-start | bytes 1474568 | tf_op jit(solution)/shard_map/ppermute | solution.py:371
  20.2 21.1 %collective-permute-start.8 = (bf16[128,1920]{1,0:T(8,128)(2,1)S(1)}, bf16[128,1920]{1,0:T(8,128)(2,1)S(1)}, u32[]{:S(2)}, u32[]{:S(2)}) collective-permute-start(bf16[128,1920]{1,0:T(8,128)(2,1)S(1)} %collective-permute-done.2.refs_4_.refs_2_), channel_id=1, source_target_pairs={{0,4},{4,0},{8,12},{12,8},{16,20},{20,16},{24,28},{28,24},{1,5},{5... | collective-permute-start | bytes 1474568 | tf_op jit(solution)/shard_map/ppermute | solution.py:371
  21.7 19.6 %collective-permute-start.7 = (bf16[128,1920]{1,0:T(8,128)(2,1)S(1)}, bf16[128,1920]{1,0:T(8,128)(2,1)}, u32[]{:S(2)}, u32[]{:S(2)}) collective-permute-start(bf16[128,1920]{1,0:T(8,128)(2,1)S(1)} %collective-permute-done.2.refs_4_.refs_2_), channel_id=1, source_target_pairs={{8,0},{12,4},{24,8},{28,12},{0,16},{4,20},{16,24},{20,28},{9,1},{1... | collective-permute-start | bytes 1474568 | tf_op jit(solution)/shard_map/ppermute | solution.py:368
  30.7 21.2 %collective-permute-start.9 = (bf16[128,1920]{1,0:T(8,128)(2,1)S(1)}, bf16[128,1920]{1,0:T(8,128)(2,1)}, u32[]{:S(2)}, u32[]{:S(2)}) collective-permute-start(bf16[128,1920]{1,0:T(8,128)(2,1)S(1)} %collective-permute-done.3.refs_5_.refs_4_), channel_id=1, source_target_pairs={{0,4},{4,0},{8,12},{12,8},{16,20},{20,16},{24,28},{28,24},{1,5},{5... | collective-permute-start | bytes 1474568 | tf_op jit(solution)/shard_map/ppermute | solution.py:371
  32.2 19.7 %collective-permute-start.11 = (bf16[128,1920]{1,0:T(8,128)(2,1)S(1)}, bf16[128,1920]{1,0:T(8,128)(2,1)}, u32[]{:S(2)}, u32[]{:S(2)}) collective-permute-start(bf16[128,1920]{1,0:T(8,128)(2,1)S(1)} %get-tuple-element.22.refs_1_.refs_0_), channel_id=1, source_target_pairs={{8,0},{12,4},{24,8},{28,12},{0,16},{4,20},{16,24},{20,28},{9,1},{1... | collective-permute-start | bytes 1474568 | tf_op jit(solution)/shard_map/ppermute | solution.py:368
  33.8 28.0 %collective-permute-start.12 = (bf16[128,1920]{1,0:T(8,128)(2,1)S(1)}, bf16[128,1920]{1,0:T(8,128)(2,1)}, u32[]{:S(2)}, u32[]{:S(2)}) collective-permute-start(bf16[128,1920]{1,0:T(8,128)(2,1)S(1)} %get-tuple-element.22.refs_1_.refs_0_), channel_id=1, source_target_pairs={{16,0},{20,4},{0,8},{4,12},{24,16},{28,20},{8,24},{12,28},{17,1},{... | collective-permute-start | bytes 1474568 | tf_op jit(solution)/shard_map/ppermute | solution.py:368
  41.2 25.1 %collective-permute-start.10 = (bf16[128,1920]{1,0:T(8,128)(2,1)}, bf16[128,1920]{1,0:T(8,128)(2,1)}, u32[]{:S(2)}, u32[]{:S(2)}) collective-permute-start(bf16[128,1920]{1,0:T(8,128)(2,1)} %collective-permute-done.7.refs_0_.refs_6_), channel_id=1, source_target_pairs={{0,4},{4,0},{8,12},{12,8},{16,20},{20,16},{24,28},{28,24},{1,5},{5... | collective-permute-start | bytes 1474568 | tf_op jit(solution)/shard_map/ppermute | solution.py:371
  51.9 26.4 %collective-permute-start.17 = (bf16[128,1920]{1,0:T(8,128)(2,1)}, bf16[128,1920]{1,0:T(8,128)(2,1)S(1)}, u32[]{:S(2)}, u32[]{:S(2)}) collective-permute-start(bf16[128,1920]{1,0:T(8,128)(2,1)} %collective-permute-done.11.refs_4_.refs_2_), channel_id=1, source_target_pairs={{0,4},{4,0},{8,12},{12,8},{16,20},{20,16},{24,28},{28,24},{1,5},{5... | collective-permute-start | bytes 1474568 | tf_op jit(solution)/shard_map/ppermute | solution.py:371
  54.3 18.6 %collective-permute-start.26 = (bf16[256,128]{1,0:T(8,128)(2,1)}, bf16[256,128]{1,0:T(8,128)(2,1)}, u32[]{:S(2)}, u32[]{:S(2)}) collective-permute-start(bf16[256,128]{1,0:T(8,128)(2,1)} %get-tuple-element.41), channel_id=1, source_target_pairs={{0,4},{4,0},{8,12},{12,8},{16,20},{20,16},{24,28},{28,24},{1,5},{5... | collective-permute-start | bytes 196616 | tf_op jit(solution)/shard_map/ppermute | solution.py:371
  54.8 23.7 %collective-permute-start.16 = (bf16[128,1920]{1,0:T(8,128)(2,1)}, bf16[128,1920]{1,0:T(8,128)(2,1)S(1)}, u32[]{:S(2)}, u32[]{:S(2)}) collective-permute-start(bf16[128,1920]{1,0:T(8,128)(2,1)} %collective-permute-done.11.refs_4_.refs_2_), channel_id=1, source_target_pairs={{8,0},{12,4},{24,8},{28,12},{0,16},{4,20},{16,24},{20,28},{9,1},{1... | collective-permute-start | bytes 1474568 | tf_op jit(solution)/shard_map/ppermute | solution.py:368
  61.8 54.4 %collective-permute-start.4 = (bf16[768,1024]{1,0:T(8,128)(2,1)}, bf16[768,1024]{1,0:T(8,128)(2,1)}, u32[]{:S(2)}, u32[]{:S(2)}) collective-permute-start(bf16[768,1024]{1,0:T(8,128)(2,1)} %pack.4.refs_0_), channel_id=1, source_target_pairs={{0,2},{4,6},{9,11},{13,15},{18,16},{22,20},{27,25},{31,29}} | collective-permute-start | bytes 4718600 | tf_op jit(solution)/shard_map/ppermute | solution.py:380
  66.4 52.3 %collective-permute-start.5 = (bf16[768,1024]{1,0:T(8,128)(2,1)}, bf16[768,1024]{1,0:T(8,128)(2,1)}, u32[]{:S(2)}, u32[]{:S(2)}) collective-permute-start(bf16[768,1024]{1,0:T(8,128)(2,1)} %pack.4.refs_0_), channel_id=1, source_target_pairs={{0,1},{4,5},{9,8},{13,12},{18,19},{22,23},{27,26},{31,30}} | collective-permute-start | bytes 4718600 | tf_op jit(solution)/shard_map/ppermute | solution.py:380
  72.9 48.9 %collective-permute-start.13 = (bf16[768,1024]{1,0:T(8,128)(2,1)}, bf16[768,1024]{1,0:T(8,128)(2,1)}, u32[]{:S(2)}, u32[]{:S(2)}) collective-permute-start(bf16[768,1024]{1,0:T(8,128)(2,1)} %pack.5.refs_4_), channel_id=1, source_target_pairs={{0,2},{4,6},{9,11},{13,15},{18,16},{22,20},{27,25},{31,29}} | collective-permute-start | bytes 4718600 | tf_op jit(solution)/shard_map/ppermute | solution.py:380
  78.3 6.2 %collective-permute-start.27 = (bf16[2,256,128]{2,1,0:T(8,128)(2,1)S(1)}, bf16[2,256,128]{2,1,0:T(8,128)(2,1)S(1)}, u32[]{:S(2)}, u32[]{:S(2)}) collective-permute-start(bf16[2,256,128]{2,1,0:T(8,128)(2,1)S(1)} %pad_maximum_fusion.1), channel_id=1, source_target_pairs={{8,0},{12,4},{24,8},{28,12},{0,16},{4,20},{16,24},{20,28},{9,1},{1... | collective-permute-start | bytes 393224 | tf_op jit(solution)/shard_map/ppermute | solution.py:368
  78.5 14.3 %collective-permute-start.22 = (bf16[128,1920]{1,0:T(8,128)(2,1)S(1)}, bf16[128,1920]{1,0:T(8,128)(2,1)S(1)}, u32[]{:S(2)}, u32[]{:S(2)}) collective-permute-start(bf16[128,1920]{1,0:T(8,128)(2,1)S(1)} %collective-permute-done.16.refs_0_.refs_6_), channel_id=1, source_target_pairs={{0,4},{4,0},{8,12},{12,8},{16,20},{20,16},{24,28},{28,24},{1,5},{5... | collective-permute-start | bytes 1474568 | tf_op jit(solution)/shard_map/ppermute | solution.py:371
  84.5 5.9 %collective-permute-start.28 = (bf16[2,256,128]{2,1,0:T(8,128)(2,1)S(1)}, bf16[2,256,128]{2,1,0:T(8,128)(2,1)S(1)}, u32[]{:S(2)}, u32[]{:S(2)}) collective-permute-start(bf16[2,256,128]{2,1,0:T(8,128)(2,1)S(1)} %pad_maximum_fusion.1), channel_id=1, source_target_pairs={{16,0},{20,4},{0,8},{4,12},{24,16},{28,20},{8,24},{12,28},{17,1},{... | collective-permute-start | bytes 393224 | tf_op jit(solution)/shard_map/ppermute | solution.py:368
  90.4 20.1 %collective-permute-start.18 = (bf16[128,1920]{1,0:T(8,128)(2,1)}, bf16[128,1920]{1,0:T(8,128)(2,1)S(1)}, u32[]{:S(2)}, u32[]{:S(2)}) collective-permute-start(bf16[128,1920]{1,0:T(8,128)(2,1)} %collective-permute-done.12.refs_5_.refs_4_), channel_id=1, source_target_pairs={{0,4},{4,0},{8,12},{12,8},{16,20},{20,16},{24,28},{28,24},{1,5},{5... | collective-permute-start | bytes 1474568 | tf_op jit(solution)/shard_map/ppermute | solution.py:371
  92.8 5.0 %collective-permute-start.29 = (bf16[2,256,128]{2,1,0:T(8,128)(2,1)S(1)}, bf16[2,256,128]{2,1,0:T(8,128)(2,1)S(1)}, u32[]{:S(2)}, u32[]{:S(2)}) collective-permute-start(bf16[2,256,128]{2,1,0:T(8,128)(2,1)S(1)} %collective-permute-done.27), channel_id=1, source_target_pairs={{8,0},{12,4},{24,8},{28,12},{0,16},{4,20},{16,24},{20,28},{9,1},{1... | collective-permute-start | bytes 393224 | tf_op jit(solution)/shard_map/ppermute | solution.py:368
  97.8 22.1 %collective-permute-start.23 = (bf16[128,1024]{1,0:T(8,128)(2,1)}, bf16[128,1024]{1,0:T(8,128)(2,1)}, u32[]{:S(2)}, u32[]{:S(2)}) collective-permute-start(bf16[128,1024]{1,0:T(8,128)(2,1)} %pack.7.refs_12_), channel_id=1, source_target_pairs={{0,2},{4,6},{9,11},{13,15},{18,16},{22,20},{27,25},{31,29}} | collective-permute-start | bytes 786440 | tf_op jit(solution)/shard_map/ppermute | solution.py:380
  113.9 60.0 %collective-permute-start.19 = (bf16[384,1024]{1,0:T(8,128)(2,1)}, bf16[384,1024]{1,0:T(8,128)(2,1)}, u32[]{:S(2)}, u32[]{:S(2)}) collective-permute-start(bf16[384,1024]{1,0:T(8,128)(2,1)} %pack.6.refs_8_), channel_id=1, source_target_pairs={{0,2},{4,6},{9,11},{13,15},{18,16},{22,20},{27,25},{31,29}} | collective-permute-start | bytes 2359304 | tf_op jit(solution)/shard_map/ppermute | solution.py:380
  116.2 75.8 %collective-permute-start.14 = (bf16[768,1024]{1,0:T(8,128)(2,1)}, bf16[768,1024]{1,0:T(8,128)(2,1)}, u32[]{:S(2)}, u32[]{:S(2)}) collective-permute-start(bf16[768,1024]{1,0:T(8,128)(2,1)} %pack.5.refs_4_), channel_id=1, source_target_pairs={{0,1},{4,5},{9,8},{13,12},{18,19},{22,23},{27,26},{31,30}} | collective-permute-start | bytes 4718600 | tf_op jit(solution)/shard_map/ppermute | solution.py:380
  118.6 41.6 %collective-permute-start.24 = (bf16[128,1024]{1,0:T(8,128)(2,1)S(1)}, bf16[128,1024]{1,0:T(8,128)(2,1)S(1)}, u32[]{:S(2)}, u32[]{:S(2)}) collective-permute-start(bf16[128,1024]{1,0:T(8,128)(2,1)S(1)} %copy-done.26), channel_id=1, source_target_pairs={{0,1},{4,5},{9,8},{13,12},{18,19},{22,23},{27,26},{31,30}} | collective-permute-start | bytes 786440 | tf_op jit(solution)/shard_map/ppermute | solution.py:380
  120.0 72.0 %collective-permute-start.6 = (bf16[768,1024]{1,0:T(8,128)(2,1)}, bf16[768,1024]{1,0:T(8,128)(2,1)}, u32[]{:S(2)}, u32[]{:S(2)}) collective-permute-start(bf16[768,1024]{1,0:T(8,128)(2,1)} %collective-permute-done.4.refs_1_), channel_id=1, source_target_pairs={{2,3},{6,7},{11,10},{15,14},{16,17},{20,21},{25,24},{29,28}} | collective-permute-start | bytes 4718600 | tf_op jit(solution)/shard_map/ppermute | solution.py:380
  121.8 70.2 %collective-permute-start.15 = (bf16[768,1024]{1,0:T(8,128)(2,1)}, bf16[768,1024]{1,0:T(8,128)(2,1)}, u32[]{:S(2)}, u32[]{:S(2)}) collective-permute-start(bf16[768,1024]{1,0:T(8,128)(2,1)} %collective-permute-done.13.refs_5_), channel_id=1, source_target_pairs={{2,3},{6,7},{11,10},{15,14},{16,17},{20,21},{25,24},{29,28}} | collective-permute-start | bytes 4718600 | tf_op jit(solution)/shard_map/ppermute | solution.py:380
  160.3 11.9 %collective-permute-start.25 = (bf16[128,1024]{1,0:T(8,128)(2,1)}, bf16[128,1024]{1,0:T(8,128)(2,1)S(1)}, u32[]{:S(2)}, u32[]{:S(2)}) collective-permute-start(bf16[128,1024]{1,0:T(8,128)(2,1)} %collective-permute-done.23.refs_13_), channel_id=1, source_target_pairs={{2,3},{6,7},{11,10},{15,14},{16,17},{20,21},{25,24},{29,28}} | collective-permute-start | bytes 786440 | tf_op jit(solution)/shard_map/ppermute | solution.py:380
  172.3 19.7 %collective-permute-start.20 = (bf16[384,1024]{1,0:T(8,128)(2,1)S(1)}, bf16[384,1024]{1,0:T(8,128)(2,1)S(1)}, u32[]{:S(2)}, u32[]{:S(2)}) collective-permute-start(bf16[384,1024]{1,0:T(8,128)(2,1)S(1)} %copy-done.25), channel_id=1, source_target_pairs={{0,1},{4,5},{9,8},{13,12},{18,19},{22,23},{27,26},{31,30}} | collective-permute-start | bytes 2359304 | tf_op jit(solution)/shard_map/ppermute | solution.py:380
  173.9 18.1 %collective-permute-start.21 = (bf16[384,1024]{1,0:T(8,128)(2,1)}, bf16[384,1024]{1,0:T(8,128)(2,1)S(1)}, u32[]{:S(2)}, u32[]{:S(2)}) collective-permute-start(bf16[384,1024]{1,0:T(8,128)(2,1)} %collective-permute-done.19.refs_9_), channel_id=1, source_target_pairs={{2,3},{6,7},{11,10},{15,14},{16,17},{20,21},{25,24},{29,28}} | collective-permute-start | bytes 2359304 | tf_op jit(solution)/shard_map/ppermute | solution.py:380
  (40 other events, 646.1 us)

commit v2 on v1

v2 whole, which is shorter than its diff:
```python
import functools

import jax
import jax.numpy as jnp
from jax import lax
from jax.experimental import pallas as pl
from jax.experimental.pallas import tpu as pltpu
from jax.sharding import PartitionSpec as P

AXES = ("tm", "panel")
HIGHEST = lax.Precision.HIGHEST
ROWS_ACROSS = (((0,), (0,)), ((), ()))
EXTRA = 128
HBM = pl.BlockSpec(memory_space=pl.ANY)
SMEM = pl.BlockSpec(memory_space=pltpu.SMEM)
SEND_Z = (((1, 0), (3, 1), (0, 2), (2, 3)), ((2, 0), (0, 1), (3, 2), (1, 3)), ((1, 0), (3, 1), (0, 2), (2, 3)), ((3, 0), (2, 1), (1, 2), (0, 3)))


COST = 1e9
SMALL = 0.5
ROWS = 12


def cost(micros):
    return pl.CostEstimate(flops=int(micros * COST), bytes_accessed=0, transcendentals=0)


def params(mib, **more):
    return pltpu.CompilerParams(vmem_limit_bytes=mib * 1024 * 1024, **more)


def whiten(meta_ref, length_ref, gain_ref, log_ref, slots, pair, held, gram_ref, across_ref, square_ref):
    size, width = held.shape
    slots = [(ref, n) for ref in slots for n in range(ref.shape[0])]
    tile_count = len(slots)
    pair_rows = size // tile_count
    shift = pair_rows.bit_length() - 1
    at = pair + meta_ref[tile_count]
    length = length_ref[at]

    def epoch(shape, axis):
        index = lax.broadcasted_iota(jnp.int32, shape, axis)
        return jnp.bitwise_and(index, pair_rows - 1) * tile_count + jnp.right_shift(index, shift)

    epoch_row, epoch_col = epoch((size, 1), 0), epoch((1, size), 1)
    first_row = jnp.where(epoch_row < length, 1, 0)
    first_col = jnp.where(epoch_col < length, 1, 0)
    gain = jnp.where(epoch_row < length, gain_ref[2 * at], gain_ref[2 * at + 1])
    log_ma = jnp.where(epoch_row < length, log_ref[2 * at], log_ref[2 * at + 1])
    spacing = epoch_row - epoch_col
    lag = jnp.maximum(spacing - 1, 0)
    size_of = gain * jnp.exp(lag.astype(jnp.float32) * log_ma)
    decayed = jnp.where(jnp.bitwise_and(lag, 1) == 1, size_of, -size_of)
    entry = jnp.where(spacing == 0, jnp.float32(1.0), decayed)
    allowed = (first_row == first_col) & (spacing >= 0)
    whitener = jnp.where(allowed, entry, jnp.float32(0.0)).astype(jnp.bfloat16)

    for n, (ref, shard) in enumerate(slots):
        place = pl.ds(pl.multiple_of(meta_ref[n] * pair_rows, pair_rows), pair_rows)
        source = pl.ds(pl.multiple_of(pair * pair_rows, pair_rows), pair_rows)
        held[place, :] = ref[shard, source].astype(jnp.float32)
    rows = held[...]
    obs = rows.astype(jnp.bfloat16)
    lane = lax.broadcasted_iota(jnp.int32, (size, width), 1)
    in_first = jnp.where(lane < width // 2, 1, 0)
    rows = jnp.where(in_first == 1, rows, pltpu.roll(rows, width // 2, axis=1))
    rows = jnp.where(in_first == first_row, rows, 0.0).astype(jnp.bfloat16)
    white = jnp.dot(whitener, rows, preferred_element_type=jnp.float32)
    eye = lax.broadcasted_iota(jnp.int32, (width, width), 0) == lax.broadcasted_iota(
        jnp.int32, (width, width), 1
    )
    gram = lax.dot_general(
        white, white, ROWS_ACROSS, precision=HIGHEST, preferred_element_type=jnp.float32
    ) + jnp.where(eye, 1.0, 0.0)
    second = lax.broadcasted_iota(jnp.int32, (width // 2, width), 1) >= width // 2
    gram_ref[pair] = jnp.where(second, gram[width // 2 :], gram[: width // 2])
    high = white.astype(jnp.bfloat16)
    rest = white - high.astype(jnp.float32)
    middle = rest.astype(jnp.bfloat16)
    low = (rest - middle.astype(jnp.float32)).astype(jnp.bfloat16)
    across_ref[pair] = sum(
        lax.dot_general(part, whitener, ROWS_ACROSS, preferred_element_type=jnp.float32)
        for part in (low, middle, high)
    )
    square_ref[pair] = lax.dot_general(
        whitener, whitener, ROWS_ACROSS, preferred_element_type=jnp.float32
    )
    return obs


def sweep(held):
    pairs, half, size = held.shape
    lane = lax.broadcasted_iota(jnp.int32, (half, size), 1)
    in_half = jnp.bitwise_and(lane, half - 1)
    base = lane - in_half
    at = lax.broadcasted_iota(jnp.int32, (half, size), 0)
    every = range(pairs)

    @pl.loop(0, half)
    def _(k):
        pick = base + k
        here = in_half == k
        rows = [jnp.broadcast_to(held[b, pl.ds(k, 1), :], (8, size)) for b in every]
        wholes = [held[b] for b in every]
        pivots = [jnp.take_along_axis(rows[b], pick[:8], axis=1)[:1] for b in every]
        columns = [jnp.take_along_axis(wholes[b], pick, axis=1) for b in every]
        inverses = [1.0 / pivots[b] for b in every]
        scaled = [rows[b][:1] * inverses[b] for b in every]
        swept = [
            jnp.where(here, columns[b] * inverses[b], wholes[b] - columns[b] * scaled[b]) for b in every
        ]
        for b in every:
            held[b] = jnp.where(at == k, jnp.where(here, -inverses[b], scaled[b]), swept[b])


def finish(across, minus, square, obs, tile_count):
    size = square.shape[0]
    half, width = minus.shape
    second = lax.broadcasted_iota(jnp.int32, (half, width), 1) >= half
    minus = jnp.concatenate([jnp.where(second, 0.0, minus), jnp.where(second, minus, 0.0)], axis=0)
    reduced = jnp.dot(minus, across, precision=HIGHEST, preferred_element_type=jnp.float32)
    whole = square + lax.dot_general(
        across, reduced, ROWS_ACROSS, precision=HIGHEST, preferred_element_type=jnp.float32
    )
    high = whole.astype(jnp.bfloat16)
    rest = whole - high.astype(jnp.float32)
    middle = rest.astype(jnp.bfloat16)
    low = (rest - middle.astype(jnp.float32)).astype(jnp.bfloat16)
    value = sum(
        jnp.dot(part, obs, preferred_element_type=jnp.float32) for part in (low, middle, high)
    )
    value = jnp.broadcast_to(value[:, width // 2 : width // 2 + 1], (size, EXTRA))
    value_high = value.astype(jnp.bfloat16).astype(jnp.float32)
    rest = value - value_high
    value_middle = rest.astype(jnp.bfloat16).astype(jnp.float32)
    value_low = rest - value_middle
    row = lax.broadcasted_iota(jnp.int32, (size, EXTRA), 0)
    lane = lax.broadcasted_iota(jnp.int32, (size, EXTRA), 1)
    shard = jnp.right_shift(row, (size // tile_count).bit_length() - 1)
    parts = jnp.where(lane == shard, value_high, 0.0)
    parts = jnp.where(lane == shard + tile_count, value_middle, parts)
    parts = jnp.where(lane == shard + 2 * tile_count, value_low, parts)
    return high, middle, parts.astype(jnp.bfloat16)


def pair_kernel(meta_ref, length_ref, gain_ref, log_ref, *refs):
    *slots, out_ref, held, gram, across, square, obs, turn = refs
    size = square.shape[1]
    tile_count = sum(ref.shape[0] for ref in slots)
    pair_rows = size // tile_count

    @pl.loop(0, square.shape[0])
    def _(pair):
        obs[pair] = whiten(
            meta_ref, length_ref, gain_ref, log_ref, slots, pair, held, gram, across, square
        )

    sweep(gram)

    @pl.loop(0, square.shape[0])
    def _(pair):
        high, middle, parts = finish(across[pair], gram[pair], square[pair], obs[pair], tile_count)
        turn[:, :size] = high
        turn[:, size : 2 * size] = middle
        turn[:, 2 * size :] = parts
        for n in range(tile_count):
            place = pl.ds(pl.multiple_of(meta_ref[n] * pair_rows, pair_rows), pair_rows)
            out_ref[pair, n * pair_rows : (n + 1) * pair_rows] = turn[place, :]


def pair_matrices(slots, shard, first_pair, arc_of_row, autoreg, movavg, pair_rows):
    tile_count = sum(slot.shape[0] for slot in slots)
    rows, width = slots[0].shape[1:]
    param_count = width // 2
    pair_count = rows // pair_rows
    size = tile_count * pair_rows
    meta = jnp.concatenate([shard, jnp.reshape(first_pair, (1,)).astype(jnp.int32)])
    first = 2 * jnp.arange(autoreg.shape[0] // 2, dtype=jnp.int32)
    lengths = jnp.sum((arc_of_row == first[None, :]).astype(jnp.int32), axis=0)
    return pl.pallas_call(
        pair_kernel,
        in_specs=[SMEM] * 4 + [pl.BlockSpec(memory_space=pltpu.VMEM)] * len(slots),
        out_specs=pl.BlockSpec(memory_space=pltpu.VMEM),
        out_shape=jax.ShapeDtypeStruct((pair_count, size, 2 * size + EXTRA), jnp.bfloat16),
        scratch_shapes=[
            pltpu.VMEM((size, width), jnp.float32),
            pltpu.VMEM((pair_count, param_count, width), jnp.float32),
            pltpu.VMEM((pair_count, width, size), jnp.float32),
            pltpu.VMEM((pair_count, size, size), jnp.float32),
            pltpu.VMEM((pair_count, size, width), jnp.bfloat16),
            pltpu.VMEM((size, 2 * size + EXTRA), jnp.bfloat16),
        ],
        compiler_params=params(58),
        cost_estimate=cost(SMALL * 2),
        name="pair_matrices",
    )(meta, lengths, autoreg + movavg, jnp.log(movavg), *slots)


def pack_kernel(count, width, meta_ref, *refs):
    slots, out, held, sems = refs[:count], refs[count], refs[count + 1], refs[count + 2]
    start = pl.multiple_of(meta_ref[1], 128)

    @pl.when(meta_ref[0] == 1)
    def _():
        into, back, at = [], [], 0
        for n, slot in enumerate(slots):
            here = pl.ds(at, slot.shape[0])
            columns = slot.at[:, pl.ds(start, width)]
            into.append(pltpu.make_async_copy(columns, held.at[here], sems.at[0, n]))
            back.append(pltpu.make_async_copy(held.at[here], out.at[here], sems.at[1, n]))
            at += slot.shape[0]
        for copy in into:
            copy.start()
        for first, second in zip(into, back):
            first.wait()
            second.start()
        for copy in back:
            copy.wait()


def pack(meta, slots, width):
    rows = sum(slot.shape[0] for slot in slots)
    return pl.pallas_call(
        functools.partial(pack_kernel, len(slots), width),
        in_specs=[SMEM] + [HBM] * len(slots),
        out_specs=HBM,
        out_shape=jax.ShapeDtypeStruct((rows, width), slots[0].dtype),
        scratch_shapes=[
            pltpu.VMEM((rows, width), slots[0].dtype),
            pltpu.SemaphoreType.DMA((2, len(slots))),
        ],
        cost_estimate=cost(SMALL * 2),
        name="pack",
    )(meta, *slots)


def middle_rows_kernel(count, scale, meta_ref, *refs):
    mids, slots, (out, rhs, panel, held, sems, middle, extra) = refs[:2], refs[2 : 2 + count], refs[2 + count :]
    pair_rows = slots[0].shape[0]
    size = count * pair_rows
    pair, pairs = pl.program_id(0), held.shape[0]
    core = meta_ref[count]

    def fetch(which, kind):
        source = mids[kind].at[which % (pairs // 2)]
        return pltpu.make_async_copy(source, held.at[which], sems.at[which])

    @pl.when(pair == 0)
    def _():
        for mine in range(2):

            @pl.when(core == mine)
            def _(mine=mine):
                for which in range(pairs):
                    fetch(which, int(which // (pairs // 2) != mine)).start()

    for n, slot in enumerate(slots):
        panel[n * pair_rows : (n + 1) * pair_rows, :] = slot[...]
    fetch(pair, 0).wait()
    product = lax.dot_general(
        held[pair], panel[...], ROWS_ACROSS, preferred_element_type=jnp.float32
    )
    middle[...] = (product[:size] + product[size : 2 * size]).astype(jnp.bfloat16)
    for n in range(count):
        place = pl.ds(pl.multiple_of(meta_ref[n] * pair_rows, pair_rows), pair_rows)
        out[n] = middle[place, :]

    @pl.when(pair == 0)
    def _():
        extra[...] = product[2 * size :]

    @pl.when(pair > 0)
    def _():
        extra[...] += product[2 * size :]

    @pl.when(pair == pairs - 1)
    def _():
        rhs[...] = jnp.sum(extra[...], axis=0, keepdims=True) * scale


def middle_rows(meta, mids, slots, pair_rows, scale):
    rows, width = slots[0].shape
    pair_count, size, columns = rows // pair_rows, mids[0].shape[1], mids[0].shape[2]
    count = len(slots)
    return pl.pallas_call(
        functools.partial(middle_rows_kernel, count, scale),
        grid=(pair_count,),
        in_specs=[SMEM] + [HBM] * 2 + [pl.BlockSpec((pair_rows, width), lambda b: (b, 0))] * count,
        out_specs=[
            pl.BlockSpec((count, pair_rows, width), lambda b: (0, b, 0)),
            pl.BlockSpec((1, width), lambda b: (0, 0)),
        ],
        out_shape=[
            jax.ShapeDtypeStruct((count, rows, width), jnp.bfloat16),
            jax.ShapeDtypeStruct((1, width), jnp.float32),
        ],
        scratch_shapes=[
            pltpu.VMEM((size, width), jnp.bfloat16),
            pltpu.VMEM((pair_count, size, columns), jnp.bfloat16),
            pltpu.SemaphoreType.DMA((pair_count,)),
            pltpu.VMEM((size, width), jnp.bfloat16),
            pltpu.VMEM((EXTRA, width), jnp.float32),
        ],
        compiler_params=params(56),
        cost_estimate=cost(ROWS),
        name="middle_rows",
    )(meta, *mids, *slots)


def collect_kernel(slot_places, over_places, slot_count, meta_ref, *refs):
    slots, overs, (out, held, sems) = refs[:slot_count], refs[slot_count:-3], refs[-3:]
    width = held.shape[1]
    rows = held.shape[0] // len(slot_places)
    start = pl.multiple_of(meta_ref[2], 128)

    def copies(near):
        found = []
        for n in range(len(slot_places)):
            which, at = slot_places[n] if near else over_places[n]
            ref = slots[which].at[pl.ds(at, rows), pl.ds(start, width)] if near else overs[which].at[pl.ds(at, rows)]
            found.append(pltpu.make_async_copy(ref, held.at[pl.ds(n * rows, rows)], sems.at[n]))
        return found

    for near in (True, False):

        @pl.when((meta_ref[0] == 1) & (meta_ref[1] == int(near)))
        def _(near=near):
            for copy in copies(near):
                copy.start()
            for n, copy in enumerate(copies(near)):
                copy.wait()
                out[:, n * rows : (n + 1) * rows] = held[n * rows : (n + 1) * rows, :].T


def collect(meta, slots, slot_places, overs, over_places, rows, width):
    total = rows * len(slot_places)
    return pl.pallas_call(
        functools.partial(collect_kernel, tuple(slot_places), tuple(over_places), len(slots)),
        in_specs=[SMEM] + [HBM] * (len(slots) + len(overs)),
        out_specs=pl.BlockSpec(memory_space=pltpu.VMEM),
        out_shape=jax.ShapeDtypeStruct((width, total), jnp.bfloat16),
        scratch_shapes=[
            pltpu.VMEM((total, width), jnp.bfloat16),
            pltpu.SemaphoreType.DMA((len(slot_places),)),
        ],
        compiler_params=params(24),
        cost_estimate=cost(SMALL * 2),
        name="collect",
    )(meta, *slots, *overs)


def tile_kernel(block_columns, scale, meta_ref, *refs):
    blocks, (*middles, out, block, sems) = refs[:4], refs[4:]
    step = middles[0].shape[2]

    def copies(kind):
        found, at = [], 0
        for n, ref in enumerate(blocks[2 * kind : 2 * kind + 2]):
            count = ref.shape[1]
            found.append(pltpu.make_async_copy(ref, block.at[:, pl.ds(at, count)], sems.at[n]))
            at += count
        return found

    @pl.when(pl.program_id(0) == 0)
    def _():
        for kind in range(2):

            @pl.when(meta_ref[0] != kind)
            def _(kind=kind):
                for copy in copies(kind):
                    copy.start()

        for copy in copies(0):
            copy.wait()

    middle = jnp.concatenate([one[...].reshape(-1, step) for one in middles], axis=0)
    offset = pl.multiple_of(meta_ref[3], 64)
    out[...] = (
        jnp.dot(block[pl.ds(offset, block_columns), :], middle, preferred_element_type=jnp.float32)
        * scale
    )


def tile(meta, middles, blocks, block_columns, scale, step):
    count, rows, width = middles[0].shape
    payload = blocks[0].shape[0]
    total = count * rows * len(middles)
    return pl.pallas_call(
        functools.partial(tile_kernel, block_columns, scale),
        grid=(pl.cdiv(width, step),),
        in_specs=[SMEM]
        + [HBM] * 4
        + [pl.BlockSpec((count, rows, step), lambda j: (0, 0, j))] * len(middles),
        out_specs=pl.BlockSpec((block_columns, step), lambda j: (0, j)),
        out_shape=jax.ShapeDtypeStruct((block_columns, width), jnp.float32),
        scratch_shapes=[pltpu.VMEM((payload, total), jnp.bfloat16), pltpu.SemaphoreType.DMA((2,))],
        compiler_params=params(48),
        cost_estimate=cost(12),
        name="tile",
    )(meta, *blocks, *middles)


def tie(value, *others):
    return lax.optimization_barrier((value, *others))[0]


def block_body(design, partials, observed, arc_of_row, autoreg, movavg):
    tile_count, panel_count = lax.axis_size("tm"), lax.axis_size("panel")
    rows_dev, width = design.shape
    block_columns = width * panel_count // tile_count
    payload = pl.cdiv(block_columns, 128) * 128
    pair_rows = 2 * rows_dev // tile_count
    scale = 1.0 / (rows_dev * tile_count)
    t, p = lax.axis_index("tm"), lax.axis_index("panel")
    z, x, y, core = t // 2, t % 2, p // 2, p % 2
    near, same_core = y == z // 2, core == z % 2

    def along_z(value, turn):
        pairs = [(2 * s + i, 2 * d + i) for s, d in SEND_Z[turn] for i in range(2)]
        return lax.ppermute(value, "tm", pairs)

    def across_x(value):
        return lax.ppermute(value, "tm", [(s, s ^ 1) for s in range(tile_count)])

    def hop(value, go):
        pairs = []
        for s in range(tile_count * panel_count):
            sz, sy, sc = s // 8, s // 2 % 2, s % 2
            to = go(sy == sz // 2, sc == sz % 2)
            if to is not None:
                pairs.append((s, s - s % 4 + (sy ^ to[0]) * 2 + (sc ^ to[1])))
        return lax.ppermute(value, AXES, pairs)

    line = [z] + [lax.rem((turn + 2) * z + turn + 1, 5) for turn in range(3)]
    shard = jnp.stack([2 * s + i for s in line for i in (x, 1 - x)]).astype(jnp.int32)

    half = rows_dev // 2
    pairs = half // pair_rows
    sent = jnp.concatenate([partials, jnp.broadcast_to(observed[:, None], partials.shape)], axis=1)
    sent = jnp.where(core == 0, sent[:half], sent[half:])
    both = jnp.stack([sent, across_x(sent)])
    sent_z = [both] + [along_z(both, turn) for turn in (0, 1, 3)]
    z1 = along_z(design, 0)
    x0 = across_x(tie(design, both))
    sent_z[0] = tie(sent_z[0], z1, x0)
    mid = pair_matrices(sent_z, shard, core * pairs, arc_of_row, autoreg, movavg, pair_rows)

    start = x * (width - payload)
    sends = (near & same_core).astype(jnp.int32)

    def picked(start, *slots):
        return pack(jnp.stack([sends, start]), slots, payload)

    def over(value):
        return hop(value, lambda near, same: (1, 0) if near and same else None)

    def beside(value):
        return hop(value, lambda near, same: (0, 1) if same else None)

    z2 = along_z(tie(design, z1, x0, *sent_z), 1)
    x1 = across_x(tie(z1, x0))
    z3 = along_z(tie(z1, z2, x1, mid), 2)
    x2 = across_x(tie(z2, x1))
    picked_1 = picked(start, design, x0, z1, x1, tie(z2, mid))
    mids = (mid, hop(tie(mid, z2), lambda near, same: (0, 1)))
    slots_meta = jnp.concatenate([shard, core[None]])
    x3 = across_x(tie(z3, x2, picked_1, mids[1]))
    picked_2 = picked(start, x2, z3)
    picked_3 = picked((1 - x) * (width - payload), z3)
    over_1, over_2 = over(picked_1), over(picked_2)
    over_3 = across_x(tie(over(picked_3), x3))

    block_meta = jnp.stack(
        [same_core.astype(jnp.int32), near.astype(jnp.int32), start, x * (payload - block_columns)]
    )
    early = collect(
        block_meta,
        (design, x0, z1, x1, z2),
        [(n, 0) for n in range(5)],
        (over_1,),
        [(0, n * rows_dev) for n in range(5)],
        rows_dev,
        payload,
    )
    slots = (design, x0, z1, x1, z2, x2, z3, tie(x3, early))
    middle, rhs = middle_rows(slots_meta, mids, slots, pair_rows, scale)
    late = collect(
        block_meta, (x2, z3, tie(x3, rhs)), [(0, 0), (1, 0), (2, 0)],
        (over_2, over_3), [(0, 0), (0, rows_dev), (1, 0)], rows_dev, payload,
    )
    blocks = (early, late, beside(early), beside(late))
    normal = tile(block_meta, (middle,), blocks, block_columns, scale, 512)
    return normal, rhs[0]


def line_body(design, partials, observed, arc_of_row, autoreg, movavg):
    tile_count = lax.axis_size("tm")
    rows_dev, width = design.shape
    pair_rows = 2 * rows_dev // tile_count
    pair_count = rows_dev // pair_rows
    size = tile_count * pair_rows
    scale = 1.0 / (rows_dev * tile_count)
    sent = jnp.concatenate([partials, jnp.broadcast_to(observed[:, None], partials.shape)], axis=1)
    sent = lax.all_gather(sent, "tm", axis=0, tiled=False)
    shard = jnp.arange(tile_count, dtype=jnp.int32)
    mids = pair_matrices([sent], shard, 0, arc_of_row, autoreg, movavg, pair_rows)
    panel = lax.all_gather(design, "tm", axis=0, tiled=False)
    whole_rows = lax.all_gather(design, "panel", axis=1, tiled=True)
    block = lax.all_to_all(whole_rows, "tm", split_axis=1, concat_axis=0, tiled=True)
    block = block.reshape(tile_count, rows_dev, -1)

    def one_pair(sums, pair):
        def rows_of(values):
            here = lax.dynamic_slice_in_dim(values, pair * pair_rows, pair_rows, 1)
            return here.reshape(size, values.shape[2])

        product = lax.dot_general(
            mids[pair], rows_of(panel), ROWS_ACROSS, preferred_element_type=jnp.float32
        )
        middle = (product[:size] + product[size : 2 * size]).astype(jnp.bfloat16)
        here = lax.dot_general(
            rows_of(block), middle, ROWS_ACROSS, preferred_element_type=jnp.float32
        )
        return (sums[0] + here, sums[1] + jnp.sum(product[2 * size :], axis=0)), None

    start = (jnp.zeros((block.shape[2], width), jnp.float32), jnp.zeros((width,), jnp.float32))
    (normal, right_hand), _ = lax.scan(one_pair, start, jnp.arange(pair_count))
    return normal * scale, right_hand * scale


def solution(mesh):
    in_specs = (P("tm", "panel"), P("tm", None), P("tm"), P(), P(), P())
    out_specs = (P("tm", "panel"), P("panel"))
    body = block_body if (mesh.shape["tm"], mesh.shape["panel"]) == (8, 4) else line_body
    return jax.shard_map(body, mesh=mesh, in_specs=in_specs, out_specs=out_specs, check_vma=False)
```

time: 209 us -> 150 us (0.72)
  Pallas kernels: 91.3 us -> 61.4 us
  starting transfers between devices: 50 us -> 26.7 us
  local copies, waits for them, and re-layouts: 14.8 us -> 4.43 us
  waiting for transfers between devices: 44.9 us -> 51.2 us
  between operations: 3.46 us -> 0.91 us
    pallas_call x9 -> x5, Pallas kernels: 80.6 us -> 52.8 us  [the longest x1 17.2 us: pair_matrices(): pl.pallas_call(pair_kernel, in_specs=[SMEM] * 4 + [pl.BlockSpec(memory_sp...]
    ppermute x9 -> x6, waiting for transfers between devices: 24.6 us -> 44 us  [along_z(): return lax.ppermute(value, 'tm', pairs)]
    ppermute x12 -> x6, starting transfers between devices: 27.1 us -> 10.2 us  [hop(): return lax.ppermute(value, AXES, pairs)]
    ppermute x9 -> x6, waiting for transfers between devices: 20.3 us -> 4.93 us  [across_x(): return lax.ppermute(value, 'tm', [(s, s ^ 1) for s in range(tile_count)])]
    unnamed x88 -> x29, local copies, waits for them, and re-layouts: 9.29 us -> 2.35 us
    ppermute x9 -> x6, starting transfers between devices: 11.7 us -> 6.49 us  [across_x(): return lax.ppermute(value, 'tm', [(s, s ^ 1) for s in range(tile_count)])]
    slice x2 -> x0, local copies, waits for them, and re-layouts: 2.52 us -> none  [the longest x1 1.26 us: block_body(): own_a, own_b = (design[:half], design[half:])]
    ppermute x12 -> x6, waiting for transfers between devices: 0.03 us -> 2.3 us  [hop(): return lax.ppermute(value, AXES, pairs)]
  transfers between devices with their start and end apart: 30 -> 18, of which waited for: 11 -> 9; matrix products, arithmetic and copies ran while one was open for 4% -> 4% of each run, Pallas kernels for 37% -> 32%
where the time goes in v2:
time: 150 us; the launch traced here: 149 us
  Pallas kernels  61.4 us (41%)
  waiting for transfers between devices  51.2 us (34%)
  starting transfers between devices  26.7 us (18%)
  other arithmetic  4.87 us (3%)
  local copies, waits for them, and re-layouts  4.43 us (3%)
    ppermute x6, waiting for transfers between devices, along_z(): return lax.ppermute(value, 'tm', pairs)  44 us
    pallas_call x1, Pallas kernels, pair_matrices(): pl.pallas_call(pair_kernel, in_specs=[SMEM] * 4 + [pl.BlockSpec(memory_sp...  17.2 us
    pallas_call x1, Pallas kernels, middle_rows(): pl.pallas_call(functools.partial(middle_rows_kernel, count, scale), grid=...  16.3 us
    pallas_call x1, Pallas kernels, tile(): pl.pallas_call(functools.partial(tile_kernel, block_columns, scale), grid...  13.6 us
    ppermute x6, starting transfers between devices, hop(): return lax.ppermute(value, AXES, pairs)  10.2 us
    ppermute x6, starting transfers between devices, along_z(): return lax.ppermute(value, 'tm', pairs)  10 us
    pallas_call x3, Pallas kernels, pack(): pl.pallas_call(functools.partial(pack_kernel, len(slots), width), in_spec...  8.51 us
    ppermute x6, starting transfers between devices, across_x(): return lax.ppermute(value, 'tm', [(s, s ^ 1) for s in range(tile_count)])  6.49 us
  transfers between devices with their start and end apart: 18, of which 9 were waited for; matrix products, arithmetic and copies ran while one was open for 4% of the time, Pallas kernels for 32%

profile of v2, /device:TPU:0, one launch (start us, length us, event | category | flops | bytes accessed | tf_op | source)
XLA Modules:
  0.0 149.5 jit_solution(5325660405709867688)
XLA Ops:
  0.6 0.9 copy.9
  1.5 0.8 broadcast_in_dim.4
  2.4 3.0 %collective-permute-start = (bf16[128,128]{1,0:T(8,128)(2,1)S(1)}, bf16[128,128]{1,0:T(8,128)(2,1)S(1)}, u32[]{:S(2)}, u32[]{:S(2)}) collective-permute-start(bf16[128,128]{1,0:T(8,128)(2,1)S(1)} %fusion.1), channel_id=1, source_target_pairs={{0,4},{4,0},{8,12},{12,8},{16,20},{20,16},{24,28},{28,24},{1,5},{5... | collective-permute-start | bytes 98312 | tf_op jit(solution)/shard_map/ppermute | solution.py:423
  5.4 2.6 %collective-permute-start.2 = (bf16[256,1920]{1,0:T(8,128)(2,1)}, bf16[256,1920]{1,0:T(8,128)(2,1)S(1)}, u32[]{:S(2)}, u32[]{:S(2)}) collective-permute-start(bf16[256,1920]{1,0:T(8,128)(2,1)} %refs_2_.1), channel_id=1, source_target_pairs={{8,0},{12,4},{24,8},{28,12},{0,16},{4,20},{16,24},{20,28},{9,1},{1... | collective-permute-start | bytes 2949128 | tf_op jit(solution)/shard_map/ppermute | solution.py:420
  8.1 1.3 collective-permute-start.1
  9.4 2.6 %collective-permute-start.4 = (bf16[2,128,128]{2,1,0:T(8,128)(2,1)S(1)}, bf16[2,128,128]{2,1,0:T(8,128)(2,1)S(1)}, u32[]{:S(2)}, u32[]{:S(2)}) collective-permute-start(bf16[2,128,128]{2,1,0:T(8,128)(2,1)S(1)} %pad_maximum_fusion.refs_0_), channel_id=1, source_target_pairs={{8,0},{12,4},{24,8},{28,12},{0,16},{4,20},{16,24},{20,28},{9,1},{1... | collective-permute-start | bytes 196616 | tf_op jit(solution)/shard_map/ppermute | solution.py:420
  12.0 3.0 %collective-permute-start.6 = (bf16[2,128,128]{2,1,0:T(8,128)(2,1)S(1)}, bf16[2,128,128]{2,1,0:T(8,128)(2,1)S(1)}, u32[]{:S(2)}, u32[]{:S(2)}) collective-permute-start(bf16[2,128,128]{2,1,0:T(8,128)(2,1)S(1)} %pad_maximum_fusion.refs_0_), channel_id=1, source_target_pairs={{24,0},{28,4},{16,8},{20,12},{8,16},{12,20},{0,24},{4,28},{25,1},{... | collective-permute-start | bytes 196616 | tf_op jit(solution)/shard_map/ppermute | solution.py:420
  15.0 15.5 %collective-permute-done.2.refs_2_.refs_4_ = bf16[256,1920]{1,0:T(8,128)(2,1)S(1)} collective-permute-done((bf16[256,1920]{1,0:T(8,128)(2,1)}, bf16[256,1920]{1,0:T(8,128)(2,1)S(1)}, u32[]{:S(2)}, u32[]{:S(2)}) %collective-permute-start.2) | collective-permute-done | bytes 983072 | tf_op jit(solution)/shard_map/ppermute | solution.py:420
  30.5 0.8 collective-permute-done.1.refs_1_.refs_3_
  31.8 2.6 %collective-permute-done.5.refs_2_ = bf16[2,128,128]{2,1,0:T(8,128)(2,1)S(1)} collective-permute-done((bf16[2,128,128]{2,1,0:T(8,128)(2,1)S(1)}, bf16[2,128,128]{2,1,0:T(8,128)(2,1)S(1)}, u32[]{:S(2)}, u32[]{:S(2)}) %collective-permute-start.5) | collective-permute-done | bytes 65568 | tf_op jit(solution)/shard_map/ppermute | solution.py:420
  34.3 0.7 collective-permute-done.6.refs_3_
  35.1 1.8 %collective-permute-start.7 = (bf16[256,1920]{1,0:T(8,128)(2,1)}, bf16[256,1920]{1,0:T(8,128)(2,1)S(1)}, u32[]{:S(2)}, u32[]{:S(2)}) collective-permute-start(bf16[256,1920]{1,0:T(8,128)(2,1)} %refs_2_.1), channel_id=1, source_target_pairs={{16,0},{20,4},{0,8},{4,12},{24,16},{28,20},{8,24},{12,28},{17,1},{... | collective-permute-start | bytes 2949128 | tf_op jit(solution)/shard_map/ppermute | solution.py:420
  38.1 1.4 convert_reduce_fusion.length_ref
  39.5 1.2 fusion.2
  40.8 17.2 %pair_matrices.1.refs_0_ = bf16[2,512,1152]{2,1,0:T(8,128)(2,1)} custom-call(s32[9]{0:T(128)} %concatenate.12.meta_ref, s32[4]{0:T(128)} %convert_reduce_fusion.length_ref, f32[8]{0:T(128)} %get-tuple-element.31.gain_ref, f32[8]{0:T(128)} %get-tuple-element.30.log_ref, bf16[2,128,128]{2,1,0:T(8,128)(2,1)} %copy-done.9, bf16[2,128,128]{2,1,0:T(8,128)(2,1)} %copy-done.11, ...), custom_call_target="tpu_custom_call" | custom-call | flops 1000000000 | tf_op jit(solution)/shard_map/pair_matrices/pallas_call | solution.py:180
  58.0 2.1 %collective-permute-done.7.refs_4_.refs_6_ = bf16[256,1920]{1,0:T(8,128)(2,1)S(1)} collective-permute-done((bf16[256,1920]{1,0:T(8,128)(2,1)}, bf16[256,1920]{1,0:T(8,128)(2,1)S(1)}, u32[]{:S(2)}, u32[]{:S(2)}) %collective-permute-start.7) | collective-permute-done | bytes 983072 | tf_op jit(solution)/shard_map/ppermute | solution.py:420
  61.0 3.3 %pack.3 = bf16[1280,1024]{1,0:T(8,128)(2,1)} custom-call(s32[2]{0:T(128)} %pad_add_fusion.1.meta_ref, bf16[256,1920]{1,0:T(8,128)(2,1)} %refs_2_.1, bf16[256,1920]{1,0:T(8,128)(2,1)} %copy-done.3, bf16[256,1920]{1,0:T(8,128)(2,1)} %copy-done.1, bf16[256,1920]{1,0:T(8,128)(2,1)} %collective-permute-done.3.refs_3_.refs_5_, bf16[256,1920]{1,0:T(8,128)(2,1)} %copy-done.5), custom_call_target="tpu_custom_call" | custom-call | flops 1000000000 | tf_op jit(solution)/shard_map/pack/pallas_call | solution.py:223
  64.3 2.8 %collective-permute-start.8 = (bf16[1280,1024]{1,0:T(8,128)(2,1)}, bf16[1280,1024]{1,0:T(8,128)(2,1)}, u32[]{:S(2)}, u32[]{:S(2)}) collective-permute-start(bf16[1280,1024]{1,0:T(8,128)(2,1)} %pack.3), channel_id=1, source_target_pairs={{0,2},{4,6},{9,11},{13,15},{18,16},{22,20},{27,25},{31,29}} | collective-permute-start | bytes 7864328 | tf_op jit(solution)/shard_map/ppermute | solution.py:432
  67.7 22.6 %collective-permute-done.10.refs_8_.refs_1_.refs_0_ = bf16[256,1920]{1,0:T(8,128)(2,1)} collective-permute-done((bf16[256,1920]{1,0:T(8,128)(2,1)}, bf16[256,1920]{1,0:T(8,128)(2,1)}, u32[]{:S(2)}, u32[]{:S(2)}) %collective-permute-start.10) | collective-permute-done | bytes 983072 | tf_op jit(solution)/shard_map/ppermute | solution.py:420
  91.5 2.5 %pack.5 = bf16[256,1024]{1,0:T(8,128)(2,1)} custom-call(s32[2]{0:T(128)} %pad_add_fusion.2.meta_ref, bf16[256,1920]{1,0:T(8,128)(2,1)} %collective-permute-done.10.refs_8_.refs_1_.refs_0_), custom_call_target="tpu_custom_call" | custom-call | flops 1000000000 | tf_op jit(solution)/shard_map/pack/pallas_call | solution.py:223
  94.1 1.6 %collective-permute-start.14 = (bf16[256,1024]{1,0:T(8,128)(2,1)}, bf16[256,1024]{1,0:T(8,128)(2,1)S(1)}, u32[]{:S(2)}, u32[]{:S(2)}) collective-permute-start(bf16[256,1024]{1,0:T(8,128)(2,1)} %pack.5), channel_id=1, source_target_pairs={{0,2},{4,6},{9,11},{13,15},{18,16},{22,20},{27,25},{31,29}} | collective-permute-start | bytes 1572872 | tf_op jit(solution)/shard_map/ppermute | solution.py:432
  96.4 2.7 %pack.4 = bf16[512,1024]{1,0:T(8,128)(2,1)} custom-call(s32[2]{0:T(128)} %pad_add_fusion.1.meta_ref, bf16[256,1920]{1,0:T(8,128)(2,1)} %copy-done.7, bf16[256,1920]{1,0:T(8,128)(2,1)} %collective-permute-done.10.refs_8_.refs_1_.refs_0_), custom_call_target="tpu_custom_call" | custom-call | flops 1000000000 | tf_op jit(solution)/shard_map/pack/pallas_call | solution.py:223
  99.1 1.4 collective-permute-start.13
  100.5 1.2 copy-done.6
  101.7 3.7 %collect.2.refs_0_ = bf16[1024,1280]{1,0:T(8,128)(2,1)} custom-call(s32[4]{0:T(128)S(1)} %pad_add_fusion.meta_ref, bf16[256,1920]{1,0:T(8,128)(2,1)S(1)} %copy-done, bf16[256,1920]{1,0:T(8,128)(2,1)S(1)} %copy-done.4, bf16[256,1920]{1,0:T(8,128)(2,1)S(1)} %copy-done.2, bf16[256,1920]{1,0:T(8,128)(2,1)} %collective-permute-done.3.refs_3_.refs_5_, ...), custom_call_target="tpu_custom_call" | custom-call | flops 1000000000 | tf_op jit(solution)/shard_map/collect/pallas_call | solution.py:337
  105.5 3.0 %collective-permute-start.16 = (bf16[1024,1280]{1,0:T(8,128)(2,1)}, bf16[1024,1280]{1,0:T(8,128)(2,1)}, u32[]{:S(2)}, u32[]{:S(2)}) collective-permute-start(bf16[1024,1280]{1,0:T(8,128)(2,1)} %collect.2.refs_0_), channel_id=1, source_target_pairs={{0,1},{2,3},{4,5},{6,7},{9,8},{11,10},{13,12},{15,14},{16,17},{18,... | collective-permute-start | bytes 7864328 | tf_op jit(solution)/shard_map/ppermute | solution.py:432
  108.5 4.1 %collective-permute-done.12.refs_9_.refs_2_ = bf16[256,1920]{1,0:T(8,128)(2,1)} collective-permute-done((bf16[256,1920]{1,0:T(8,128)(2,1)}, bf16[256,1920]{1,0:T(8,128)(2,1)}, u32[]{:S(2)}, u32[]{:S(2)}) %collective-permute-start.12) | collective-permute-done | bytes 983072 | tf_op jit(solution)/shard_map/ppermute | solution.py:423
  113.2 16.3 %middle_rows.1 = (bf16[8,256,1920]{2,1,0:T(8,128)(2,1)}, f32[1,1920]{1,0:T(1,128)}) custom-call(s32[9]{0:T(128)} %concatenate.13.meta_ref, bf16[2,512,1152]{2,1,0:T(8,128)(2,1)} %pair_matrices.1.refs_0_, bf16[2,512,1152]{2,1,0:T(8,128)(2,1)} %collective-permute-done.11.refs_1_, bf16[256,1920]{1,0:T(8,128)(2,1)} %refs_2_.1, bf16[256,1920]{1,0:T(8,128)(2,1)} %copy-done.3, ...), custom_call_target="tpu_custom_call" | custom-call | flops 12000000000 | tf_op jit(solution)/shard_map/middle_rows/pallas_call | solution.py:285
  129.5 2.0 %collect.3.refs_1_ = bf16[1024,768]{1,0:T(8,128)(2,1)S(1)} custom-call(s32[4]{0:T(128)S(1)} %pad_add_fusion.meta_ref, bf16[256,1920]{1,0:T(8,128)(2,1)S(1)} %copy-done.8, bf16[256,1920]{1,0:T(8,128)(2,1)} %collective-permute-done.10.refs_8_.refs_1_.refs_0_, bf16[256,1920]{1,0:T(8,128)(2,1)} %collective-permute-done.12.refs_9_.refs_2_, ...), custom_call_target="tpu_custom_call" | custom-call | flops 1000000000 | tf_op jit(solution)/shard_map/collect/pallas_call | solution.py:337
  131.6 1.4 collective-permute-start.17
  133.6 2.3 %collective-permute-done.17.refs_3_ = bf16[1024,768]{1,0:T(8,128)(2,1)S(1)} collective-permute-done((bf16[1024,768]{1,0:T(8,128)(2,1)S(1)}, bf16[1024,768]{1,0:T(8,128)(2,1)S(1)}, u32[]{:S(2)}, u32[]{:S(2)}) %collective-permute-start.17) | collective-permute-done | bytes 1572896 | tf_op jit(solution)/shard_map/ppermute | solution.py:432
  135.9 13.6 %tile.1 = f32[960,1920]{1,0:T(8,128)} custom-call(s32[4]{0:T(128)S(1)} %pad_add_fusion.meta_ref, bf16[1024,1280]{1,0:T(8,128)(2,1)} %collect.2.refs_0_, bf16[1024,768]{1,0:T(8,128)(2,1)S(1)} %collect.3.refs_1_, bf16[1024,1280]{1,0:T(8,128)(2,1)} %collective-permute-done.16.refs_2_, bf16[1024,768]{1,0:T(8,128)(2,1)S(1)} %collective-permute-done.17.refs_3_, ...), custom_call_target="tpu_custom_call" | custom-call | flops 12000000000 | tf_op jit(solution)/shard_map/tile/pallas_call | solution.py:388
  (54 shorter events, 6.5 us)
Async XLA Ops:
  2.4 5.7 %collective-permute-start = (bf16[128,128]{1,0:T(8,128)(2,1)S(1)}, bf16[128,128]{1,0:T(8,128)(2,1)S(1)}, u32[]{:S(2)}, u32[]{:S(2)}) collective-permute-start(bf16[128,128]{1,0:T(8,128)(2,1)S(1)} %fusion.1), channel_id=1, source_target_pairs={{0,4},{4,0},{8,12},{12,8},{16,20},{20,16},{24,28},{28,24},{1,5},{5... | collective-permute-start | bytes 98312 | tf_op jit(solution)/shard_map/ppermute | solution.py:423
  5.4 25.1 %collective-permute-start.2 = (bf16[256,1920]{1,0:T(8,128)(2,1)}, bf16[256,1920]{1,0:T(8,128)(2,1)S(1)}, u32[]{:S(2)}, u32[]{:S(2)}) collective-permute-start(bf16[256,1920]{1,0:T(8,128)(2,1)} %refs_2_.1), channel_id=1, source_target_pairs={{8,0},{12,4},{24,8},{28,12},{0,16},{4,20},{16,24},{20,28},{9,1},{1... | collective-permute-start | bytes 2949128 | tf_op jit(solution)/shard_map/ppermute | solution.py:420
  8.1 32.7 %copy-start.9 = (bf16[2,128,128]{2,1,0:T(8,128)(2,1)}, bf16[2,128,128]{2,1,0:T(8,128)(2,1)S(1)}, u32[]{:S(2)}) copy-start(bf16[2,128,128]{2,1,0:T(8,128)(2,1)S(1)} %pad_maximum_fusion.refs_0_) | copy-start | bytes 196612
  8.1 23.2 %collective-permute-start.1 = (bf16[256,1920]{1,0:T(8,128)(2,1)}, bf16[256,1920]{1,0:T(8,128)(2,1)S(1)}, u32[]{:S(2)}, u32[]{:S(2)}) collective-permute-start(bf16[256,1920]{1,0:T(8,128)(2,1)} %refs_2_.1), channel_id=1, source_target_pairs={{0,4},{4,0},{8,12},{12,8},{16,20},{20,16},{24,28},{28,24},{1,5},{5... | collective-permute-start | bytes 2949128 | tf_op jit(solution)/shard_map/ppermute | solution.py:423
  9.4 22.4 %collective-permute-start.4 = (bf16[2,128,128]{2,1,0:T(8,128)(2,1)S(1)}, bf16[2,128,128]{2,1,0:T(8,128)(2,1)S(1)}, u32[]{:S(2)}, u32[]{:S(2)}) collective-permute-start(bf16[2,128,128]{2,1,0:T(8,128)(2,1)S(1)} %pad_maximum_fusion.refs_0_), channel_id=1, source_target_pairs={{8,0},{12,4},{24,8},{28,12},{0,16},{4,20},{16,24},{20,28},{9,1},{1... | collective-permute-start | bytes 196616 | tf_op jit(solution)/shard_map/ppermute | solution.py:420
  12.0 22.4 %collective-permute-start.5 = (bf16[2,128,128]{2,1,0:T(8,128)(2,1)S(1)}, bf16[2,128,128]{2,1,0:T(8,128)(2,1)S(1)}, u32[]{:S(2)}, u32[]{:S(2)}) collective-permute-start(bf16[2,128,128]{2,1,0:T(8,128)(2,1)S(1)} %pad_maximum_fusion.refs_0_), channel_id=1, source_target_pairs={{16,0},{20,4},{0,8},{4,12},{24,16},{28,20},{8,24},{12,28},{17,1},{... | collective-permute-start | bytes 196616 | tf_op jit(solution)/shard_map/ppermute | solution.py:420
  12.0 23.1 %collective-permute-start.6 = (bf16[2,128,128]{2,1,0:T(8,128)(2,1)S(1)}, bf16[2,128,128]{2,1,0:T(8,128)(2,1)S(1)}, u32[]{:S(2)}, u32[]{:S(2)}) collective-permute-start(bf16[2,128,128]{2,1,0:T(8,128)(2,1)S(1)} %pad_maximum_fusion.refs_0_), channel_id=1, source_target_pairs={{24,0},{28,4},{16,8},{20,12},{8,16},{12,20},{0,24},{4,28},{25,1},{... | collective-permute-start | bytes 196616 | tf_op jit(solution)/shard_map/ppermute | solution.py:420
  30.5 30.3 %copy-start.1 = (bf16[256,1920]{1,0:T(8,128)(2,1)}, bf16[256,1920]{1,0:T(8,128)(2,1)S(1)}, u32[]{:S(2)}) copy-start(bf16[256,1920]{1,0:T(8,128)(2,1)S(1)} %collective-permute-done.2.refs_2_.refs_4_) | copy-start | bytes 2949124
  31.3 29.5 %copy-start.3 = (bf16[256,1920]{1,0:T(8,128)(2,1)}, bf16[256,1920]{1,0:T(8,128)(2,1)S(1)}, u32[]{:S(2)}) copy-start(bf16[256,1920]{1,0:T(8,128)(2,1)S(1)} %collective-permute-done.1.refs_1_.refs_3_) | copy-start | bytes 2949124
  31.8 9.0 %copy-start.11 = (bf16[2,128,128]{2,1,0:T(8,128)(2,1)}, bf16[2,128,128]{2,1,0:T(8,128)(2,1)S(1)}, u32[]{:S(2)}) copy-start(bf16[2,128,128]{2,1,0:T(8,128)(2,1)S(1)} %collective-permute-done.4.refs_1_) | copy-start | bytes 196612
  34.3 6.4 %copy-start.12 = (bf16[2,128,128]{2,1,0:T(8,128)(2,1)}, bf16[2,128,128]{2,1,0:T(8,128)(2,1)S(1)}, u32[]{:S(2)}) copy-start(bf16[2,128,128]{2,1,0:T(8,128)(2,1)S(1)} %collective-permute-done.5.refs_2_) | copy-start | bytes 196612
  35.1 5.7 %copy-start.13 = (bf16[2,128,128]{2,1,0:T(8,128)(2,1)}, bf16[2,128,128]{2,1,0:T(8,128)(2,1)S(1)}, u32[]{:S(2)}) copy-start(bf16[2,128,128]{2,1,0:T(8,128)(2,1)S(1)} %collective-permute-done.6.refs_3_) | copy-start | bytes 196612
  35.1 25.0 %collective-permute-start.7 = (bf16[256,1920]{1,0:T(8,128)(2,1)}, bf16[256,1920]{1,0:T(8,128)(2,1)S(1)}, u32[]{:S(2)}, u32[]{:S(2)}) collective-permute-start(bf16[256,1920]{1,0:T(8,128)(2,1)} %refs_2_.1), channel_id=1, source_target_pairs={{16,0},{20,4},{0,8},{4,12},{24,16},{28,20},{8,24},{12,28},{17,1},{... | collective-permute-start | bytes 2949128 | tf_op jit(solution)/shard_map/ppermute | solution.py:420
  36.9 23.9 %collective-permute-start.3 = (bf16[256,1920]{1,0:T(8,128)(2,1)S(1)}, bf16[256,1920]{1,0:T(8,128)(2,1)}, u32[]{:S(2)}, u32[]{:S(2)}) collective-permute-start(bf16[256,1920]{1,0:T(8,128)(2,1)S(1)} %collective-permute-done.2.refs_2_.refs_4_), channel_id=1, source_target_pairs={{0,4},{4,0},{8,12},{12,8},{16,20},{20,16},{24,28},{28,24},{1,5},{5... | collective-permute-start | bytes 2949128 | tf_op jit(solution)/shard_map/ppermute | solution.py:423
  60.1 1.0 copy-start.5
  60.1 30.2 %collective-permute-start.11 = (bf16[2,512,1152]{2,1,0:T(8,128)(2,1)}, bf16[2,512,1152]{2,1,0:T(8,128)(2,1)}, u32[]{:S(2)}, u32[]{:S(2)}) collective-permute-start(bf16[2,512,1152]{2,1,0:T(8,128)(2,1)} %pair_matrices.1.refs_0_), channel_id=1, source_target_pairs={{0,1},{1,0},{2,3},{3,2},{4,5},{5,4},{6,7},{7,6},{8,9},{9,8},{10,11... | collective-permute-start | bytes 7077896 | tf_op jit(solution)/shard_map/ppermute | solution.py:432
  64.3 36.2 %collective-permute-start.8 = (bf16[1280,1024]{1,0:T(8,128)(2,1)}, bf16[1280,1024]{1,0:T(8,128)(2,1)}, u32[]{:S(2)}, u32[]{:S(2)}) collective-permute-start(bf16[1280,1024]{1,0:T(8,128)(2,1)} %pack.3), channel_id=1, source_target_pairs={{0,2},{4,6},{9,11},{13,15},{18,16},{22,20},{27,25},{31,29}} | collective-permute-start | bytes 7864328 | tf_op jit(solution)/shard_map/ppermute | solution.py:432
  67.1 23.2 %collective-permute-start.10 = (bf16[256,1920]{1,0:T(8,128)(2,1)}, bf16[256,1920]{1,0:T(8,128)(2,1)}, u32[]{:S(2)}, u32[]{:S(2)}) collective-permute-start(bf16[256,1920]{1,0:T(8,128)(2,1)} %copy-done.1), channel_id=1, source_target_pairs={{8,0},{12,4},{24,8},{28,12},{0,16},{4,20},{16,24},{20,28},{9,1},{1... | collective-permute-start | bytes 2949128 | tf_op jit(solution)/shard_map/ppermute | solution.py:420
  67.1 23.2 %collective-permute-start.9 = (bf16[256,1920]{1,0:T(8,128)(2,1)}, bf16[256,1920]{1,0:T(8,128)(2,1)S(1)}, u32[]{:S(2)}, u32[]{:S(2)}) collective-permute-start(bf16[256,1920]{1,0:T(8,128)(2,1)} %copy-done.5), channel_id=1, source_target_pairs={{0,4},{4,0},{8,12},{12,8},{16,20},{20,16},{24,28},{28,24},{1,5},{5... | collective-permute-start | bytes 2949128 | tf_op jit(solution)/shard_map/ppermute | solution.py:423
  90.3 1.2 copy-start.7
  90.3 22.3 %collective-permute-start.12 = (bf16[256,1920]{1,0:T(8,128)(2,1)}, bf16[256,1920]{1,0:T(8,128)(2,1)}, u32[]{:S(2)}, u32[]{:S(2)}) collective-permute-start(bf16[256,1920]{1,0:T(8,128)(2,1)} %collective-permute-done.10.refs_8_.refs_1_.refs_0_), channel_id=1, source_target_pairs={{0,4},{4,0},{8,12},{12,8},{16,20},{20,16},{24,28},{28,24},{1,5},{5... | collective-permute-start | bytes 2949128 | tf_op jit(solution)/shard_map/ppermute | solution.py:423
  94.1 6.5 %copy-start = (bf16[256,1920]{1,0:T(8,128)(2,1)S(1)}, bf16[256,1920]{1,0:T(8,128)(2,1)}, u32[]{:S(2)}) copy-start(bf16[256,1920]{1,0:T(8,128)(2,1)} %refs_2_.1) | copy-start | bytes 2949124
  94.1 6.5 %copy-start.2 = (bf16[256,1920]{1,0:T(8,128)(2,1)S(1)}, bf16[256,1920]{1,0:T(8,128)(2,1)}, u32[]{:S(2)}) copy-start(bf16[256,1920]{1,0:T(8,128)(2,1)} %copy-done.1) | copy-start | bytes 2949124
  94.1 6.5 %copy-start.4 = (bf16[256,1920]{1,0:T(8,128)(2,1)S(1)}, bf16[256,1920]{1,0:T(8,128)(2,1)}, u32[]{:S(2)}) copy-start(bf16[256,1920]{1,0:T(8,128)(2,1)} %copy-done.3) | copy-start | bytes 2949124
  94.1 14.4 %collective-permute-start.14 = (bf16[256,1024]{1,0:T(8,128)(2,1)}, bf16[256,1024]{1,0:T(8,128)(2,1)S(1)}, u32[]{:S(2)}, u32[]{:S(2)}) collective-permute-start(bf16[256,1024]{1,0:T(8,128)(2,1)} %pack.5), channel_id=1, source_target_pairs={{0,2},{4,6},{9,11},{13,15},{18,16},{22,20},{27,25},{31,29}} | collective-permute-start | bytes 1572872 | tf_op jit(solution)/shard_map/ppermute | solution.py:432
  99.1 30.4 %collective-permute-start.13 = (bf16[512,1024]{1,0:T(8,128)(2,1)}, bf16[512,1024]{1,0:T(8,128)(2,1)S(1)}, u32[]{:S(2)}, u32[]{:S(2)}) collective-permute-start(bf16[512,1024]{1,0:T(8,128)(2,1)} %pack.4), channel_id=1, source_target_pairs={{0,2},{4,6},{9,11},{13,15},{18,16},{22,20},{27,25},{31,29}} | collective-permute-start | bytes 3145736 | tf_op jit(solution)/shard_map/ppermute | solution.py:432
  100.5 1.2 copy-start.6
  105.5 24.0 %copy-start.8 = (bf16[256,1920]{1,0:T(8,128)(2,1)S(1)}, bf16[256,1920]{1,0:T(8,128)(2,1)}, u32[]{:S(2)}) copy-start(bf16[256,1920]{1,0:T(8,128)(2,1)} %copy-done.7) | copy-start | bytes 2949124
  105.5 28.1 %collective-permute-start.16 = (bf16[1024,1280]{1,0:T(8,128)(2,1)}, bf16[1024,1280]{1,0:T(8,128)(2,1)}, u32[]{:S(2)}, u32[]{:S(2)}) collective-permute-start(bf16[1024,1280]{1,0:T(8,128)(2,1)} %collect.2.refs_0_), channel_id=1, source_target_pairs={{0,1},{2,3},{4,5},{6,7},{9,8},{11,10},{13,12},{15,14},{16,17},{18,... | collective-permute-start | bytes 7864328 | tf_op jit(solution)/shard_map/ppermute | solution.py:432
  112.6 16.9 %collective-permute-start.15 = (bf16[256,1024]{1,0:T(8,128)(2,1)S(1)}, bf16[256,1024]{1,0:T(8,128)(2,1)S(1)}, u32[]{:S(2)}, u32[]{:S(2)}) collective-permute-start(bf16[256,1024]{1,0:T(8,128)(2,1)S(1)} %collective-permute-done.14), channel_id=1, source_target_pairs={{0,4},{4,0},{8,12},{12,8},{16,20},{20,16},{24,28},{28,24},{1,5},{5... | collective-permute-start | bytes 1572872 | tf_op jit(solution)/shard_map/ppermute | solution.py:423
  129.5 3.5 %copy-start.10 = (f32[1,1920]{1,0:T(1,128)S(1)}, f32[1,1920]{1,0:T(1,128)}, u32[]{:S(2)}) copy-start(f32[1,1920]{1,0:T(1,128)} %get-tuple-element.26) | copy-start | bytes 23044
  131.6 4.3 %collective-permute-start.17 = (bf16[1024,768]{1,0:T(8,128)(2,1)S(1)}, bf16[1024,768]{1,0:T(8,128)(2,1)S(1)}, u32[]{:S(2)}, u32[]{:S(2)}) collective-permute-start(bf16[1024,768]{1,0:T(8,128)(2,1)S(1)} %collect.3.refs_1_), channel_id=1, source_target_pairs={{0,1},{2,3},{4,5},{6,7},{9,8},{11,10},{13,12},{15,14},{16,17},{18,... | collective-permute-start | bytes 4718600 | tf_op jit(solution)/shard_map/ppermute | solution.py:432

commit v3 on v2

--- a/solution.py
+++ b/solution.py
@@ -10,7 +10,7 @@
 AXES = ("tm", "panel")
 HIGHEST = lax.Precision.HIGHEST
 ROWS_ACROSS = (((0,), (0,)), ((), ()))
-EXTRA = 128
+EXTRA = 16
 HBM = pl.BlockSpec(memory_space=pl.ANY)
 SMEM = pl.BlockSpec(memory_space=pltpu.SMEM)
 SEND_Z = (((1, 0), (3, 1), (0, 2), (2, 3)), ((2, 0), (0, 1), (3, 2), (1, 3)), ((1, 0), (3, 1), (0, 2), (2, 3)), ((3, 0), (2, 1), (1, 2), (0, 3)))
@@ -60,7 +60,7 @@
         source = pl.ds(pl.multiple_of(pair * pair_rows, pair_rows), pair_rows)
         held[place, :] = ref[shard, source].astype(jnp.float32)
     rows = held[...]
-    obs = rows.astype(jnp.bfloat16)
+    obs = rows.T[width // 2 : width // 2 + EXTRA].astype(jnp.bfloat16)
     lane = lax.broadcasted_iota(jnp.int32, (size, width), 1)
     in_first = jnp.where(lane < width // 2, 1, 0)
     rows = jnp.where(in_first == 1, rows, pltpu.roll(rows, width // 2, axis=1))
@@ -113,7 +113,7 @@
             held[b] = jnp.where(at == k, jnp.where(here, -inverses[b], scaled[b]), swept[b])
 
 
-def finish(across, minus, square, obs, tile_count):
+def finish(across, minus, square, obs):
     size = square.shape[0]
     half, width = minus.shape
     second = lax.broadcasted_iota(jnp.int32, (half, width), 1) >= half
@@ -127,19 +127,16 @@
     middle = rest.astype(jnp.bfloat16)
     low = (rest - middle.astype(jnp.float32)).astype(jnp.bfloat16)
     value = sum(
-        jnp.dot(part, obs, preferred_element_type=jnp.float32) for part in (low, middle, high)
-    )
-    value = jnp.broadcast_to(value[:, width // 2 : width // 2 + 1], (size, EXTRA))
+        jnp.dot(obs, part, preferred_element_type=jnp.float32) for part in (low, middle, high)
+    )
     value_high = value.astype(jnp.bfloat16).astype(jnp.float32)
     rest = value - value_high
     value_middle = rest.astype(jnp.bfloat16).astype(jnp.float32)
     value_low = rest - value_middle
-    row = lax.broadcasted_iota(jnp.int32, (size, EXTRA), 0)
-    lane = lax.broadcasted_iota(jnp.int32, (size, EXTRA), 1)
-    shard = jnp.right_shift(row, (size // tile_count).bit_length() - 1)
-    parts = jnp.where(lane == shard, value_high, 0.0)
-    parts = jnp.where(lane == shard + tile_count, value_middle, parts)
-    parts = jnp.where(lane == shard + 2 * tile_count, value_low, parts)
+    at = lax.broadcasted_iota(jnp.int32, (EXTRA, size), 0)
+    parts = jnp.where(at == 0, value_high, 0.0)
+    parts = jnp.where(at == 1, value_middle, parts)
+    parts = jnp.where(at == 2, value_low, parts)
     return high, middle, parts.astype(jnp.bfloat16)
 
 
@@ -159,13 +156,13 @@
 
     @pl.loop(0, square.shape[0])
     def _(pair):
-        high, middle, parts = finish(across[pair], gram[pair], square[pair], obs[pair], tile_count)
-        turn[:, :size] = high
-        turn[:, size : 2 * size] = middle
-        turn[:, 2 * size :] = parts
-        for n in range(tile_count):
-            place = pl.ds(pl.multiple_of(meta_ref[n] * pair_rows, pair_rows), pair_rows)
-            out_ref[pair, n * pair_rows : (n + 1) * pair_rows] = turn[place, :]
+        high, middle, parts = finish(across[pair], gram[pair], square[pair], obs[pair])
+        out_ref[pair, 2 * size :] = parts
+        for first, part in ((0, high), (size, middle)):
+            turn[...] = part
+            for n in range(tile_count):
+                place = pl.ds(pl.multiple_of(meta_ref[n] * pair_rows, pair_rows), pair_rows)
+                out_ref[pair, first + n * pair_rows : first + (n + 1) * pair_rows] = turn[place, :]
 
 
 def pair_matrices(slots, shard, first_pair, arc_of_row, autoreg, movavg, pair_rows):
@@ -181,14 +178,14 @@
         pair_kernel,
         in_specs=[SMEM] * 4 + [pl.BlockSpec(memory_space=pltpu.VMEM)] * len(slots),
         out_specs=pl.BlockSpec(memory_space=pltpu.VMEM),
-        out_shape=jax.ShapeDtypeStruct((pair_count, size, 2 * size + EXTRA), jnp.bfloat16),
+        out_shape=jax.ShapeDtypeStruct((pair_count, 2 * size + EXTRA, size), jnp.bfloat16),
         scratch_shapes=[
             pltpu.VMEM((size, width), jnp.float32),
             pltpu.VMEM((pair_count, param_count, width), jnp.float32),
             pltpu.VMEM((pair_count, width, size), jnp.float32),
             pltpu.VMEM((pair_count, size, size), jnp.float32),
-            pltpu.VMEM((pair_count, size, width), jnp.bfloat16),
-            pltpu.VMEM((size, 2 * size + EXTRA), jnp.bfloat16),
+            pltpu.VMEM((pair_count, EXTRA, size), jnp.bfloat16),
+            pltpu.VMEM((size, size), jnp.bfloat16),
         ],
         compiler_params=params(58),
         cost_estimate=cost(SMALL * 2),
@@ -234,9 +231,9 @@
     )(meta, *slots)
 
 
-def middle_rows_kernel(count, scale, meta_ref, *refs):
-    mids, slots, (out, rhs, panel, held, sems, middle, extra) = refs[:2], refs[2 : 2 + count], refs[2 + count :]
-    pair_rows = slots[0].shape[0]
+def middle_rows_kernel(count, scale, step, meta_ref, *refs):
+    mids, slots, (out, rhs, panel, held, sems) = refs[:2], refs[2 : 2 + count], refs[2 + count :]
+    pair_rows, width = slots[0].shape
     size = count * pair_rows
     pair, pairs = pl.program_id(0), held.shape[0]
     core = meta_ref[count]
@@ -247,6 +244,7 @@
 
     @pl.when(pair == 0)
     def _():
+        rhs[...] = jnp.zeros_like(rhs)
         for mine in range(2):
 
             @pl.when(core == mine)
@@ -255,35 +253,24 @@
                     fetch(which, int(which // (pairs // 2) != mine)).start()
 
     for n, slot in enumerate(slots):
-        panel[n * pair_rows : (n + 1) * pair_rows, :] = slot[...]
+        place = pl.ds(pl.multiple_of(meta_ref[n] * pair_rows, pair_rows), pair_rows)
+        panel[place, :] = slot[...]
     fetch(pair, 0).wait()
-    product = lax.dot_general(
-        held[pair], panel[...], ROWS_ACROSS, preferred_element_type=jnp.float32
-    )
-    middle[...] = (product[:size] + product[size : 2 * size]).astype(jnp.bfloat16)
-    for n in range(count):
-        place = pl.ds(pl.multiple_of(meta_ref[n] * pair_rows, pair_rows), pair_rows)
-        out[n] = middle[place, :]
-
-    @pl.when(pair == 0)
-    def _():
-        extra[...] = product[2 * size :]
-
-    @pl.when(pair > 0)
-    def _():
-        extra[...] += product[2 * size :]
-
-    @pl.when(pair == pairs - 1)
-    def _():
-        rhs[...] = jnp.sum(extra[...], axis=0, keepdims=True) * scale
-
-
-def middle_rows(meta, mids, slots, pair_rows, scale):
+    for at in range(0, width, step):
+        here = slice(at, min(at + step, width))
+        product = jnp.dot(held[pair], panel[:, here], preferred_element_type=jnp.float32)
+        middle = (product[:size] + product[size : 2 * size]).astype(jnp.bfloat16)
+        for n in range(count):
+            out[n, :, here] = middle[n * pair_rows : (n + 1) * pair_rows]
+        rhs[:, here] += jnp.sum(product[2 * size :], axis=0, keepdims=True) * scale
+
+
+def middle_rows(meta, mids, slots, pair_rows, scale, step):
     rows, width = slots[0].shape
-    pair_count, size, columns = rows // pair_rows, mids[0].shape[1], mids[0].shape[2]
+    pair_count, size, columns = rows // pair_rows, mids[0].shape[2], mids[0].shape[1]
     count = len(slots)
     return pl.pallas_call(
-        functools.partial(middle_rows_kernel, count, scale),
+        functools.partial(middle_rows_kernel, count, scale, step),
         grid=(pair_count,),
         in_specs=[SMEM] + [HBM] * 2 + [pl.BlockSpec((pair_rows, width), lambda b: (b, 0))] * count,
         out_specs=[
@@ -296,19 +283,18 @@
         ],
         scratch_shapes=[
             pltpu.VMEM((size, width), jnp.bfloat16),
-            pltpu.VMEM((pair_count, size, columns), jnp.bfloat16),
+            pltpu.VMEM((pair_count, columns, size), jnp.bfloat16),
             pltpu.SemaphoreType.DMA((pair_count,)),
-            pltpu.VMEM((size, width), jnp.bfloat16),
-            pltpu.VMEM((EXTRA, width), jnp.float32),
-        ],
-        compiler_params=params(56),
+        ],
+        compiler_params=params(48),
         cost_estimate=cost(ROWS),
         name="middle_rows",
     )(meta, *mids, *slots)
 
 
 def collect_kernel(slot_places, over_places, slot_count, meta_ref, *refs):
-    slots, overs, (out, held, sems) = refs[:slot_count], refs[slot_count:-3], refs[-3:]
+    slots, overs, (out, held, turned, sems) = refs[:slot_count], refs[slot_count:-4], refs[-4:]
+    offset = pl.multiple_of(meta_ref[3], 64)
     width = held.shape[1]
     rows = held.shape[0] // len(slot_places)
     start = pl.multiple_of(meta_ref[2], 128)
@@ -329,18 +315,20 @@
                 copy.start()
             for n, copy in enumerate(copies(near)):
                 copy.wait()
-                out[:, n * rows : (n + 1) * rows] = held[n * rows : (n + 1) * rows, :].T
-
-
-def collect(meta, slots, slot_places, overs, over_places, rows, width):
+                turned[...] = held[n * rows : (n + 1) * rows, :].T
+                out[:, n * rows : (n + 1) * rows] = turned[pl.ds(offset, out.shape[0]), :]
+
+
+def collect(meta, slots, slot_places, overs, over_places, rows, width, block_columns):
     total = rows * len(slot_places)
     return pl.pallas_call(
         functools.partial(collect_kernel, tuple(slot_places), tuple(over_places), len(slots)),
         in_specs=[SMEM] + [HBM] * (len(slots) + len(overs)),
         out_specs=pl.BlockSpec(memory_space=pltpu.VMEM),
-        out_shape=jax.ShapeDtypeStruct((width, total), jnp.bfloat16),
+        out_shape=jax.ShapeDtypeStruct((block_columns, total), jnp.bfloat16),
         scratch_shapes=[
             pltpu.VMEM((total, width), jnp.bfloat16),
+            pltpu.VMEM((width, rows), jnp.bfloat16),
             pltpu.SemaphoreType.DMA((len(slot_places),)),
         ],
         compiler_params=params(24),
@@ -349,9 +337,8 @@
     )(meta, *slots, *overs)
 
 
-def tile_kernel(block_columns, scale, meta_ref, *refs):
-    blocks, (*middles, out, block, sems) = refs[:4], refs[4:]
-    step = middles[0].shape[2]
+def tile_kernel(scale, meta_ref, *refs):
+    blocks, (middle_ref, out, block, sems) = refs[:4], refs[4:]
 
     def copies(kind):
         found, at = [], 0
@@ -373,31 +360,27 @@
         for copy in copies(0):
             copy.wait()
 
-    middle = jnp.concatenate([one[...].reshape(-1, step) for one in middles], axis=0)
-    offset = pl.multiple_of(meta_ref[3], 64)
-    out[...] = (
-        jnp.dot(block[pl.ds(offset, block_columns), :], middle, preferred_element_type=jnp.float32)
-        * scale
-    )
-
-
-def tile(meta, middles, blocks, block_columns, scale, step):
-    count, rows, width = middles[0].shape
-    payload = blocks[0].shape[0]
-    total = count * rows * len(middles)
+    middle = middle_ref[...].reshape(-1, middle_ref.shape[2])
+    out[...] = jnp.dot(block[...], middle, preferred_element_type=jnp.float32) * scale
+
+
+def tile(meta, middle, blocks, scale, step):
+    count, rows, width = middle.shape
+    block_columns = blocks[0].shape[0]
     return pl.pallas_call(
-        functools.partial(tile_kernel, block_columns, scale),
+        functools.partial(tile_kernel, scale),
         grid=(pl.cdiv(width, step),),
-        in_specs=[SMEM]
-        + [HBM] * 4
-        + [pl.BlockSpec((count, rows, step), lambda j: (0, 0, j))] * len(middles),
+        in_specs=[SMEM] + [HBM] * 4 + [pl.BlockSpec((count, rows, step), lambda j: (0, 0, j))],
         out_specs=pl.BlockSpec((block_columns, step), lambda j: (0, j)),
         out_shape=jax.ShapeDtypeStruct((block_columns, width), jnp.float32),
-        scratch_shapes=[pltpu.VMEM((payload, total), jnp.bfloat16), pltpu.SemaphoreType.DMA((2,))],
+        scratch_shapes=[
+            pltpu.VMEM((block_columns, count * rows), jnp.bfloat16),
+            pltpu.SemaphoreType.DMA((2,)),
+        ],
         compiler_params=params(48),
         cost_estimate=cost(12),
         name="tile",
-    )(meta, *blocks, *middles)
+    )(meta, *blocks, middle)
 
 
 def tie(value, *others):
@@ -461,13 +444,14 @@
     x1 = across_x(tie(z1, x0))
     z3 = along_z(tie(z1, z2, x1, mid), 2)
     x2 = across_x(tie(z2, x1))
-    picked_1 = picked(start, design, x0, z1, x1, tie(z2, mid))
-    mids = (mid, hop(tie(mid, z2), lambda near, same: (0, 1)))
+    picked_0 = picked(start, design, x0, tie(z1, z2, mid))
+    picked_1 = picked(start, x1, tie(z2, mid))
+    mids = (mid, hop(mid, lambda near, same: (0, 1)))
     slots_meta = jnp.concatenate([shard, core[None]])
-    x3 = across_x(tie(z3, x2, picked_1, mids[1]))
+    x3 = across_x(tie(z3, x2, picked_0, picked_1))
     picked_2 = picked(start, x2, z3)
     picked_3 = picked((1 - x) * (width - payload), z3)
-    over_1, over_2 = over(picked_1), over(picked_2)
+    over_0, over_1, over_2 = over(picked_0), over(picked_1), over(picked_2)
     over_3 = across_x(tie(over(picked_3), x3))
 
     block_meta = jnp.stack(
@@ -477,19 +461,20 @@
         block_meta,
         (design, x0, z1, x1, z2),
         [(n, 0) for n in range(5)],
-        (over_1,),
-        [(0, n * rows_dev) for n in range(5)],
+        (over_0, over_1),
+        [(n // 3, n % 3 * rows_dev) for n in range(5)],
         rows_dev,
         payload,
+        block_columns,
     )
     slots = (design, x0, z1, x1, z2, x2, z3, tie(x3, early))
-    middle, rhs = middle_rows(slots_meta, mids, slots, pair_rows, scale)
+    middle, rhs = middle_rows(slots_meta, mids, slots, pair_rows, scale, 512)
     late = collect(
         block_meta, (x2, z3, tie(x3, rhs)), [(0, 0), (1, 0), (2, 0)],
-        (over_2, over_3), [(0, 0), (0, rows_dev), (1, 0)], rows_dev, payload,
+        (over_2, over_3), [(0, 0), (0, rows_dev), (1, 0)], rows_dev, payload, block_columns,
     )
     blocks = (early, late, beside(early), beside(late))
-    normal = tile(block_meta, (middle,), blocks, block_columns, scale, 512)
+    normal = tile(block_meta, middle, blocks, scale, 512)
     return normal, rhs[0]
 
 
@@ -514,9 +499,7 @@
             here = lax.dynamic_slice_in_dim(values, pair * pair_rows, pair_rows, 1)
             return here.reshape(size, values.shape[2])
 
-        product = lax.dot_general(
-            mids[pair], rows_of(panel), ROWS_ACROSS, preferred_element_type=jnp.float32
-        )
+        product = jnp.dot(mids[pair], rows_of(panel), preferred_element_type=jnp.float32)
         middle = (product[:size] + product[size : 2 * size]).astype(jnp.bfloat16)
         here = lax.dot_general(
             rows_of(block), middle, ROWS_ACROSS, preferred_element_type=jnp.float32

time: 150 us -> 146 us (0.973)
  waiting for transfers between devices: 51.2 us -> 41.1 us
  starting transfers between devices: 26.7 us -> 34.3 us
  Pallas kernels: 61.4 us -> 59.8 us
    ppermute x6, waiting for transfers between devices: 44 us -> 32.9 us  [along_z(): return lax.ppermute(value, 'tm', pairs)]
    ppermute x6 -> x7, starting transfers between devices: 10.2 us -> 15.2 us  [hop(): return lax.ppermute(value, AXES, pairs)]
    ppermute x6 -> x7, waiting for transfers between devices: 2.3 us -> 5.56 us  [hop(): return lax.ppermute(value, AXES, pairs)]
    pallas_call x2, Pallas kernels: 29.9 us -> 27.4 us  [the longest x1 13.9 us: middle_rows(): pl.pallas_call(functools.partial(middle_rows_kernel, count, scale, step),...]
    pallas_call x3 -> x4, Pallas kernels: 8.51 us -> 10.9 us  [pack(): pl.pallas_call(functools.partial(pack_kernel, len(slots), width), in_spec...]
    ppermute x6, waiting for transfers between devices: 4.93 us -> 2.59 us  [across_x(): return lax.ppermute(value, 'tm', [(s, s ^ 1) for s in range(tile_count)])]
    ppermute x6, starting transfers between devices: 10 us -> 11.8 us  [along_z(): return lax.ppermute(value, 'tm', pairs)]
    pallas_call x1, Pallas kernels: 17.2 us -> 15.6 us  [pair_matrices(): pl.pallas_call(pair_kernel, in_specs=[SMEM] * 4 + [pl.BlockSpec(memory_sp...]
  transfers between devices with their start and end apart: 18 -> 19, of which waited for: 9 -> 11; matrix products, arithmetic and copies ran while one was open for 4% -> 4% of each run, Pallas kernels for 32% -> 32%
where the time goes in v3:
time: 146 us; the launch traced here: 145 us
  Pallas kernels  59.8 us (41%)
  waiting for transfers between devices  41.1 us (28%)
  starting transfers between devices  34.3 us (23%)
  other arithmetic  4.81 us (3%)
  local copies, waits for them, and re-layouts  4.17 us (3%)
    ppermute x6, waiting for transfers between devices, along_z(): return lax.ppermute(value, 'tm', pairs)  32.9 us
    pallas_call x1, Pallas kernels, pair_matrices(): pl.pallas_call(pair_kernel, in_specs=[SMEM] * 4 + [pl.BlockSpec(memory_sp...  15.6 us
    ppermute x7, starting transfers between devices, hop(): return lax.ppermute(value, AXES, pairs)  15.2 us
    pallas_call x1, Pallas kernels, middle_rows(): pl.pallas_call(functools.partial(middle_rows_kernel, count, scale, step),...  13.9 us
    pallas_call x1, Pallas kernels, tile(): pl.pallas_call(functools.partial(tile_kernel, scale), grid=(pl.cdiv(width...  13.5 us
    ppermute x6, starting transfers between devices, along_z(): return lax.ppermute(value, 'tm', pairs)  11.8 us
    pallas_call x4, Pallas kernels, pack(): pl.pallas_call(functools.partial(pack_kernel, len(slots), width), in_spec...  10.9 us
    ppermute x6, starting transfers between devices, across_x(): return lax.ppermute(value, 'tm', [(s, s ^ 1) for s in range(tile_count)])  7.37 us
  transfers between devices with their start and end apart: 19, of which 11 were waited for; matrix products, arithmetic and copies ran while one was open for 4% of the time, Pallas kernels for 32%

profile of v3, /device:TPU:0, one launch (start us, length us, event | category | flops | bytes accessed | tf_op | source)
XLA Modules:
  0.0 145.1 jit_solution(4343478604413823610)
XLA Ops:
  2.4 3.0 %collective-permute-start = (bf16[128,128]{1,0:T(8,128)(2,1)S(1)}, bf16[128,128]{1,0:T(8,128)(2,1)S(1)}, u32[]{:S(2)}, u32[]{:S(2)}) collective-permute-start(bf16[128,128]{1,0:T(8,128)(2,1)S(1)} %fusion.1), channel_id=1, source_target_pairs={{0,4},{4,0},{8,12},{12,8},{16,20},{20,16},{24,28},{28,24},{1,5},{5... | collective-permute-start | bytes 98312 | tf_op jit(solution)/shard_map/ppermute | solution.py:406
  5.4 2.6 %collective-permute-start.2 = (bf16[256,1920]{1,0:T(8,128)(2,1)}, bf16[256,1920]{1,0:T(8,128)(2,1)S(1)}, u32[]{:S(2)}, u32[]{:S(2)}) collective-permute-start(bf16[256,1920]{1,0:T(8,128)(2,1)} %refs_2_.1), channel_id=1, source_target_pairs={{8,0},{12,4},{24,8},{28,12},{0,16},{4,20},{16,24},{20,28},{9,1},{1... | collective-permute-start | bytes 2949128 | tf_op jit(solution)/shard_map/ppermute | solution.py:403
  8.1 1.3 collective-permute-start.1
  9.4 2.6 %collective-permute-start.4 = (bf16[2,128,128]{2,1,0:T(8,128)(2,1)S(1)}, bf16[2,128,128]{2,1,0:T(8,128)(2,1)S(1)}, u32[]{:S(2)}, u32[]{:S(2)}) collective-permute-start(bf16[2,128,128]{2,1,0:T(8,128)(2,1)S(1)} %pad_maximum_fusion.refs_0_), channel_id=1, source_target_pairs={{8,0},{12,4},{24,8},{28,12},{0,16},{4,20},{16,24},{20,28},{9,1},{1... | collective-permute-start | bytes 196616 | tf_op jit(solution)/shard_map/ppermute | solution.py:403
  12.0 3.0 %collective-permute-start.6 = (bf16[2,128,128]{2,1,0:T(8,128)(2,1)S(1)}, bf16[2,128,128]{2,1,0:T(8,128)(2,1)S(1)}, u32[]{:S(2)}, u32[]{:S(2)}) collective-permute-start(bf16[2,128,128]{2,1,0:T(8,128)(2,1)S(1)} %pad_maximum_fusion.refs_0_), channel_id=1, source_target_pairs={{24,0},{28,4},{16,8},{20,12},{8,16},{12,20},{0,24},{4,28},{25,1},{... | collective-permute-start | bytes 196616 | tf_op jit(solution)/shard_map/ppermute | solution.py:403
  15.0 15.5 %collective-permute-done.2.refs_2_.refs_4_ = bf16[256,1920]{1,0:T(8,128)(2,1)S(1)} collective-permute-done((bf16[256,1920]{1,0:T(8,128)(2,1)}, bf16[256,1920]{1,0:T(8,128)(2,1)S(1)}, u32[]{:S(2)}, u32[]{:S(2)}) %collective-permute-start.2) | collective-permute-done | bytes 983072 | tf_op jit(solution)/shard_map/ppermute | solution.py:403
  31.8 2.6 %collective-permute-done.5.refs_2_ = bf16[2,128,128]{2,1,0:T(8,128)(2,1)S(1)} collective-permute-done((bf16[2,128,128]{2,1,0:T(8,128)(2,1)S(1)}, bf16[2,128,128]{2,1,0:T(8,128)(2,1)S(1)}, u32[]{:S(2)}, u32[]{:S(2)}) %collective-permute-start.5) | collective-permute-done | bytes 65568 | tf_op jit(solution)/shard_map/ppermute | solution.py:403
  35.1 1.8 %collective-permute-start.7 = (bf16[256,1920]{1,0:T(8,128)(2,1)}, bf16[256,1920]{1,0:T(8,128)(2,1)S(1)}, u32[]{:S(2)}, u32[]{:S(2)}) collective-permute-start(bf16[256,1920]{1,0:T(8,128)(2,1)} %refs_2_.1), channel_id=1, source_target_pairs={{16,0},{20,4},{0,8},{4,12},{24,16},{28,20},{8,24},{12,28},{17,1},{... | collective-permute-start | bytes 2949128 | tf_op jit(solution)/shard_map/ppermute | solution.py:403
  38.1 1.4 convert_reduce_fusion.length_ref
  39.5 1.3 fusion.2
  40.7 15.6 %pair_matrices.1.refs_0_ = bf16[2,1040,512]{2,1,0:T(8,128)(2,1)} custom-call(s32[9]{0:T(128)} %concatenate.12.meta_ref, s32[4]{0:T(128)} %convert_reduce_fusion.length_ref, f32[8]{0:T(128)} %get-tuple-element.31.gain_ref, f32[8]{0:T(128)} %get-tuple-element.30.log_ref, bf16[2,128,128]{2,1,0:T(8,128)(2,1)} %copy-done.9, bf16[2,128,128]{2,1,0:T(8,128)(2,1)} %copy-done.10, ...), custom_call_target="tpu_custom_call" | custom-call | flops 1000000000 | tf_op jit(solution)/shard_map/pair_matrices/pallas_call | solution.py:177
  56.3 3.7 %collective-permute-done.7.refs_1_.refs_4_.refs_6_ = bf16[256,1920]{1,0:T(8,128)(2,1)S(1)} collective-permute-done((bf16[256,1920]{1,0:T(8,128)(2,1)}, bf16[256,1920]{1,0:T(8,128)(2,1)S(1)}, u32[]{:S(2)}, u32[]{:S(2)}) %collective-permute-start.7) | collective-permute-done | bytes 983072 | tf_op jit(solution)/shard_map/ppermute | solution.py:403
  61.0 1.7 %collective-permute-start.11 = (bf16[256,1920]{1,0:T(8,128)(2,1)S(1)}, bf16[256,1920]{1,0:T(8,128)(2,1)}, u32[]{:S(2)}, u32[]{:S(2)}) collective-permute-start(bf16[256,1920]{1,0:T(8,128)(2,1)S(1)} %collective-permute-done.2.refs_2_.refs_4_), channel_id=1, source_target_pairs={{8,0},{12,4},{24,8},{28,12},{0,16},{4,20},{16,24},{20,28},{9,1},{1... | collective-permute-start | bytes 2949128 | tf_op jit(solution)/shard_map/ppermute | solution.py:403
  63.9 2.9 %pack.4 = bf16[768,1024]{1,0:T(8,128)(2,1)} custom-call(s32[2]{0:T(128)} %pad_add_fusion.1.meta_ref, bf16[256,1920]{1,0:T(8,128)(2,1)} %refs_2_.1, bf16[256,1920]{1,0:T(8,128)(2,1)} %copy-done.3, bf16[256,1920]{1,0:T(8,128)(2,1)} %copy-done.1), custom_call_target="tpu_custom_call" | custom-call | flops 1000000000 | tf_op jit(solution)/shard_map/pack/pallas_call | solution.py:220
  66.8 2.4 %collective-permute-start.8 = (bf16[768,1024]{1,0:T(8,128)(2,1)}, bf16[768,1024]{1,0:T(8,128)(2,1)}, u32[]{:S(2)}, u32[]{:S(2)}) collective-permute-start(bf16[768,1024]{1,0:T(8,128)(2,1)} %pack.4), channel_id=1, source_target_pairs={{0,2},{4,6},{9,11},{13,15},{18,16},{22,20},{27,25},{31,29}} | collective-permute-start | bytes 4718600 | tf_op jit(solution)/shard_map/ppermute | solution.py:415
  69.3 2.7 %pack.5 = bf16[512,1024]{1,0:T(8,128)(2,1)} custom-call(s32[2]{0:T(128)} %pad_add_fusion.1.meta_ref, bf16[256,1920]{1,0:T(8,128)(2,1)} %collective-permute-done.3.refs_0_.refs_3_.refs_5_, bf16[256,1920]{1,0:T(8,128)(2,1)} %copy-done.7), custom_call_target="tpu_custom_call" | custom-call | flops 1000000000 | tf_op jit(solution)/shard_map/pack/pallas_call | solution.py:220
  72.0 2.3 %collective-permute-start.9 = (bf16[512,1024]{1,0:T(8,128)(2,1)}, bf16[512,1024]{1,0:T(8,128)(2,1)}, u32[]{:S(2)}, u32[]{:S(2)}) collective-permute-start(bf16[512,1024]{1,0:T(8,128)(2,1)} %pack.5), channel_id=1, source_target_pairs={{0,2},{4,6},{9,11},{13,15},{18,16},{22,20},{27,25},{31,29}} | collective-permute-start | bytes 3145736 | tf_op jit(solution)/shard_map/ppermute | solution.py:415
  74.3 9.9 %collective-permute-done.11.refs_8_.refs_1_.refs_0_ = bf16[256,1920]{1,0:T(8,128)(2,1)} collective-permute-done((bf16[256,1920]{1,0:T(8,128)(2,1)S(1)}, bf16[256,1920]{1,0:T(8,128)(2,1)}, u32[]{:S(2)}, u32[]{:S(2)}) %collective-permute-start.11) | collective-permute-done | bytes 983072 | tf_op jit(solution)/shard_map/ppermute | solution.py:403
  84.2 1.5 %collective-permute-done.10.refs_7_.refs_0_ = bf16[256,1920]{1,0:T(8,128)(2,1)S(1)} collective-permute-done((bf16[256,1920]{1,0:T(8,128)(2,1)}, bf16[256,1920]{1,0:T(8,128)(2,1)S(1)}, u32[]{:S(2)}, u32[]{:S(2)}) %collective-permute-start.10) | collective-permute-done | bytes 983072 | tf_op jit(solution)/shard_map/ppermute | solution.py:406
  86.8 2.5 %pack.7 = bf16[256,1024]{1,0:T(8,128)(2,1)} custom-call(s32[2]{0:T(128)} %pad_add_fusion.2.meta_ref, bf16[256,1920]{1,0:T(8,128)(2,1)} %collective-permute-done.11.refs_8_.refs_1_.refs_0_), custom_call_target="tpu_custom_call" | custom-call | flops 1000000000 | tf_op jit(solution)/shard_map/pack/pallas_call | solution.py:220
  89.4 1.9 %collective-permute-start.15 = (bf16[256,1024]{1,0:T(8,128)(2,1)}, bf16[256,1024]{1,0:T(8,128)(2,1)S(1)}, u32[]{:S(2)}, u32[]{:S(2)}) collective-permute-start(bf16[256,1024]{1,0:T(8,128)(2,1)} %pack.7), channel_id=1, source_target_pairs={{0,2},{4,6},{9,11},{13,15},{18,16},{22,20},{27,25},{31,29}} | collective-permute-start | bytes 1572872 | tf_op jit(solution)/shard_map/ppermute | solution.py:415
  91.5 2.7 %pack.6 = bf16[512,1024]{1,0:T(8,128)(2,1)} custom-call(s32[2]{0:T(128)} %pad_add_fusion.1.meta_ref, bf16[256,1920]{1,0:T(8,128)(2,1)} %copy-done.5, bf16[256,1920]{1,0:T(8,128)(2,1)} %collective-permute-done.11.refs_8_.refs_1_.refs_0_), custom_call_target="tpu_custom_call" | custom-call | flops 1000000000 | tf_op jit(solution)/shard_map/pack/pallas_call | solution.py:220
  94.2 3.4 %collective-permute-done.9.refs_6_ = bf16[512,1024]{1,0:T(8,128)(2,1)} collective-permute-done((bf16[512,1024]{1,0:T(8,128)(2,1)}, bf16[512,1024]{1,0:T(8,128)(2,1)}, u32[]{:S(2)}, u32[]{:S(2)}) %collective-permute-start.9) | collective-permute-done | bytes 1048608 | tf_op jit(solution)/shard_map/ppermute | solution.py:415
  97.6 4.4 %collective-permute-start.14 = (bf16[512,1024]{1,0:T(8,128)(2,1)}, bf16[512,1024]{1,0:T(8,128)(2,1)S(1)}, u32[]{:S(2)}, u32[]{:S(2)}) collective-permute-start(bf16[512,1024]{1,0:T(8,128)(2,1)} %pack.6), channel_id=1, source_target_pairs={{0,2},{4,6},{9,11},{13,15},{18,16},{22,20},{27,25},{31,29}} | collective-permute-start | bytes 3145736 | tf_op jit(solution)/shard_map/ppermute | solution.py:415
  103.3 3.7 %collect.2.refs_0_ = bf16[960,1280]{1,0:T(8,128)(2,1)} custom-call(s32[4]{0:T(128)S(1)} %pad_add_fusion.meta_ref, bf16[256,1920]{1,0:T(8,128)(2,1)S(1)} %copy-done, bf16[256,1920]{1,0:T(8,128)(2,1)S(1)} %copy-done.4, bf16[256,1920]{1,0:T(8,128)(2,1)S(1)} %copy-done.2, bf16[256,1920]{1,0:T(8,128)(2,1)} %collective-permute-done.3.refs_0_.refs_3_.refs_5_, ...), custom_call_target="tpu_custom_call" | custom-call | flops 1000000000 | tf_op jit(solution)/shard_map/collect/pallas_call | solution.py:324
  107.0 2.8 %collective-permute-start.17 = (bf16[960,1280]{1,0:T(8,128)(2,1)}, bf16[960,1280]{1,0:T(8,128)(2,1)}, u32[]{:S(2)}, u32[]{:S(2)}) collective-permute-start(bf16[960,1280]{1,0:T(8,128)(2,1)} %collect.2.refs_0_), channel_id=1, source_target_pairs={{0,1},{2,3},{4,5},{6,7},{9,8},{11,10},{13,12},{15,14},{16,17},{18,... | collective-permute-start | bytes 7372808 | tf_op jit(solution)/shard_map/ppermute | solution.py:415
  109.8 1.5 %collective-permute-start.16 = (bf16[256,1024]{1,0:T(8,128)(2,1)S(1)}, bf16[256,1024]{1,0:T(8,128)(2,1)S(1)}, u32[]{:S(2)}, u32[]{:S(2)}) collective-permute-start(bf16[256,1024]{1,0:T(8,128)(2,1)S(1)} %collective-permute-done.15), channel_id=1, source_target_pairs={{0,4},{4,0},{8,12},{12,8},{16,20},{20,16},{24,28},{28,24},{1,5},{5... | collective-permute-start | bytes 1572872 | tf_op jit(solution)/shard_map/ppermute | solution.py:406
  111.3 13.9 %middle_rows.1 = (bf16[8,256,1920]{2,1,0:T(8,128)(2,1)}, f32[1,1920]{1,0:T(1,128)S(1)}) custom-call(s32[9]{0:T(128)S(1)} %concatenate.13.meta_ref, bf16[2,1040,512]{2,1,0:T(8,128)(2,1)} %pair_matrices.1.refs_0_, bf16[2,1040,512]{2,1,0:T(8,128)(2,1)} %collective-permute-done.13.refs_1_, bf16[256,1920]{1,0:T(8,128)(2,1)S(1)} %copy-done, ...), custom_call_target="tpu_custom_call" | custom-call | flops 12000000000 | tf_op jit(solution)/shard_map/middle_rows/pallas_call | solution.py:272
  125.2 2.1 %collect.3.refs_1_ = bf16[960,768]{1,0:T(8,128)(2,1)S(1)} custom-call(s32[4]{0:T(128)S(1)} %pad_add_fusion.meta_ref, bf16[256,1920]{1,0:T(8,128)(2,1)S(1)} %copy-done.6, bf16[256,1920]{1,0:T(8,128)(2,1)} %collective-permute-done.11.refs_8_.refs_1_.refs_0_, bf16[256,1920]{1,0:T(8,128)(2,1)} %collective-permute-done.12.refs_9_.refs_2_, ...), custom_call_target="tpu_custom_call" | custom-call | flops 1000000000 | tf_op jit(solution)/shard_map/collect/pallas_call | solution.py:324
  127.4 1.4 collective-permute-start.18
  129.4 2.2 %collective-permute-done.18.refs_3_ = bf16[960,768]{1,0:T(8,128)(2,1)S(1)} collective-permute-done((bf16[960,768]{1,0:T(8,128)(2,1)S(1)}, bf16[960,768]{1,0:T(8,128)(2,1)S(1)}, u32[]{:S(2)}, u32[]{:S(2)}) %collective-permute-start.18) | collective-permute-done | bytes 1474592 | tf_op jit(solution)/shard_map/ppermute | solution.py:415
  131.5 13.5 %tile.1 = f32[960,1920]{1,0:T(8,128)} custom-call(s32[4]{0:T(128)S(1)} %pad_add_fusion.meta_ref, bf16[960,1280]{1,0:T(8,128)(2,1)} %collect.2.refs_0_, bf16[960,768]{1,0:T(8,128)(2,1)S(1)} %collect.3.refs_1_, bf16[960,1280]{1,0:T(8,128)(2,1)} %collective-permute-done.17.refs_2_, bf16[960,768]{1,0:T(8,128)(2,1)S(1)} %collective-permute-done.18.refs_3_, ...), custom_call_target="tpu_custom_call" | custom-call | flops 12000000000 | tf_op jit(solution)/shard_map/tile/pallas_call | solution.py:370
  (55 shorter events, 10.3 us)
Async XLA Ops:
  2.4 5.7 %collective-permute-start = (bf16[128,128]{1,0:T(8,128)(2,1)S(1)}, bf16[128,128]{1,0:T(8,128)(2,1)S(1)}, u32[]{:S(2)}, u32[]{:S(2)}) collective-permute-start(bf16[128,128]{1,0:T(8,128)(2,1)S(1)} %fusion.1), channel_id=1, source_target_pairs={{0,4},{4,0},{8,12},{12,8},{16,20},{20,16},{24,28},{28,24},{1,5},{5... | collective-permute-start | bytes 98312 | tf_op jit(solution)/shard_map/ppermute | solution.py:406
  5.4 25.1 %collective-permute-start.2 = (bf16[256,1920]{1,0:T(8,128)(2,1)}, bf16[256,1920]{1,0:T(8,128)(2,1)S(1)}, u32[]{:S(2)}, u32[]{:S(2)}) collective-permute-start(bf16[256,1920]{1,0:T(8,128)(2,1)} %refs_2_.1), channel_id=1, source_target_pairs={{8,0},{12,4},{24,8},{28,12},{0,16},{4,20},{16,24},{20,28},{9,1},{1... | collective-permute-start | bytes 2949128 | tf_op jit(solution)/shard_map/ppermute | solution.py:403
  8.1 32.6 %copy-start.9 = (bf16[2,128,128]{2,1,0:T(8,128)(2,1)}, bf16[2,128,128]{2,1,0:T(8,128)(2,1)S(1)}, u32[]{:S(2)}) copy-start(bf16[2,128,128]{2,1,0:T(8,128)(2,1)S(1)} %pad_maximum_fusion.refs_0_) | copy-start | bytes 196612
  8.1 23.2 %collective-permute-start.1 = (bf16[256,1920]{1,0:T(8,128)(2,1)}, bf16[256,1920]{1,0:T(8,128)(2,1)S(1)}, u32[]{:S(2)}, u32[]{:S(2)}) collective-permute-start(bf16[256,1920]{1,0:T(8,128)(2,1)} %refs_2_.1), channel_id=1, source_target_pairs={{0,4},{4,0},{8,12},{12,8},{16,20},{20,16},{24,28},{28,24},{1,5},{5... | collective-permute-start | bytes 2949128 | tf_op jit(solution)/shard_map/ppermute | solution.py:406
  9.4 22.4 %collective-permute-start.4 = (bf16[2,128,128]{2,1,0:T(8,128)(2,1)S(1)}, bf16[2,128,128]{2,1,0:T(8,128)(2,1)S(1)}, u32[]{:S(2)}, u32[]{:S(2)}) collective-permute-start(bf16[2,128,128]{2,1,0:T(8,128)(2,1)S(1)} %pad_maximum_fusion.refs_0_), channel_id=1, source_target_pairs={{8,0},{12,4},{24,8},{28,12},{0,16},{4,20},{16,24},{20,28},{9,1},{1... | collective-permute-start | bytes 196616 | tf_op jit(solution)/shard_map/ppermute | solution.py:403
  12.0 22.4 %collective-permute-start.5 = (bf16[2,128,128]{2,1,0:T(8,128)(2,1)S(1)}, bf16[2,128,128]{2,1,0:T(8,128)(2,1)S(1)}, u32[]{:S(2)}, u32[]{:S(2)}) collective-permute-start(bf16[2,128,128]{2,1,0:T(8,128)(2,1)S(1)} %pad_maximum_fusion.refs_0_), channel_id=1, source_target_pairs={{16,0},{20,4},{0,8},{4,12},{24,16},{28,20},{8,24},{12,28},{17,1},{... | collective-permute-start | bytes 196616 | tf_op jit(solution)/shard_map/ppermute | solution.py:403
  12.0 23.1 %collective-permute-start.6 = (bf16[2,128,128]{2,1,0:T(8,128)(2,1)S(1)}, bf16[2,128,128]{2,1,0:T(8,128)(2,1)S(1)}, u32[]{:S(2)}, u32[]{:S(2)}) collective-permute-start(bf16[2,128,128]{2,1,0:T(8,128)(2,1)S(1)} %pad_maximum_fusion.refs_0_), channel_id=1, source_target_pairs={{24,0},{28,4},{16,8},{20,12},{8,16},{12,20},{0,24},{4,28},{25,1},{... | collective-permute-start | bytes 196616 | tf_op jit(solution)/shard_map/ppermute | solution.py:403
  30.5 33.3 %copy-start.1 = (bf16[256,1920]{1,0:T(8,128)(2,1)}, bf16[256,1920]{1,0:T(8,128)(2,1)S(1)}, u32[]{:S(2)}) copy-start(bf16[256,1920]{1,0:T(8,128)(2,1)S(1)} %collective-permute-done.2.refs_2_.refs_4_) | copy-start | bytes 2949124
  31.3 32.6 %copy-start.3 = (bf16[256,1920]{1,0:T(8,128)(2,1)}, bf16[256,1920]{1,0:T(8,128)(2,1)S(1)}, u32[]{:S(2)}) copy-start(bf16[256,1920]{1,0:T(8,128)(2,1)S(1)} %collective-permute-done.1.refs_1_.refs_3_) | copy-start | bytes 2949124
  31.8 8.9 %copy-start.10 = (bf16[2,128,128]{2,1,0:T(8,128)(2,1)}, bf16[2,128,128]{2,1,0:T(8,128)(2,1)S(1)}, u32[]{:S(2)}) copy-start(bf16[2,128,128]{2,1,0:T(8,128)(2,1)S(1)} %collective-permute-done.4.refs_1_) | copy-start | bytes 196612
  34.3 6.4 %copy-start.11 = (bf16[2,128,128]{2,1,0:T(8,128)(2,1)}, bf16[2,128,128]{2,1,0:T(8,128)(2,1)S(1)}, u32[]{:S(2)}) copy-start(bf16[2,128,128]{2,1,0:T(8,128)(2,1)S(1)} %collective-permute-done.5.refs_2_) | copy-start | bytes 196612
  35.1 5.6 %copy-start.12 = (bf16[2,128,128]{2,1,0:T(8,128)(2,1)}, bf16[2,128,128]{2,1,0:T(8,128)(2,1)S(1)}, u32[]{:S(2)}) copy-start(bf16[2,128,128]{2,1,0:T(8,128)(2,1)S(1)} %collective-permute-done.6.refs_3_) | copy-start | bytes 196612
  35.1 25.0 %collective-permute-start.7 = (bf16[256,1920]{1,0:T(8,128)(2,1)}, bf16[256,1920]{1,0:T(8,128)(2,1)S(1)}, u32[]{:S(2)}, u32[]{:S(2)}) collective-permute-start(bf16[256,1920]{1,0:T(8,128)(2,1)} %refs_2_.1), channel_id=1, source_target_pairs={{16,0},{20,4},{0,8},{4,12},{24,16},{28,20},{8,24},{12,28},{17,1},{... | collective-permute-start | bytes 2949128 | tf_op jit(solution)/shard_map/ppermute | solution.py:403
  36.9 23.5 %collective-permute-start.3 = (bf16[256,1920]{1,0:T(8,128)(2,1)S(1)}, bf16[256,1920]{1,0:T(8,128)(2,1)}, u32[]{:S(2)}, u32[]{:S(2)}) collective-permute-start(bf16[256,1920]{1,0:T(8,128)(2,1)S(1)} %collective-permute-done.2.refs_2_.refs_4_), channel_id=1, source_target_pairs={{0,4},{4,0},{8,12},{12,8},{16,20},{20,16},{24,28},{28,24},{1,5},{5... | collective-permute-start | bytes 2949128 | tf_op jit(solution)/shard_map/ppermute | solution.py:406
  56.3 55.0 %collective-permute-start.13 = (bf16[2,1040,512]{2,1,0:T(8,128)(2,1)}, bf16[2,1040,512]{2,1,0:T(8,128)(2,1)}, u32[]{:S(2)}, u32[]{:S(2)}) collective-permute-start(bf16[2,1040,512]{2,1,0:T(8,128)(2,1)} %pair_matrices.1.refs_0_), channel_id=1, source_target_pairs={{0,1},{1,0},{2,3},{3,2},{4,5},{5,4},{6,7},{7,6},{8,9},{9,8},{10,11... | collective-permute-start | bytes 6389768 | tf_op jit(solution)/shard_map/ppermute | solution.py:415
  60.1 0.9 copy-start.7
  61.0 23.2 %collective-permute-start.11 = (bf16[256,1920]{1,0:T(8,128)(2,1)S(1)}, bf16[256,1920]{1,0:T(8,128)(2,1)}, u32[]{:S(2)}, u32[]{:S(2)}) collective-permute-start(bf16[256,1920]{1,0:T(8,128)(2,1)S(1)} %collective-permute-done.2.refs_2_.refs_4_), channel_id=1, source_target_pairs={{8,0},{12,4},{24,8},{28,12},{0,16},{4,20},{16,24},{20,28},{9,1},{1... | collective-permute-start | bytes 2949128 | tf_op jit(solution)/shard_map/ppermute | solution.py:403
  62.8 22.9 %collective-permute-start.10 = (bf16[256,1920]{1,0:T(8,128)(2,1)}, bf16[256,1920]{1,0:T(8,128)(2,1)S(1)}, u32[]{:S(2)}, u32[]{:S(2)}) collective-permute-start(bf16[256,1920]{1,0:T(8,128)(2,1)} %copy-done.7), channel_id=1, source_target_pairs={{0,4},{4,0},{8,12},{12,8},{16,20},{20,16},{24,28},{28,24},{1,5},{5... | collective-permute-start | bytes 2949128 | tf_op jit(solution)/shard_map/ppermute | solution.py:406
  66.8 35.2 %collective-permute-start.8 = (bf16[768,1024]{1,0:T(8,128)(2,1)}, bf16[768,1024]{1,0:T(8,128)(2,1)}, u32[]{:S(2)}, u32[]{:S(2)}) collective-permute-start(bf16[768,1024]{1,0:T(8,128)(2,1)} %pack.4), channel_id=1, source_target_pairs={{0,2},{4,6},{9,11},{13,15},{18,16},{22,20},{27,25},{31,29}} | collective-permute-start | bytes 4718600 | tf_op jit(solution)/shard_map/ppermute | solution.py:415
  72.0 25.6 %collective-permute-start.9 = (bf16[512,1024]{1,0:T(8,128)(2,1)}, bf16[512,1024]{1,0:T(8,128)(2,1)}, u32[]{:S(2)}, u32[]{:S(2)}) collective-permute-start(bf16[512,1024]{1,0:T(8,128)(2,1)} %pack.5), channel_id=1, source_target_pairs={{0,2},{4,6},{9,11},{13,15},{18,16},{22,20},{27,25},{31,29}} | collective-permute-start | bytes 3145736 | tf_op jit(solution)/shard_map/ppermute | solution.py:415
  85.6 1.2 copy-start.5
  85.6 24.2 %collective-permute-start.12 = (bf16[256,1920]{1,0:T(8,128)(2,1)}, bf16[256,1920]{1,0:T(8,128)(2,1)}, u32[]{:S(2)}, u32[]{:S(2)}) collective-permute-start(bf16[256,1920]{1,0:T(8,128)(2,1)} %collective-permute-done.11.refs_8_.refs_1_.refs_0_), channel_id=1, source_target_pairs={{0,4},{4,0},{8,12},{12,8},{16,20},{20,16},{24,28},{28,24},{1,5},{5... | collective-permute-start | bytes 2949128 | tf_op jit(solution)/shard_map/ppermute | solution.py:406
  89.4 12.7 %copy-start = (bf16[256,1920]{1,0:T(8,128)(2,1)S(1)}, bf16[256,1920]{1,0:T(8,128)(2,1)}, u32[]{:S(2)}) copy-start(bf16[256,1920]{1,0:T(8,128)(2,1)} %refs_2_.1) | copy-start | bytes 2949124
  89.4 12.7 %copy-start.2 = (bf16[256,1920]{1,0:T(8,128)(2,1)S(1)}, bf16[256,1920]{1,0:T(8,128)(2,1)}, u32[]{:S(2)}) copy-start(bf16[256,1920]{1,0:T(8,128)(2,1)} %copy-done.1) | copy-start | bytes 2949124
  89.4 12.7 %copy-start.4 = (bf16[256,1920]{1,0:T(8,128)(2,1)S(1)}, bf16[256,1920]{1,0:T(8,128)(2,1)}, u32[]{:S(2)}) copy-start(bf16[256,1920]{1,0:T(8,128)(2,1)} %copy-done.3) | copy-start | bytes 2949124
  89.4 20.4 %collective-permute-start.15 = (bf16[256,1024]{1,0:T(8,128)(2,1)}, bf16[256,1024]{1,0:T(8,128)(2,1)S(1)}, u32[]{:S(2)}, u32[]{:S(2)}) collective-permute-start(bf16[256,1024]{1,0:T(8,128)(2,1)} %pack.7), channel_id=1, source_target_pairs={{0,2},{4,6},{9,11},{13,15},{18,16},{22,20},{27,25},{31,29}} | collective-permute-start | bytes 1572872 | tf_op jit(solution)/shard_map/ppermute | solution.py:415
  94.2 17.1 %copy-start.6 = (bf16[256,1920]{1,0:T(8,128)(2,1)S(1)}, bf16[256,1920]{1,0:T(8,128)(2,1)}, u32[]{:S(2)}) copy-start(bf16[256,1920]{1,0:T(8,128)(2,1)} %copy-done.5) | copy-start | bytes 2949124
  97.6 27.6 %collective-permute-start.14 = (bf16[512,1024]{1,0:T(8,128)(2,1)}, bf16[512,1024]{1,0:T(8,128)(2,1)S(1)}, u32[]{:S(2)}, u32[]{:S(2)}) collective-permute-start(bf16[512,1024]{1,0:T(8,128)(2,1)} %pack.6), channel_id=1, source_target_pairs={{0,2},{4,6},{9,11},{13,15},{18,16},{22,20},{27,25},{31,29}} | collective-permute-start | bytes 3145736 | tf_op jit(solution)/shard_map/ppermute | solution.py:415
  102.1 1.2 copy-start.8
  107.0 24.5 %collective-permute-start.17 = (bf16[960,1280]{1,0:T(8,128)(2,1)}, bf16[960,1280]{1,0:T(8,128)(2,1)}, u32[]{:S(2)}, u32[]{:S(2)}) collective-permute-start(bf16[960,1280]{1,0:T(8,128)(2,1)} %collect.2.refs_0_), channel_id=1, source_target_pairs={{0,1},{2,3},{4,5},{6,7},{9,8},{11,10},{13,12},{15,14},{16,17},{18,... | collective-permute-start | bytes 7372808 | tf_op jit(solution)/shard_map/ppermute | solution.py:415
  109.8 15.4 %collective-permute-start.16 = (bf16[256,1024]{1,0:T(8,128)(2,1)S(1)}, bf16[256,1024]{1,0:T(8,128)(2,1)S(1)}, u32[]{:S(2)}, u32[]{:S(2)}) collective-permute-start(bf16[256,1024]{1,0:T(8,128)(2,1)S(1)} %collective-permute-done.15), channel_id=1, source_target_pairs={{0,4},{4,0},{8,12},{12,8},{16,20},{20,16},{24,28},{28,24},{1,5},{5... | collective-permute-start | bytes 1572872 | tf_op jit(solution)/shard_map/ppermute | solution.py:406
  127.4 4.2 %collective-permute-start.18 = (bf16[960,768]{1,0:T(8,128)(2,1)S(1)}, bf16[960,768]{1,0:T(8,128)(2,1)S(1)}, u32[]{:S(2)}, u32[]{:S(2)}) collective-permute-start(bf16[960,768]{1,0:T(8,128)(2,1)S(1)} %collect.3.refs_1_), channel_id=1, source_target_pairs={{0,1},{2,3},{4,5},{6,7},{9,8},{11,10},{13,12},{15,14},{16,17},{18,... | collective-permute-start | bytes 4423688 | tf_op jit(solution)/shard_map/ppermute | solution.py:415

commit v4 on v3

--- a/solution.py
+++ b/solution.py
@@ -193,19 +193,22 @@
     )(meta, lengths, autoreg + movavg, jnp.log(movavg), *slots)
 
 
-def pack_kernel(count, width, meta_ref, *refs):
-    slots, out, held, sems = refs[:count], refs[count], refs[count + 1], refs[count + 2]
-    start = pl.multiple_of(meta_ref[1], 128)
+def pack_kernel(parts, width, meta_ref, *refs):
+    count = 1 + max(slot for part in parts for slot in part)
+    slots, outs, held, sems = refs[:count], refs[count:-2], refs[-2], refs[-1]
 
     @pl.when(meta_ref[0] == 1)
     def _():
-        into, back, at = [], [], 0
-        for n, slot in enumerate(slots):
-            here = pl.ds(at, slot.shape[0])
-            columns = slot.at[:, pl.ds(start, width)]
-            into.append(pltpu.make_async_copy(columns, held.at[here], sems.at[0, n]))
-            back.append(pltpu.make_async_copy(held.at[here], out.at[here], sems.at[1, n]))
-            at += slot.shape[0]
+        into, back, row = [], [], 0
+        for which, (part, out) in enumerate(zip(parts, outs)):
+            start, at = pl.multiple_of(meta_ref[1 + which], 128), 0
+            for slot in part:
+                rows, n = slots[slot].shape[0], len(into)
+                here = held.at[pl.ds(row, rows)]
+                columns = slots[slot].at[:, pl.ds(start, width)]
+                into.append(pltpu.make_async_copy(columns, here, sems.at[0, n]))
+                back.append(pltpu.make_async_copy(here, out.at[pl.ds(at, rows)], sems.at[1, n]))
+                at, row = at + rows, row + rows
         for copy in into:
             copy.start()
         for first, second in zip(into, back):
@@ -215,16 +218,17 @@
             copy.wait()
 
 
-def pack(meta, slots, width):
-    rows = sum(slot.shape[0] for slot in slots)
+def pack(meta, slots, parts, width):
+    rows = [sum(slots[slot].shape[0] for slot in part) for part in parts]
+    copies = sum(len(part) for part in parts)
     return pl.pallas_call(
-        functools.partial(pack_kernel, len(slots), width),
+        functools.partial(pack_kernel, tuple(parts), width),
         in_specs=[SMEM] + [HBM] * len(slots),
-        out_specs=HBM,
-        out_shape=jax.ShapeDtypeStruct((rows, width), slots[0].dtype),
+        out_specs=[HBM] * len(parts),
+        out_shape=[jax.ShapeDtypeStruct((count, width), slots[0].dtype) for count in rows],
         scratch_shapes=[
-            pltpu.VMEM((rows, width), slots[0].dtype),
-            pltpu.SemaphoreType.DMA((2, len(slots))),
+            pltpu.VMEM((sum(rows), width), slots[0].dtype),
+            pltpu.SemaphoreType.DMA((2, copies)),
         ],
         cost_estimate=cost(SMALL * 2),
         name="pack",
@@ -232,7 +236,7 @@
 
 
 def middle_rows_kernel(count, scale, step, meta_ref, *refs):
-    mids, slots, (out, rhs, panel, held, sems) = refs[:2], refs[2 : 2 + count], refs[2 + count :]
+    mids, slots, (out, rhs, panel, held, sems) = refs[:2], refs[2:-5], refs[-5:]
     pair_rows, width = slots[0].shape
     size = count * pair_rows
     pair, pairs = pl.program_id(0), held.shape[0]
@@ -252,9 +256,20 @@
                 for which in range(pairs):
                     fetch(which, int(which // (pairs // 2) != mine)).start()
 
-    for n, slot in enumerate(slots):
-        place = pl.ds(pl.multiple_of(meta_ref[n] * pair_rows, pair_rows), pair_rows)
+    places = [
+        pl.ds(pl.multiple_of(meta_ref[n] * pair_rows, pair_rows), pair_rows) for n in range(count)
+    ]
+    for place, slot in zip(places, slots[: count - 1]):
         panel[place, :] = slot[...]
+
+    @pl.when(pair < pairs // 2)
+    def _():
+        panel[places[-1], :] = slots[-2][...]
+
+    @pl.when(pair >= pairs // 2)
+    def _():
+        panel[places[-1], :] = slots[-1][...]
+
     fetch(pair, 0).wait()
     for at in range(0, width, step):
         here = slice(at, min(at + step, width))
@@ -268,11 +283,17 @@
 def middle_rows(meta, mids, slots, pair_rows, scale, step):
     rows, width = slots[0].shape
     pair_count, size, columns = rows // pair_rows, mids[0].shape[2], mids[0].shape[1]
-    count = len(slots)
+    count = len(slots) - 1
+    half = pair_count // 2
+    slot_specs = [pl.BlockSpec((pair_rows, width), lambda b: (b, 0))] * (count - 1)
+    slot_specs += [
+        pl.BlockSpec((pair_rows, width), lambda b: (jnp.minimum(b, half - 1), 0)),
+        pl.BlockSpec((pair_rows, width), lambda b: (jnp.maximum(b - half, 0), 0)),
+    ]
     return pl.pallas_call(
         functools.partial(middle_rows_kernel, count, scale, step),
         grid=(pair_count,),
-        in_specs=[SMEM] + [HBM] * 2 + [pl.BlockSpec((pair_rows, width), lambda b: (b, 0))] * count,
+        in_specs=[SMEM] + [HBM] * 2 + slot_specs,
         out_specs=[
             pl.BlockSpec((count, pair_rows, width), lambda b: (0, b, 0)),
             pl.BlockSpec((1, width), lambda b: (0, 0)),
@@ -432,7 +453,7 @@
     sends = (near & same_core).astype(jnp.int32)
 
     def picked(start, *slots):
-        return pack(jnp.stack([sends, start]), slots, payload)
+        return pack(jnp.stack([sends, start]), slots, (tuple(range(len(slots))),), payload)[0]
 
     def over(value):
         return hop(value, lambda near, same: (1, 0) if near and same else None)
@@ -442,17 +463,19 @@
 
     z2 = along_z(tie(design, z1, x0, *sent_z), 1)
     x1 = across_x(tie(z1, x0))
-    z3 = along_z(tie(z1, z2, x1, mid), 2)
+    picked_0 = picked(start, design, x0, z1)
+    z3 = along_z(tie(z1, z2, x1, mid, picked_0), 2)
     x2 = across_x(tie(z2, x1))
-    picked_0 = picked(start, design, x0, tie(z1, z2, mid))
-    picked_1 = picked(start, x1, tie(z2, mid))
+    x1_half = x1[:half]
+    picked_1 = picked(start, x1, tie(z2, mid, x1_half))
     mids = (mid, hop(mid, lambda near, same: (0, 1)))
     slots_meta = jnp.concatenate([shard, core[None]])
-    x3 = across_x(tie(z3, x2, picked_0, picked_1))
-    picked_2 = picked(start, x2, z3)
-    picked_3 = picked((1 - x) * (width - payload), z3)
+    last_a = along_z(tie(x1_half, z3, x2), 2)
+    last_b = across_x(tie(z3[half:], x2, picked_0, picked_1))
+    across = (1 - x) * (width - payload)
+    picked_3, picked_2 = pack(jnp.stack([sends, across, start]), (x2, z3), ((1,), (0, 1)), payload)
     over_0, over_1, over_2 = over(picked_0), over(picked_1), over(picked_2)
-    over_3 = across_x(tie(over(picked_3), x3))
+    over_3 = across_x(tie(over(picked_3), last_b, last_a))
 
     block_meta = jnp.stack(
         [same_core.astype(jnp.int32), near.astype(jnp.int32), start, x * (payload - block_columns)]
@@ -467,11 +490,17 @@
         payload,
         block_columns,
     )
-    slots = (design, x0, z1, x1, z2, x2, z3, tie(x3, early))
+    slots = (design, x0, z1, x1, z2, x2, z3, last_a, tie(last_b, early))
     middle, rhs = middle_rows(slots_meta, mids, slots, pair_rows, scale, 512)
     late = collect(
-        block_meta, (x2, z3, tie(x3, rhs)), [(0, 0), (1, 0), (2, 0)],
-        (over_2, over_3), [(0, 0), (0, rows_dev), (1, 0)], rows_dev, payload, block_columns,
+        block_meta,
+        (x2, z3, last_a, tie(last_b, rhs)),
+        [(0, 0), (0, half), (1, 0), (1, half), (2, 0), (3, 0)],
+        (over_2, over_3),
+        [(n // 4, n % 4 * half) for n in range(6)],
+        half,
+        payload,
+        block_columns,
     )
     blocks = (early, late, beside(early), beside(late))
     normal = tile(block_meta, middle, blocks, scale, 512)

time: 146 us -> 143 us (0.979)
  waiting for transfers between devices: 41.1 us -> 35.5 us
  starting transfers between devices: 34.3 us -> 36.9 us
  local copies, waits for them, and re-layouts: 4.17 us -> 6.29 us
  Pallas kernels: 59.8 us -> 57.9 us
    ppermute x7, waiting for transfers between devices: 5.56 us -> 2.18 us  [hop(): return lax.ppermute(value, AXES, pairs)]
    ppermute x7, starting transfers between devices: 15.2 us -> 17.9 us  [hop(): return lax.ppermute(value, AXES, pairs)]
    slice x0 -> x2, local copies, waits for them, and re-layouts: none -> 2.67 us  [the longest x1 1.85 us: block_body(): last_b = across_x(tie(z3[half:], x2, picked_0, picked_1))]
    pallas_call x4 -> x3, Pallas kernels: 10.9 us -> 8.6 us  [pack(): pl.pallas_call(functools.partial(pack_kernel, tuple(parts), width), in_sp...]
    ppermute x6 -> x7, waiting for transfers between devices: 32.9 us -> 32 us  [along_z(): return lax.ppermute(value, 'tm', pairs)]
    ppermute x6 -> x7, starting transfers between devices: 11.8 us -> 11.7 us  [along_z(): return lax.ppermute(value, 'tm', pairs)]
  transfers between devices with their start and end apart: 19 -> 20, of which waited for: 11 -> 8; matrix products, arithmetic and copies ran while one was open for 4% -> 6% of each run, Pallas kernels for 32% -> 31%
where the time goes in v4:
time: 143 us; the launch traced here: 142 us
  Pallas kernels  57.9 us (40%)
  starting transfers between devices  36.9 us (26%)
  waiting for transfers between devices  35.5 us (25%)
  local copies, waits for them, and re-layouts  6.29 us (4%)
  other arithmetic  4.71 us (3%)
    ppermute x7, waiting for transfers between devices, along_z(): return lax.ppermute(value, 'tm', pairs)  32 us
    ppermute x7, starting transfers between devices, hop(): return lax.ppermute(value, AXES, pairs)  17.9 us
    pallas_call x1, Pallas kernels, pair_matrices(): pl.pallas_call(pair_kernel, in_specs=[SMEM] * 4 + [pl.BlockSpec(memory_sp...  15.6 us
    pallas_call x1, Pallas kernels, middle_rows(): pl.pallas_call(functools.partial(middle_rows_kernel, count, scale, step),...  14.1 us
    pallas_call x1, Pallas kernels, tile(): pl.pallas_call(functools.partial(tile_kernel, scale), grid=(pl.cdiv(width...  13.5 us
    ppermute x7, starting transfers between devices, along_z(): return lax.ppermute(value, 'tm', pairs)  11.7 us
    pallas_call x3, Pallas kernels, pack(): pl.pallas_call(functools.partial(pack_kernel, tuple(parts), width), in_sp...  8.6 us
    ppermute x6, starting transfers between devices, across_x(): return lax.ppermute(value, 'tm', [(s, s ^ 1) for s in range(tile_count)])  7.38 us
  transfers between devices with their start and end apart: 20, of which 8 were waited for; matrix products, arithmetic and copies ran while one was open for 6% of the time, Pallas kernels for 31%

profile of v4, /device:TPU:0, one launch (start us, length us, event | category | flops | bytes accessed | tf_op | source)
XLA Modules:
  0.0 142.2 jit_solution(3661985027532026812)
XLA Ops:
  0.6 0.9 copy.9
  2.4 3.0 %collective-permute-start = (bf16[128,128]{1,0:T(8,128)(2,1)S(1)}, bf16[128,128]{1,0:T(8,128)(2,1)S(1)}, u32[]{:S(2)}, u32[]{:S(2)}) collective-permute-start(bf16[128,128]{1,0:T(8,128)(2,1)S(1)} %fusion.1), channel_id=1, source_target_pairs={{0,4},{4,0},{8,12},{12,8},{16,20},{20,16},{24,28},{28,24},{1,5},{5... | collective-permute-start | bytes 98312 | tf_op jit(solution)/shard_map/ppermute | solution.py:427
  5.4 2.6 %collective-permute-start.2 = (bf16[256,1920]{1,0:T(8,128)(2,1)}, bf16[256,1920]{1,0:T(8,128)(2,1)S(1)}, u32[]{:S(2)}, u32[]{:S(2)}) collective-permute-start(bf16[256,1920]{1,0:T(8,128)(2,1)} %refs_2_.1), channel_id=1, source_target_pairs={{8,0},{12,4},{24,8},{28,12},{0,16},{4,20},{16,24},{20,28},{9,1},{1... | collective-permute-start | bytes 2949128 | tf_op jit(solution)/shard_map/ppermute | solution.py:424
  8.1 1.3 collective-permute-start.1
  10.1 2.6 %collective-permute-start.4 = (bf16[2,128,128]{2,1,0:T(8,128)(2,1)S(1)}, bf16[2,128,128]{2,1,0:T(8,128)(2,1)S(1)}, u32[]{:S(2)}, u32[]{:S(2)}) collective-permute-start(bf16[2,128,128]{2,1,0:T(8,128)(2,1)S(1)} %pad_maximum_fusion.refs_0_), channel_id=1, source_target_pairs={{8,0},{12,4},{24,8},{28,12},{0,16},{4,20},{16,24},{20,28},{9,1},{1... | collective-permute-start | bytes 196616 | tf_op jit(solution)/shard_map/ppermute | solution.py:424
  12.7 3.0 %collective-permute-start.6 = (bf16[2,128,128]{2,1,0:T(8,128)(2,1)S(1)}, bf16[2,128,128]{2,1,0:T(8,128)(2,1)S(1)}, u32[]{:S(2)}, u32[]{:S(2)}) collective-permute-start(bf16[2,128,128]{2,1,0:T(8,128)(2,1)S(1)} %pad_maximum_fusion.refs_0_), channel_id=1, source_target_pairs={{24,0},{28,4},{16,8},{20,12},{8,16},{12,20},{0,24},{4,28},{25,1},{... | collective-permute-start | bytes 196616 | tf_op jit(solution)/shard_map/ppermute | solution.py:424
  15.7 1.4 convert_reduce_fusion.length_ref
  17.1 13.4 %collective-permute-done.2.refs_2_.refs_4_ = bf16[256,1920]{1,0:T(8,128)(2,1)S(1)} collective-permute-done((bf16[256,1920]{1,0:T(8,128)(2,1)}, bf16[256,1920]{1,0:T(8,128)(2,1)S(1)}, u32[]{:S(2)}, u32[]{:S(2)}) %collective-permute-start.2) | collective-permute-done | bytes 983072 | tf_op jit(solution)/shard_map/ppermute | solution.py:424
  31.8 2.6 %collective-permute-done.5.refs_2_ = bf16[2,128,128]{2,1,0:T(8,128)(2,1)S(1)} collective-permute-done((bf16[2,128,128]{2,1,0:T(8,128)(2,1)S(1)}, bf16[2,128,128]{2,1,0:T(8,128)(2,1)S(1)}, u32[]{:S(2)}, u32[]{:S(2)}) %collective-permute-start.5) | collective-permute-done | bytes 65568 | tf_op jit(solution)/shard_map/ppermute | solution.py:424
  35.1 1.8 %collective-permute-start.7 = (bf16[256,1920]{1,0:T(8,128)(2,1)}, bf16[256,1920]{1,0:T(8,128)(2,1)}, u32[]{:S(2)}, u32[]{:S(2)}) collective-permute-start(bf16[256,1920]{1,0:T(8,128)(2,1)} %refs_2_.1), channel_id=1, source_target_pairs={{16,0},{20,4},{0,8},{4,12},{24,16},{28,20},{8,24},{12,28},{17,1},{... | collective-permute-start | bytes 2949128 | tf_op jit(solution)/shard_map/ppermute | solution.py:424
  38.0 1.2 fusion.2
  39.3 15.6 %pair_matrices.1.refs_0_ = bf16[2,1040,512]{2,1,0:T(8,128)(2,1)} custom-call(s32[9]{0:T(128)} %concatenate.12.meta_ref, s32[4]{0:T(128)} %convert_reduce_fusion.length_ref, f32[8]{0:T(128)} %get-tuple-element.35.gain_ref, f32[8]{0:T(128)} %get-tuple-element.34.log_ref, bf16[2,128,128]{2,1,0:T(8,128)(2,1)} %copy-done.8, bf16[2,128,128]{2,1,0:T(8,128)(2,1)} %copy-done.9, ...), custom_call_target="tpu_custom_call" | custom-call | flops 1000000000 | tf_op jit(solution)/shard_map/pair_matrices/pallas_call | solution.py:177
  54.9 2.9 %pack.3 = bf16[768,1024]{1,0:T(8,128)(2,1)} custom-call(s32[2]{0:T(128)} %pad_add_fusion.1.meta_ref, bf16[256,1920]{1,0:T(8,128)(2,1)} %refs_2_.1, bf16[256,1920]{1,0:T(8,128)(2,1)} %copy-done.3, bf16[256,1920]{1,0:T(8,128)(2,1)} %copy-done.1), custom_call_target="tpu_custom_call" | custom-call | flops 1000000000 | tf_op jit(solution)/shard_map/pack/pallas_call | solution.py:224
  57.9 2.4 %collective-permute-start.8 = (bf16[768,1024]{1,0:T(8,128)(2,1)}, bf16[768,1024]{1,0:T(8,128)(2,1)}, u32[]{:S(2)}, u32[]{:S(2)}) collective-permute-start(bf16[768,1024]{1,0:T(8,128)(2,1)} %pack.3), channel_id=1, source_target_pairs={{0,2},{4,6},{9,11},{13,15},{18,16},{22,20},{27,25},{31,29}} | collective-permute-start | bytes 4718600 | tf_op jit(solution)/shard_map/ppermute | solution.py:436
  60.3 1.6 %collective-permute-start.11 = (bf16[256,1920]{1,0:T(8,128)(2,1)}, bf16[256,1920]{1,0:T(8,128)(2,1)}, u32[]{:S(2)}, u32[]{:S(2)}) collective-permute-start(bf16[256,1920]{1,0:T(8,128)(2,1)} %copy-done.1), channel_id=1, source_target_pairs={{8,0},{12,4},{24,8},{28,12},{0,16},{4,20},{16,24},{20,28},{9,1},{1... | collective-permute-start | bytes 2949128 | tf_op jit(solution)/shard_map/ppermute | solution.py:424
  63.3 2.7 %pack.4 = bf16[512,1024]{1,0:T(8,128)(2,1)} custom-call(s32[2]{0:T(128)} %pad_add_fusion.1.meta_ref, bf16[256,1920]{1,0:T(8,128)(2,1)} %copy-done.5, bf16[256,1920]{1,0:T(8,128)(2,1)} %collective-permute-done.7.refs_1_.refs_4_.refs_6_), custom_call_target="tpu_custom_call" | custom-call | flops 1000000000 | tf_op jit(solution)/shard_map/pack/pallas_call | solution.py:224
  66.0 2.9 %collective-permute-start.9 = (bf16[512,1024]{1,0:T(8,128)(2,1)}, bf16[512,1024]{1,0:T(8,128)(2,1)}, u32[]{:S(2)}, u32[]{:S(2)}) collective-permute-start(bf16[512,1024]{1,0:T(8,128)(2,1)} %pack.4), channel_id=1, source_target_pairs={{0,2},{4,6},{9,11},{13,15},{18,16},{22,20},{27,25},{31,29}} | collective-permute-start | bytes 3145736 | tf_op jit(solution)/shard_map/ppermute | solution.py:436
  69.5 14.8 %collective-permute-done.11.refs_8_.refs_1_ = bf16[256,1920]{1,0:T(8,128)(2,1)} collective-permute-done((bf16[256,1920]{1,0:T(8,128)(2,1)}, bf16[256,1920]{1,0:T(8,128)(2,1)}, u32[]{:S(2)}, u32[]{:S(2)}) %collective-permute-start.11) | collective-permute-done | bytes 983072 | tf_op jit(solution)/shard_map/ppermute | solution.py:424
  84.8 2.9 %pack.5 = (bf16[256,1024]{1,0:T(8,128)(2,1)}, bf16[512,1024]{1,0:T(8,128)(2,1)}) custom-call(s32[3]{0:T(128)} %pad_add_fusion.2.meta_ref, bf16[256,1920]{1,0:T(8,128)(2,1)} %collective-permute-done.10.refs_7_.refs_0_, bf16[256,1920]{1,0:T(8,128)(2,1)} %collective-permute-done.11.refs_8_.refs_1_), custom_call_target="tpu_custom_call" | custom-call | flops 1000000000 | tf_op jit(solution)/shard_map/pack/pallas_call | solution.py:224
  87.7 2.1 %collective-permute-start.16 = (bf16[256,1024]{1,0:T(8,128)(2,1)}, bf16[256,1024]{1,0:T(8,128)(2,1)}, u32[]{:S(2)}, u32[]{:S(2)}) collective-permute-start(bf16[256,1024]{1,0:T(8,128)(2,1)} %get-tuple-element.31), channel_id=1, source_target_pairs={{0,2},{4,6},{9,11},{13,15},{18,16},{22,20},{27,25},{31,29}} | collective-permute-start | bytes 1572872 | tf_op jit(solution)/shard_map/ppermute | solution.py:436
  89.8 1.9 %slice.19 = bf16[128,1920]{1,0:T(8,128)(2,1)} slice(bf16[256,1920]{1,0:T(8,128)(2,1)} %collective-permute-done.11.refs_8_.refs_1_), slice={[128:256], [0:1920]} | slice | bytes 983040 | tf_op jit(solution)/shard_map/slice | solution.py:474
  91.7 1.0 collective-permute-start.13
  92.9 6.3 %collective-permute-start.15 = (bf16[512,1024]{1,0:T(8,128)(2,1)}, bf16[512,1024]{1,0:T(8,128)(2,1)S(1)}, u32[]{:S(2)}, u32[]{:S(2)}) collective-permute-start(bf16[512,1024]{1,0:T(8,128)(2,1)} %get-tuple-element.30), channel_id=1, source_target_pairs={{0,2},{4,6},{9,11},{13,15},{18,16},{22,20},{27,25},{31,29}} | collective-permute-start | bytes 3145736 | tf_op jit(solution)/shard_map/ppermute | solution.py:436
  99.2 1.2 copy-done.6
  100.4 3.5 %collect.2.refs_0_ = bf16[960,1280]{1,0:T(8,128)(2,1)} custom-call(s32[4]{0:T(128)S(1)} %pad_add_fusion.meta_ref, bf16[256,1920]{1,0:T(8,128)(2,1)S(1)} %copy-done, bf16[256,1920]{1,0:T(8,128)(2,1)S(1)} %copy-done.4, bf16[256,1920]{1,0:T(8,128)(2,1)S(1)} %copy-done.2, bf16[256,1920]{1,0:T(8,128)(2,1)S(1)} %copy-done.6, ...), custom_call_target="tpu_custom_call" | custom-call | flops 1000000000 | tf_op jit(solution)/shard_map/collect/pallas_call | solution.py:345
  103.9 2.8 %collective-permute-start.18 = (bf16[960,1280]{1,0:T(8,128)(2,1)}, bf16[960,1280]{1,0:T(8,128)(2,1)}, u32[]{:S(2)}, u32[]{:S(2)}) collective-permute-start(bf16[960,1280]{1,0:T(8,128)(2,1)} %collect.2.refs_0_), channel_id=1, source_target_pairs={{0,1},{2,3},{4,5},{6,7},{9,8},{11,10},{13,12},{15,14},{16,17},{18,... | collective-permute-start | bytes 7372808 | tf_op jit(solution)/shard_map/ppermute | solution.py:436
  106.7 1.0 collective-permute-start.17
  107.8 14.1 %middle_rows.1 = (bf16[8,256,1920]{2,1,0:T(8,128)(2,1)}, f32[1,1920]{1,0:T(1,128)S(1)}) custom-call(s32[9]{0:T(128)S(1)} %concatenate.13.meta_ref, bf16[2,1040,512]{2,1,0:T(8,128)(2,1)} %pair_matrices.1.refs_0_, bf16[2,1040,512]{2,1,0:T(8,128)(2,1)} %collective-permute-done.14.refs_1_, bf16[256,1920]{1,0:T(8,128)(2,1)S(1)} %copy-done, ...), custom_call_target="tpu_custom_call" | custom-call | flops 12000000000 | tf_op jit(solution)/shard_map/middle_rows/pallas_call | solution.py:293
  121.9 2.6 %collect.3.refs_1_ = bf16[960,768]{1,0:T(8,128)(2,1)S(1)} custom-call(s32[4]{0:T(128)S(1)} %pad_add_fusion.meta_ref, bf16[256,1920]{1,0:T(8,128)(2,1)} %collective-permute-done.10.refs_7_.refs_0_, bf16[256,1920]{1,0:T(8,128)(2,1)} %collective-permute-done.11.refs_8_.refs_1_, bf16[128,1920]{1,0:T(8,128)(2,1)} %collective-permute-done.12.refs_9_.refs_2_, ...), custom_call_target="tpu_custom_call" | custom-call | flops 1000000000 | tf_op jit(solution)/shard_map/collect/pallas_call | solution.py:345
  124.5 1.4 collective-permute-start.19
  126.5 2.2 %collective-permute-done.19.refs_3_ = bf16[960,768]{1,0:T(8,128)(2,1)S(1)} collective-permute-done((bf16[960,768]{1,0:T(8,128)(2,1)S(1)}, bf16[960,768]{1,0:T(8,128)(2,1)S(1)}, u32[]{:S(2)}, u32[]{:S(2)}) %collective-permute-start.19) | collective-permute-done | bytes 1474592 | tf_op jit(solution)/shard_map/ppermute | solution.py:436
  128.6 13.5 %tile.1 = f32[960,1920]{1,0:T(8,128)} custom-call(s32[4]{0:T(128)S(1)} %pad_add_fusion.meta_ref, bf16[960,1280]{1,0:T(8,128)(2,1)} %collect.2.refs_0_, bf16[960,768]{1,0:T(8,128)(2,1)S(1)} %collect.3.refs_1_, bf16[960,1280]{1,0:T(8,128)(2,1)} %collective-permute-done.18.refs_2_, bf16[960,768]{1,0:T(8,128)(2,1)S(1)} %collective-permute-done.19.refs_3_, ...), custom_call_target="tpu_custom_call" | custom-call | flops 12000000000 | tf_op jit(solution)/shard_map/tile/pallas_call | solution.py:391
  (56 shorter events, 8.0 us)
Async XLA Ops:
  2.4 5.7 %collective-permute-start = (bf16[128,128]{1,0:T(8,128)(2,1)S(1)}, bf16[128,128]{1,0:T(8,128)(2,1)S(1)}, u32[]{:S(2)}, u32[]{:S(2)}) collective-permute-start(bf16[128,128]{1,0:T(8,128)(2,1)S(1)} %fusion.1), channel_id=1, source_target_pairs={{0,4},{4,0},{8,12},{12,8},{16,20},{20,16},{24,28},{28,24},{1,5},{5... | collective-permute-start | bytes 98312 | tf_op jit(solution)/shard_map/ppermute | solution.py:427
  5.4 25.1 %collective-permute-start.2 = (bf16[256,1920]{1,0:T(8,128)(2,1)}, bf16[256,1920]{1,0:T(8,128)(2,1)S(1)}, u32[]{:S(2)}, u32[]{:S(2)}) collective-permute-start(bf16[256,1920]{1,0:T(8,128)(2,1)} %refs_2_.1), channel_id=1, source_target_pairs={{8,0},{12,4},{24,8},{28,12},{0,16},{4,20},{16,24},{20,28},{9,1},{1... | collective-permute-start | bytes 2949128 | tf_op jit(solution)/shard_map/ppermute | solution.py:424
  8.1 31.2 %copy-start.8 = (bf16[2,128,128]{2,1,0:T(8,128)(2,1)}, bf16[2,128,128]{2,1,0:T(8,128)(2,1)S(1)}, u32[]{:S(2)}) copy-start(bf16[2,128,128]{2,1,0:T(8,128)(2,1)S(1)} %pad_maximum_fusion.refs_0_) | copy-start | bytes 196612
  8.1 23.2 %collective-permute-start.1 = (bf16[256,1920]{1,0:T(8,128)(2,1)}, bf16[256,1920]{1,0:T(8,128)(2,1)S(1)}, u32[]{:S(2)}, u32[]{:S(2)}) collective-permute-start(bf16[256,1920]{1,0:T(8,128)(2,1)} %refs_2_.1), channel_id=1, source_target_pairs={{0,4},{4,0},{8,12},{12,8},{16,20},{20,16},{24,28},{28,24},{1,5},{5... | collective-permute-start | bytes 2949128 | tf_op jit(solution)/shard_map/ppermute | solution.py:427
  10.1 21.7 %collective-permute-start.4 = (bf16[2,128,128]{2,1,0:T(8,128)(2,1)S(1)}, bf16[2,128,128]{2,1,0:T(8,128)(2,1)S(1)}, u32[]{:S(2)}, u32[]{:S(2)}) collective-permute-start(bf16[2,128,128]{2,1,0:T(8,128)(2,1)S(1)} %pad_maximum_fusion.refs_0_), channel_id=1, source_target_pairs={{8,0},{12,4},{24,8},{28,12},{0,16},{4,20},{16,24},{20,28},{9,1},{1... | collective-permute-start | bytes 196616 | tf_op jit(solution)/shard_map/ppermute | solution.py:424
  12.7 21.7 %collective-permute-start.5 = (bf16[2,128,128]{2,1,0:T(8,128)(2,1)S(1)}, bf16[2,128,128]{2,1,0:T(8,128)(2,1)S(1)}, u32[]{:S(2)}, u32[]{:S(2)}) collective-permute-start(bf16[2,128,128]{2,1,0:T(8,128)(2,1)S(1)} %pad_maximum_fusion.refs_0_), channel_id=1, source_target_pairs={{16,0},{20,4},{0,8},{4,12},{24,16},{28,20},{8,24},{12,28},{17,1},{... | collective-permute-start | bytes 196616 | tf_op jit(solution)/shard_map/ppermute | solution.py:424
  12.7 22.4 %collective-permute-start.6 = (bf16[2,128,128]{2,1,0:T(8,128)(2,1)S(1)}, bf16[2,128,128]{2,1,0:T(8,128)(2,1)S(1)}, u32[]{:S(2)}, u32[]{:S(2)}) collective-permute-start(bf16[2,128,128]{2,1,0:T(8,128)(2,1)S(1)} %pad_maximum_fusion.refs_0_), channel_id=1, source_target_pairs={{24,0},{28,4},{16,8},{20,12},{8,16},{12,20},{0,24},{4,28},{25,1},{... | collective-permute-start | bytes 196616 | tf_op jit(solution)/shard_map/ppermute | solution.py:424
  30.5 24.4 %copy-start.1 = (bf16[256,1920]{1,0:T(8,128)(2,1)}, bf16[256,1920]{1,0:T(8,128)(2,1)S(1)}, u32[]{:S(2)}) copy-start(bf16[256,1920]{1,0:T(8,128)(2,1)S(1)} %collective-permute-done.2.refs_2_.refs_4_) | copy-start | bytes 2949124
  31.3 23.6 %copy-start.3 = (bf16[256,1920]{1,0:T(8,128)(2,1)}, bf16[256,1920]{1,0:T(8,128)(2,1)S(1)}, u32[]{:S(2)}) copy-start(bf16[256,1920]{1,0:T(8,128)(2,1)S(1)} %collective-permute-done.1.refs_1_.refs_3_) | copy-start | bytes 2949124
  31.8 7.5 %copy-start.9 = (bf16[2,128,128]{2,1,0:T(8,128)(2,1)}, bf16[2,128,128]{2,1,0:T(8,128)(2,1)S(1)}, u32[]{:S(2)}) copy-start(bf16[2,128,128]{2,1,0:T(8,128)(2,1)S(1)} %collective-permute-done.4.refs_1_) | copy-start | bytes 196612
  34.3 4.9 %copy-start.10 = (bf16[2,128,128]{2,1,0:T(8,128)(2,1)}, bf16[2,128,128]{2,1,0:T(8,128)(2,1)S(1)}, u32[]{:S(2)}) copy-start(bf16[2,128,128]{2,1,0:T(8,128)(2,1)S(1)} %collective-permute-done.5.refs_2_) | copy-start | bytes 196612
  35.1 4.2 %copy-start.11 = (bf16[2,128,128]{2,1,0:T(8,128)(2,1)}, bf16[2,128,128]{2,1,0:T(8,128)(2,1)S(1)}, u32[]{:S(2)}) copy-start(bf16[2,128,128]{2,1,0:T(8,128)(2,1)S(1)} %collective-permute-done.6.refs_3_) | copy-start | bytes 196612
  35.1 25.2 %collective-permute-start.7 = (bf16[256,1920]{1,0:T(8,128)(2,1)}, bf16[256,1920]{1,0:T(8,128)(2,1)}, u32[]{:S(2)}, u32[]{:S(2)}) collective-permute-start(bf16[256,1920]{1,0:T(8,128)(2,1)} %refs_2_.1), channel_id=1, source_target_pairs={{16,0},{20,4},{0,8},{4,12},{24,16},{28,20},{8,24},{12,28},{17,1},{... | collective-permute-start | bytes 2949128 | tf_op jit(solution)/shard_map/ppermute | solution.py:424
  36.9 23.4 %collective-permute-start.3 = (bf16[256,1920]{1,0:T(8,128)(2,1)S(1)}, bf16[256,1920]{1,0:T(8,128)(2,1)S(1)}, u32[]{:S(2)}, u32[]{:S(2)}) collective-permute-start(bf16[256,1920]{1,0:T(8,128)(2,1)S(1)} %collective-permute-done.2.refs_2_.refs_4_), channel_id=1, source_target_pairs={{0,4},{4,0},{8,12},{12,8},{16,20},{20,16},{24,28},{28,24},{1,5},{5... | collective-permute-start | bytes 2949128 | tf_op jit(solution)/shard_map/ppermute | solution.py:427
  54.9 52.9 %collective-permute-start.14 = (bf16[2,1040,512]{2,1,0:T(8,128)(2,1)}, bf16[2,1040,512]{2,1,0:T(8,128)(2,1)}, u32[]{:S(2)}, u32[]{:S(2)}) collective-permute-start(bf16[2,1040,512]{2,1,0:T(8,128)(2,1)} %pair_matrices.1.refs_0_), channel_id=1, source_target_pairs={{0,1},{1,0},{2,3},{3,2},{4,5},{5,4},{6,7},{7,6},{8,9},{9,8},{10,11... | collective-permute-start | bytes 6389768 | tf_op jit(solution)/shard_map/ppermute | solution.py:436
  57.9 34.8 %collective-permute-start.8 = (bf16[768,1024]{1,0:T(8,128)(2,1)}, bf16[768,1024]{1,0:T(8,128)(2,1)}, u32[]{:S(2)}, u32[]{:S(2)}) collective-permute-start(bf16[768,1024]{1,0:T(8,128)(2,1)} %pack.3), channel_id=1, source_target_pairs={{0,2},{4,6},{9,11},{13,15},{18,16},{22,20},{27,25},{31,29}} | collective-permute-start | bytes 4718600 | tf_op jit(solution)/shard_map/ppermute | solution.py:436
  60.3 3.0 %copy-start.5 = (bf16[256,1920]{1,0:T(8,128)(2,1)}, bf16[256,1920]{1,0:T(8,128)(2,1)S(1)}, u32[]{:S(2)}) copy-start(bf16[256,1920]{1,0:T(8,128)(2,1)S(1)} %collective-permute-done.3.refs_0_.refs_3_.refs_5_) | copy-start | bytes 2949124
  60.3 24.0 %collective-permute-start.11 = (bf16[256,1920]{1,0:T(8,128)(2,1)}, bf16[256,1920]{1,0:T(8,128)(2,1)}, u32[]{:S(2)}, u32[]{:S(2)}) collective-permute-start(bf16[256,1920]{1,0:T(8,128)(2,1)} %copy-done.1), channel_id=1, source_target_pairs={{8,0},{12,4},{24,8},{28,12},{0,16},{4,20},{16,24},{20,28},{9,1},{1... | collective-permute-start | bytes 2949128 | tf_op jit(solution)/shard_map/ppermute | solution.py:424
  61.9 22.9 %collective-permute-start.10 = (bf16[256,1920]{1,0:T(8,128)(2,1)}, bf16[256,1920]{1,0:T(8,128)(2,1)}, u32[]{:S(2)}, u32[]{:S(2)}) collective-permute-start(bf16[256,1920]{1,0:T(8,128)(2,1)} %collective-permute-done.7.refs_1_.refs_4_.refs_6_), channel_id=1, source_target_pairs={{0,4},{4,0},{8,12},{12,8},{16,20},{20,16},{24,28},{28,24},{1,5},{5... | collective-permute-start | bytes 2949128 | tf_op jit(solution)/shard_map/ppermute | solution.py:427
  66.0 26.9 %collective-permute-start.9 = (bf16[512,1024]{1,0:T(8,128)(2,1)}, bf16[512,1024]{1,0:T(8,128)(2,1)}, u32[]{:S(2)}, u32[]{:S(2)}) collective-permute-start(bf16[512,1024]{1,0:T(8,128)(2,1)} %pack.4), channel_id=1, source_target_pairs={{0,2},{4,6},{9,11},{13,15},{18,16},{22,20},{27,25},{31,29}} | collective-permute-start | bytes 3145736 | tf_op jit(solution)/shard_map/ppermute | solution.py:436
  69.5 29.7 %copy-start = (bf16[256,1920]{1,0:T(8,128)(2,1)S(1)}, bf16[256,1920]{1,0:T(8,128)(2,1)}, u32[]{:S(2)}) copy-start(bf16[256,1920]{1,0:T(8,128)(2,1)} %refs_2_.1) | copy-start | bytes 2949124
  69.5 29.7 %copy-start.2 = (bf16[256,1920]{1,0:T(8,128)(2,1)S(1)}, bf16[256,1920]{1,0:T(8,128)(2,1)}, u32[]{:S(2)}) copy-start(bf16[256,1920]{1,0:T(8,128)(2,1)} %copy-done.1) | copy-start | bytes 2949124
  69.5 29.7 %copy-start.4 = (bf16[256,1920]{1,0:T(8,128)(2,1)S(1)}, bf16[256,1920]{1,0:T(8,128)(2,1)}, u32[]{:S(2)}) copy-start(bf16[256,1920]{1,0:T(8,128)(2,1)} %copy-done.3) | copy-start | bytes 2949124
  87.7 19.0 %collective-permute-start.16 = (bf16[256,1024]{1,0:T(8,128)(2,1)}, bf16[256,1024]{1,0:T(8,128)(2,1)}, u32[]{:S(2)}, u32[]{:S(2)}) collective-permute-start(bf16[256,1024]{1,0:T(8,128)(2,1)} %get-tuple-element.31), channel_id=1, source_target_pairs={{0,2},{4,6},{9,11},{13,15},{18,16},{22,20},{27,25},{31,29}} | collective-permute-start | bytes 1572872 | tf_op jit(solution)/shard_map/ppermute | solution.py:436
  91.7 12.2 %collective-permute-start.13 = (bf16[128,1920]{1,0:T(8,128)(2,1)}, bf16[128,1920]{1,0:T(8,128)(2,1)S(1)}, u32[]{:S(2)}, u32[]{:S(2)}) collective-permute-start(bf16[128,1920]{1,0:T(8,128)(2,1)} %slice.19), channel_id=1, source_target_pairs={{0,4},{4,0},{8,12},{12,8},{16,20},{20,16},{24,28},{28,24},{1,5},{5... | collective-permute-start | bytes 1474568 | tf_op jit(solution)/shard_map/ppermute | solution.py:427
  92.7 14.0 %collective-permute-start.12 = (bf16[128,1920]{1,0:T(8,128)(2,1)}, bf16[128,1920]{1,0:T(8,128)(2,1)}, u32[]{:S(2)}, u32[]{:S(2)}) collective-permute-start(bf16[128,1920]{1,0:T(8,128)(2,1)} %slice.18), channel_id=1, source_target_pairs={{8,0},{12,4},{24,8},{28,12},{0,16},{4,20},{16,24},{20,28},{9,1},{1... | collective-permute-start | bytes 1474568 | tf_op jit(solution)/shard_map/ppermute | solution.py:424
  92.9 29.0 %collective-permute-start.15 = (bf16[512,1024]{1,0:T(8,128)(2,1)}, bf16[512,1024]{1,0:T(8,128)(2,1)S(1)}, u32[]{:S(2)}, u32[]{:S(2)}) collective-permute-start(bf16[512,1024]{1,0:T(8,128)(2,1)} %get-tuple-element.30), channel_id=1, source_target_pairs={{0,2},{4,6},{9,11},{13,15},{18,16},{22,20},{27,25},{31,29}} | collective-permute-start | bytes 3145736 | tf_op jit(solution)/shard_map/ppermute | solution.py:436
  99.2 1.2 copy-start.6
  100.4 7.4 %copy-start.7 = (bf16[256,1920]{1,0:T(8,128)(2,1)S(1)}, bf16[256,1920]{1,0:T(8,128)(2,1)}, u32[]{:S(2)}) copy-start(bf16[256,1920]{1,0:T(8,128)(2,1)} %copy-done.5) | copy-start | bytes 2949124
  103.9 24.7 %collective-permute-start.18 = (bf16[960,1280]{1,0:T(8,128)(2,1)}, bf16[960,1280]{1,0:T(8,128)(2,1)}, u32[]{:S(2)}, u32[]{:S(2)}) collective-permute-start(bf16[960,1280]{1,0:T(8,128)(2,1)} %collect.2.refs_0_), channel_id=1, source_target_pairs={{0,1},{2,3},{4,5},{6,7},{9,8},{11,10},{13,12},{15,14},{16,17},{18,... | collective-permute-start | bytes 7372808 | tf_op jit(solution)/shard_map/ppermute | solution.py:436
  106.7 15.1 %collective-permute-start.17 = (bf16[256,1024]{1,0:T(8,128)(2,1)}, bf16[256,1024]{1,0:T(8,128)(2,1)S(1)}, u32[]{:S(2)}, u32[]{:S(2)}) collective-permute-start(bf16[256,1024]{1,0:T(8,128)(2,1)} %collective-permute-done.16), channel_id=1, source_target_pairs={{0,4},{4,0},{8,12},{12,8},{16,20},{20,16},{24,28},{28,24},{1,5},{5... | collective-permute-start | bytes 1572872 | tf_op jit(solution)/shard_map/ppermute | solution.py:427
  124.5 4.2 %collective-permute-start.19 = (bf16[960,768]{1,0:T(8,128)(2,1)S(1)}, bf16[960,768]{1,0:T(8,128)(2,1)S(1)}, u32[]{:S(2)}, u32[]{:S(2)}) collective-permute-start(bf16[960,768]{1,0:T(8,128)(2,1)S(1)} %collect.3.refs_1_), channel_id=1, source_target_pairs={{0,1},{2,3},{4,5},{6,7},{9,8},{11,10},{13,12},{15,14},{16,17},{18,... | collective-permute-start | bytes 4423688 | tf_op jit(solution)/shard_map/ppermute | solution.py:436
